TPU v7x, 128 devices: a whole 4x4x4 slice. The times are simulated.
128 devices in a mesh: row: 8 (over z, core), col: 16 (over x, y).
Axes of the slice: x: 4, y: 4, z: 4, core: 2. Of those that a mesh axis runs over, the one named last changes fastest.
Arguments:
- stored: float32 [16384, 16384], P('row', 'col'), may hold values from -2 to 72, as said below
Outputs:
- trailing: float32 [16384, 16384], P('row', 'col')
- factor: float32 [16384, 256], P('row')
Inputs may be any that keep to these rules, and one draw needn't show every extreme that they name: stored is the block-cyclic storage of a symmetric positive definite matrix whose two leading block columns are well conditioned.
All inputs are finite; a program needn't handle non-finite values.
Results may differ from a plain program's by a relative error of at most 0.00012.
Values sent between devices are 32-bit elements; how exact they have to be, the bound alone decides.
No kernel may reach another device: no remote copies, remote signals or barrier semaphores. Data moves between devices by JAX's collectives and lax.ppermute only.
A program may use at most 128 MiB of HBM per device.

v0:
```python
import jax
import jax.numpy as jnp
from jax import lax
from jax.sharding import PartitionSpec as P

BLOCK = 128
PANELS = 2


def from_root(block, axis, holder):
    block = jnp.where(lax.axis_index(axis) == holder, block, jnp.zeros_like(block))
    return lax.psum(block, axis)


def outer_product(left, right):
    return jnp.dot(
        left, right.T, precision=lax.Precision.HIGHEST, preferred_element_type=jnp.float32
    )


def on_device(stored):
    row_count = lax.axis_size("row")
    col_count = lax.axis_size("col")
    local_rows, local_cols = stored.shape
    row_blocks = local_rows // BLOCK
    col_blocks = local_cols // BLOCK
    matrix_order = local_rows * row_count
    my_row = lax.axis_index("row")
    my_col = lax.axis_index("col")
    block_index = jnp.arange(matrix_order) // BLOCK
    row_parts = []
    working = stored
    for panel_index in range(PANELS):
        start = panel_index // col_count * BLOCK
        gathered = lax.all_gather(working[:, start : start + BLOCK], "row", axis=0, tiled=True)
        fetch_full_column = from_root(gathered, "col", panel_index % col_count)
        shaped = fetch_full_column.reshape(row_count, row_blocks, BLOCK, BLOCK)
        column = shaped.transpose(1, 0, 2, 3).reshape(matrix_order, BLOCK)
        diag_block = column[panel_index * BLOCK : (panel_index + 1) * BLOCK]
        lower = jnp.linalg.cholesky(diag_block)
        solved = jax.scipy.linalg.solve_triangular(lower, column.T, lower=True).T
        solved = jnp.where((block_index < panel_index)[:, None], jnp.float32(0.0), solved)
        panel = solved.at[panel_index * BLOCK : (panel_index + 1) * BLOCK].set(lower)
        by_rows = panel.reshape(row_blocks, row_count, BLOCK, BLOCK)
        row_part = lax.dynamic_index_in_dim(by_rows, my_row, 1, False).reshape(local_rows, BLOCK)
        by_cols = panel.reshape(col_blocks, col_count, BLOCK, BLOCK)
        col_part = lax.dynamic_index_in_dim(by_cols, my_col, 1, False).reshape(local_cols, BLOCK)
        row_part, col_part = (row_part, col_part)
        row_parts.append(row_part)
        working = working - outer_product(row_part, col_part)
    factor = jnp.concatenate(row_parts, axis=1)
    return (working, factor)


def solution(mesh):
    in_specs = (P("row", "col"),)
    out_specs = (P("row", "col"), P("row", None))
    return jax.shard_map(
        on_device, mesh=mesh, in_specs=in_specs, out_specs=out_specs, check_vma=False
    )
```

profile of v0, /device:TPU:1, one launch (start us, length us, event | category | flops | bytes accessed | tf_op | source)
XLA Modules:
  0.0 567.4 jit_solution(9120046685810418516)
XLA Ops:
  7.2 2.3 slice.54
  9.6 54.3 %all-gather.3.cloned.1.call-done = f32[16384,128]{1,0:T(8,128)} async-done(((f32[2048,128]{1,0:T(8,128)}), f32[16384,128]{1,0:T(8,128)}) %all-gather.3.cloned.1.call-update) | async-done | bytes 8388624 | tf_op jit(solution)/shard_map/all_gather | solution.py:35
  63.9 5.9 %broadcast_select_fusion.1 = f32[16384,128]{1,0:T(8,128)} fusion(f32[16384,128]{1,0:T(8,128)} %all-gather.3.cloned.1.call-done, pred[]{:T(512)S(6)} %eq.6), kind=kLoop, calls=%fused_computation.11 | loop fusion | flops 2097152 | bytes 16777216 | tf_op jit(solution)/shard_map/jit(_where)/select_n | solution.py:11
  69.8 9.3 %copy.3 = f32[8,16,128,128]{2,0,1,3:T(8,128)} copy(f32[8,16,128,128]{3,2,1,0:T(8,128)} %bitcast.84) | data formatting | bytes 16777216 | tf_op jit(solution)/shard_map/reshape | solution.py:37
  79.1 13.3 %copy.30 = f32[16,8,128,128]{3,1,2,0:T(8,128)} copy(f32[16,8,128,128]{3,2,1,0:T(8,128)} %bitcast.88) | data formatting | bytes 16777216
  92.6 138.1 %all-reduce.3.cloned.1.call-done = f32[16384,128]{0,1:T(8,128)} async-done(((f32[16384,128]{0,1:T(8,128)}), f32[16384,128]{0,1:T(8,128)}) %all-reduce.3.cloned.1.call-update) | async-done | bytes 8388624 | tf_op jit(solution)/shard_map/psum | solution.py:12
  230.8 0.8 slice.58
  231.7 0.9 fusion.15
  232.6 11.7 %cholesky.44 = f32[128,128]{1,0:T(8,128)S(1)} custom-call(f32[128,128]{1,0:T(8,128)S(1)} %fusion.15), custom_call_target="Cholesky" | custom-call | tf_op jit(solution)/shard_map/jit(cholesky)/cholesky | solution.py:40
  245.6 9.8 %custom-call.6 = f32[1,128,128]{1,2,0:T(8,128)S(1)} custom-call(f32[1,128,128]{2,1,0:T(8,128)S(1)} %get-tuple-element.30), custom_call_target="InvertDiagBlocksLowerTriangular" | custom-call | tf_op jit(solution)/shard_map/jit(_solve_triangular)/triangular_solve | solution.py:41
  255.5 10.6 %fusion.1 = f32[16384,128]{0,1:T(8,128)S(1)} fusion(f32[16384,128]{0,1:T(8,128)} %all-reduce.3.cloned.1.call-done, pred[16384]{0:T(1024)(128)(4,1)S(1)} %fusion.11, f32[1,128,128]{1,2,0:T(8,128)S(1)} %custom-call.6), kind=kOutput, calls=%fused_computation.3 | convolution fusion | flops 3223322624 | bytes 16859136 | tf_op jit(solution)/shard_map/jit(_solve_triangular)/triangular_solve | solution.py:41
  266.1 1.5 copy.12
  267.6 3.4 copy-done.1
  271.0 1.1 constant_dynamic-slice_fusion.1
  272.8 3.7 dynamic-slice_reduce_fusion.1
  276.5 9.5 %convolution_subtract_fusion.1 = f32[2048,1024]{1,0:T(8,128)S(1)} fusion(f32[2048,1024]{1,0:T(8,128)} %param.8, f32[2048,128]{1,0:T(8,128)S(1)} %bitcast.94, f32[16,8,8,128]{3,2,1,0:T(8,128)S(1)} %bitcast.99), kind=kOutput, calls=%fused_computation.9 | convolution fusion | flops 3223322624 | bytes 18350080 | tf_op jit(solution)/shard_map/dot_general | solution.py:16
  286.0 3.4 copy-done
  289.4 1.1 slice.59
  290.6 49.9 %all-gather.5.cloned.1.call-done = f32[16384,128]{1,0:T(8,128)} async-done(((f32[2048,128]{1,0:T(8,128)}), f32[16384,128]{1,0:T(8,128)}) %all-gather.5.cloned.1.call-update) | async-done | bytes 8388624 | tf_op jit(solution)/shard_map/all_gather | solution.py:35
  340.5 3.5 broadcast_select_fusion
  344.0 9.7 %copy.7 = f32[8,16,128,128]{2,0,1,3:T(8,128)} copy(f32[8,16,128,128]{3,2,1,0:T(8,128)} %bitcast.85) | data formatting | bytes 16777216 | tf_op jit(solution)/shard_map/reshape | solution.py:37
  353.7 13.1 %copy.29 = f32[16,8,128,128]{3,1,2,0:T(8,128)} copy(f32[16,8,128,128]{3,2,1,0:T(8,128)} %bitcast.89) | data formatting | bytes 16777216
  366.9 140.5 %all-reduce.5.cloned.1.call-done = f32[16384,128]{0,1:T(8,128)} async-done(((f32[16384,128]{0,1:T(8,128)}), f32[16384,128]{0,1:T(8,128)}) %all-reduce.5.cloned.1.call-update) | async-done | bytes 8388624 | tf_op jit(solution)/shard_map/psum | solution.py:12
  508.4 0.9 fusion.13
  509.3 11.7 %cholesky.55 = f32[128,128]{1,0:T(8,128)S(1)} custom-call(f32[128,128]{1,0:T(8,128)S(1)} %fusion.13), custom_call_target="Cholesky" | custom-call | tf_op jit(solution)/shard_map/jit(cholesky)/cholesky | solution.py:40
  522.3 10.0 %custom-call.7 = f32[1,128,128]{1,2,0:T(8,128)S(1)} custom-call(f32[1,128,128]{2,1,0:T(8,128)S(1)} %get-tuple-element.28), custom_call_target="InvertDiagBlocksLowerTriangular" | custom-call | tf_op jit(solution)/shard_map/jit(_solve_triangular)/triangular_solve | solution.py:41
  532.4 10.4 %fusion = f32[16384,128]{0,1:T(8,128)S(1)} fusion(f32[16384,128]{0,1:T(8,128)} %all-reduce.5.cloned.1.call-done, pred[16384]{0:T(1024)(128)(4,1)S(1)} %fusion.10, f32[1,128,128]{1,2,0:T(8,128)S(1)} %custom-call.7), kind=kOutput, calls=%fused_computation.1 | convolution fusion | flops 3223322624 | bytes 16859136 | tf_op jit(solution)/shard_map/jit(_solve_triangular)/triangular_solve | solution.py:41
  542.8 1.5 copy.16
  544.2 2.2 dynamic-slice_reduce_fusion
  546.4 1.1 constant_dynamic-slice_fusion
  548.3 1.5 pad_maximum_fusion
  549.7 11.0 %convolution_subtract_fusion = f32[2048,1024]{1,0:T(8,128)} fusion(f32[2048,1024]{1,0:T(8,128)} %copy-done, f32[2048,128]{1,0:T(8,128)S(1)} %bitcast.97, f32[16,8,8,128]{3,2,1,0:T(8,128)} %bitcast.98), kind=kOutput, calls=%fused_computation.8 | convolution fusion | flops 3223322624 | bytes 18350080 | tf_op jit(solution)/shard_map/dot_general | solution.py:16
  (27 shorter events, 5.8 us)
Async XLA Ops:
  7.2 56.7 %all-gather.3.cloned.1.call-start = ((), (), s32[]{:S(2)}) async-start(), calls=%async_computation | async-start | bytes 9437184 | tf_op jit(solution)/shard_map/all_gather | solution.py:35
  9.5 221.3 %all-reduce.3.cloned.1.call-start = ((), (), s32[]{:S(2)}) async-start(), calls=%async_computation.1 | async-start | bytes 16777216 | tf_op jit(solution)/shard_map/psum | solution.py:12
  92.4 248.1 %all-gather.5.cloned.1.call-start = ((), (), s32[]{:S(2)}) async-start(), calls=%async_computation.2 | async-start | bytes 9437184 | tf_op jit(solution)/shard_map/all_gather | solution.py:35
  267.6 3.4 copy-start.1
  286.0 3.4 copy-start
  290.5 216.9 %all-reduce.5.cloned.1.call-start = ((), (), s32[]{:S(2)}) async-start(), calls=%async_computation.3 | async-start | bytes 16777216 | tf_op jit(solution)/shard_map/psum | solution.py:12
Sparse Core Ops, SparseCore 0:
  10.3 53.5 all-gather.2
  92.5 138.2 all-reduce.2
  290.7 49.8 all-gather.4
  367.0 140.3 all-reduce.4
where the time goes:
time: 574 us; the launch traced here: 567 us
  waiting for transfers between devices  383 us (67%)
  local copies, waits for them, and re-layouts  70.2 us (12%)
  other arithmetic  58.4 us (10%)
  matrix products  41.4 us (7%)
  between operations  14.2 us (2%)
    psum x2, waiting for transfers between devices, from_root(): return lax.psum(block, axis)  279 us
    all_gather x2, waiting for transfers between devices, on_device(): lax.all_gather(working[:, start:start + BLOCK], 'row', axis=0, tiled=True)  104 us
    unnamed x8, local copies, waits for them, and re-layouts  36.2 us
    another operation x6, other arithmetic, on_device(): lower = jnp.linalg.cholesky(diag_block)  24.8 us
    another operation x4, other arithmetic, on_device(): solved = jax.scipy.linalg.solve_triangular(lower, column.T, lower=True).T  21.1 us
    another operation x2, matrix products, on_device(): solved = jax.scipy.linalg.solve_triangular(lower, column.T, lower=True).T  20.9 us
    dot_general x2, matrix products, outer_product(): jnp.dot(left, right.T, precision=lax.Precision.HIGHEST, preferred_element...  20.4 us
    reshape x2, local copies, waits for them, and re-layouts, on_device(): shaped = fetch_full_column.reshape(row_count, row_blocks, BLOCK, BLOCK)  19 us
  transfers between devices with their start and end apart: 4, of which 4 were waited for; matrix products, arithmetic and copies ran while one was open for 0% of the time, Pallas kernels for 0%

commit v1 on v0

v1 whole, which is shorter than its diff:
```python
import functools

import jax
import jax.numpy as jnp
from jax import lax
from jax.experimental import pallas as pl
from jax.experimental.pallas import tpu as pltpu
from jax.sharding import PartitionSpec as P

BLOCK = 128
WIDE = 2 * BLOCK
GROUP = 4
TILE = 256
F32 = jnp.float32
BF16 = jnp.bfloat16
AXES = ("row", "col")
NT = (((1,), (1,)), ((), ()))
NN = (((1,), (0,)), ((), ()))


def exact(left, right, dims):
    return lax.dot_general(
        left, right, dims, precision=lax.Precision.HIGHEST, preferred_element_type=F32
    )


def eliminate(matrix):
    lane = lax.broadcasted_iota(jnp.int32, (8, BLOCK), 1)
    sub = lax.broadcasted_iota(jnp.int32, (8, BLOCK), 0)
    rows = [matrix[8 * i : 8 * i + 8, :] for i in range(BLOCK // 8)]
    for first in range(0, BLOCK, GROUP):
        at = first // 8
        cols = {}
        for j in range(GROUP):
            for i in range(at, BLOCK // 8):
                cols[j, i] = jnp.broadcast_to(rows[i][:, first + j : first + j + 1], (8, BLOCK))
        for j in range(GROUP):
            k = first + j
            s = k % 8
            here = lane == k
            pivot = 1.0 / cols[j, at][s : s + 1, :]
            row = jnp.where(here[:1], 1.0, rows[at][s : s + 1, :])
            heads = {m: cols[m, at][s : s + 1, :] for m in range(j + 1, GROUP)}
            for i in range(at, BLOCK // 8):
                factor = cols[j, i] * pivot
                if i == at:
                    factor = jnp.where(sub > s, factor, 0.0)
                    rows[i] = jnp.where(here & (sub > s), 0.0, rows[i]) - factor * row
                else:
                    rows[i] = jnp.where(here, 0.0, rows[i]) - factor * row
                for m in range(j + 1, GROUP):
                    cols[m, i] = cols[m, i] - factor * heads[m]
    return jnp.concatenate(rows, axis=0)


def factor_block(matrix):
    done = eliminate(matrix)
    r = lax.broadcasted_iota(jnp.int32, (BLOCK, BLOCK), 0)
    c = lax.broadcasted_iota(jnp.int32, (BLOCK, BLOCK), 1)
    pivots = jnp.sum(jnp.where(r == c, done, 0.0), axis=1, keepdims=True)
    scale = lax.rsqrt(pivots)
    scale = scale * (1.5 - 0.5 * pivots * scale * scale)
    upper = jnp.where(r <= c, done, 0.0) * scale
    inverse = jnp.where(r > c, done, jnp.where(r == c, 1.0, 0.0)) * scale
    return upper.T, inverse


def head_kernel(diag_ref, lower_ref, inverse_ref):
    zero = jnp.zeros((BLOCK, BLOCK), F32)
    l00, i00 = factor_block(diag_ref[0])
    l10 = exact(diag_ref[1], i00, NT)
    l11, i11 = factor_block(diag_ref[2] - exact(l10, l10, NT))
    i10 = -exact(i11, exact(l10, i00, NN), NN)
    lower_ref[0, :, :BLOCK] = l00
    lower_ref[0, :, BLOCK:] = zero
    lower_ref[1, :, :BLOCK] = l10
    lower_ref[1, :, BLOCK:] = l11
    inverse_ref[:BLOCK, :BLOCK] = i00
    inverse_ref[:BLOCK, BLOCK:] = zero
    inverse_ref[BLOCK:, :BLOCK] = i10
    inverse_ref[BLOCK:, BLOCK:] = i11


def head(diag):
    return pl.pallas_call(
        head_kernel,
        out_shape=(
            jax.ShapeDtypeStruct((2, BLOCK, WIDE), F32),
            jax.ShapeDtypeStruct((WIDE, WIDE), F32),
        ),
        cost_estimate=pl.CostEstimate(flops=10**8, bytes_accessed=10**6, transcendentals=0),
        name="head",
    )(diag)


def split(x):
    high = x.astype(BF16)
    return high, (x - high.astype(F32)).astype(BF16)


def update_kernel(where_ref, lower_ref, inverse_ref, row_ref, col_ref, a_ref, out_ref, factor_ref, right_ref):
    my_row = where_ref[0]
    my_col = where_ref[1]

    @pl.when(pl.program_id(0) == 0)
    def _():
        def put(columns, start, width):
            high, low = split(columns)
            right_ref[0:WIDE, start : start + width] = high
            right_ref[WIDE : 2 * WIDE, start : start + width] = low
            right_ref[2 * WIDE : 3 * WIDE, start : start + width] = high

        for start in range(0, col_ref.shape[1], WIDE):
            put(exact(inverse_ref[...], col_ref[:, start : start + WIDE], NN), start, WIDE)

        @pl.when(my_col < 2)
        def _():
            put(lower_ref[my_col].T, 0, BLOCK)

    factor_ref[...] = exact(row_ref[...], inverse_ref[...], NT)

    @pl.when((pl.program_id(0) == 0) & (my_row < 2))
    def _():
        factor_ref[0:BLOCK, :] = lower_ref[my_row]

    high, low = split(factor_ref[...])
    left = jnp.concatenate([high, high, low], axis=1)
    out_ref[...] = a_ref[...] - lax.dot_general(left, right_ref[...], NN, preferred_element_type=F32)


def update(where, lower, inverse, row_part, col_part, stored):
    rows, cols = stored.shape
    grid_spec = pltpu.PrefetchScalarGridSpec(
        num_scalar_prefetch=1,
        grid=(rows // TILE,),
        in_specs=[
            pl.BlockSpec((2, BLOCK, WIDE), lambda i, w: (0, 0, 0)),
            pl.BlockSpec((WIDE, WIDE), lambda i, w: (0, 0)),
            pl.BlockSpec((TILE, WIDE), lambda i, w: (i, 0)),
            pl.BlockSpec((WIDE, cols), lambda i, w: (0, 0)),
            pl.BlockSpec((TILE, cols), lambda i, w: (i, 0)),
        ],
        out_specs=[
            pl.BlockSpec((TILE, cols), lambda i, w: (i, 0)),
            pl.BlockSpec((TILE, WIDE), lambda i, w: (i, 0)),
        ],
        scratch_shapes=[pltpu.VMEM((3 * WIDE, cols), BF16)],
    )
    return pl.pallas_call(
        update_kernel,
        grid_spec=grid_spec,
        out_shape=(
            jax.ShapeDtypeStruct((rows, cols), F32),
            jax.ShapeDtypeStruct((rows, WIDE), F32),
        ),
        compiler_params=pltpu.CompilerParams(vmem_limit_bytes=40 * 2**20),
        name="update",
    )(where, lower, inverse, row_part, col_part, stored)


def on_device(stored, n_row, n_col):
    my_row = lax.axis_index("row")
    my_col = lax.axis_index("col")
    core = my_row % 2
    depth = my_row // 2

    def at(r, c):
        return r * n_col + c

    def send(x, pairs):
        return lax.ppermute(x, AXES, pairs)

    corner = stored[:BLOCK, :BLOCK]
    other = send(corner, [(at(r, c), at(1 - r, c)) for r in (0, 1) for c in (0, 1)])
    half = jnp.where(core == 0, jnp.stack([corner, other]), jnp.stack([other, corner]))
    other = send(half, [(at(r, c), at(r, 1 - c)) for r in (0, 1) for c in (0, 1)])
    first, second = jnp.where(my_col == 0, half, other), jnp.where(my_col == 0, other, half)
    diag = jnp.stack([first[0], first[1], second[1]])
    got = [
        send(diag, [(at(r, c), at(r, c + 4 * d)) for r in (0, 1) for c in (0, 1)])
        for d in (1, 3, 2)
    ]
    diag = jnp.where(my_col < 2, diag, got[0] + got[1] + got[2])
    have = [(r, 4 * x + y) for r in (0, 1) for x in range(4) for y in (0, 1)]
    got = [send(diag, [(at(r, c), at(r + 2 * d, c)) for r, c in have]) for d in (1, 3, 2)]
    diag = jnp.where(my_row < 2, diag, got[0] + got[1] + got[2])
    have = [(r, 4 * x + y) for r in range(n_row) for x in range(4) for y in (0, 1)]
    got = send(diag, [(at(r, c), at(r, c - c % 4 + 3 - c % 4)) for r, c in have])
    diag = jnp.where(my_col % 4 < 2, diag, got)

    strip = stored[:BLOCK].reshape(BLOCK, n_row // 2, 2, BLOCK)
    keep = lax.dynamic_index_in_dim(strip, core, 2, False).transpose(1, 0, 2)
    give = lax.dynamic_index_in_dim(strip, 1 - core, 2, False).transpose(1, 0, 2)
    other = send(give, [(at(r, c), at(1 - r, c)) for r in (0, 1) for c in range(n_col)])
    both = jnp.where(core == 0, jnp.stack([keep, other], 1), jnp.stack([other, keep], 1))
    got = [
        send(both[d], [(at(r, c), at(r + 2 * d, c)) for r in (0, 1) for c in range(n_col)])
        for d in (1, 3, 2)
    ]
    block = jnp.where(depth == 0, both[0], got[0] + got[1] + got[2]).reshape(WIDE, BLOCK)
    col_part = lax.all_gather(block, "row", axis=0, tiled=False)
    col_part = col_part.transpose(1, 0, 2).reshape(WIDE, n_row * BLOCK)

    turned = send(
        block,
        [(at(r, c), at(c % n_row, 2 * r + c // n_row)) for r in range(n_row) for c in range(n_col)],
    )
    row_part = lax.all_gather(turned.T, "col", axis=0, tiled=True)

    lower, inverse = head(diag)
    where = jnp.stack([my_row, my_col]).astype(jnp.int32)
    trailing, factor = update(where, lower, inverse, row_part, col_part, stored)
    return trailing, factor


def solution(mesh):
    body = functools.partial(on_device, n_row=mesh.shape["row"], n_col=mesh.shape["col"])
    return jax.shard_map(
        body,
        mesh=mesh,
        in_specs=(P("row", "col"),),
        out_specs=(P("row", "col"), P("row", None)),
        check_vma=False,
    )
```

time: 574 us -> 124 us (0.22); the launches traced: 567 us -> 124 us
  waiting for transfers between devices: 383 us -> 34.1 us
  local copies, waits for them, and re-layouts: 70.2 us -> 12.7 us
  other arithmetic: 58.4 us -> 1.77 us
  matrix products: 41.4 us -> 0 us
  starting transfers between devices: 0.34 us -> 32.6 us
  Pallas kernels: 0 us -> 28.1 us
    psum x2 -> x0, waiting for transfers between devices: 279 us -> none  [from_root(): return lax.psum(block, axis)]
    all_gather x2, waiting for transfers between devices: 104 us -> 9.53 us  [the longest x1 9.53 us: on_device(): row_part = lax.all_gather(turned.T, 'col', axis=0, tiled=True)]
    another operation x10 -> x2, other arithmetic: 45.9 us -> 0.09 us  [the longest x1 0.08 us: on_device(): where = jnp.stack([my_row, my_col]).astype(jnp.int32)]
    ppermute x0 -> x14, starting transfers between devices: none -> 32.6 us  [send(): return lax.ppermute(x, AXES, pairs)]
    unnamed x8 -> x11, local copies, waits for them, and re-layouts: 36.2 us -> 7.52 us
    pallas_call x0 -> x2, Pallas kernels: none -> 28.1 us  [the longest x1 14.2 us: head(): pl.pallas_call(head_kernel, out_shape=(jax.ShapeDtypeStruct((2, BLOCK, WI...]
    ppermute x0 -> x14, waiting for transfers between devices: none -> 24.5 us  [send(): return lax.ppermute(x, AXES, pairs)]
    another operation x2 -> x0, matrix products: 20.9 us -> none  [on_device(): solved = jax.scipy.linalg.solve_triangular(lower, column.T, lower=True).T]
  transfers between devices with their start and end apart: 4 -> 16, of which waited for: 4 -> 14; matrix products, arithmetic and copies ran while one was open for 0% -> 3% of each run, Pallas kernels for 0% -> 12%
where the time goes in v1:
time: 124 us
  waiting for transfers between devices  34.1 us (28%)
  starting transfers between devices  32.6 us (26%)
  Pallas kernels  28.1 us (23%)
  between operations  14.4 us (12%)
  local copies, waits for them, and re-layouts  12.7 us (10%)
  other arithmetic  1.77 us (1%)
    ppermute x14, starting transfers between devices, send(): return lax.ppermute(x, AXES, pairs)  32.6 us
    ppermute x14, waiting for transfers between devices, send(): return lax.ppermute(x, AXES, pairs)  24.5 us
    pallas_call x1, Pallas kernels, head(): pl.pallas_call(head_kernel, out_shape=(jax.ShapeDtypeStruct((2, BLOCK, WI...  14.2 us
    pallas_call x1, Pallas kernels, update(): pl.pallas_call(update_kernel, grid_spec=grid_spec, out_shape=(jax.ShapeDt...  13.9 us
    all_gather x1, waiting for transfers between devices, on_device(): row_part = lax.all_gather(turned.T, 'col', axis=0, tiled=True)  9.53 us
    unnamed x11, local copies, waits for them, and re-layouts  7.52 us
  transfers between devices with their start and end apart: 16, of which 14 were waited for; matrix products, arithmetic and copies ran while one was open for 3% of the time, Pallas kernels for 12%

profile of v1, /device:TPU:1, one launch (start us, length us, event | category | flops | bytes accessed | tf_op | source)
XLA Modules:
  0.0 123.7 jit_solution(12684076177869909097)
XLA Ops:
  7.2 1.1 slice.26
  9.4 3.3 %collective-permute-start.9 = (f32[4,128,128]{1,2,0:T(8,128)S(1)}, f32[4,128,128]{1,2,0:T(8,128)S(1)}, u32[]{:S(2)}, u32[]{:S(2)}) collective-permute-start(f32[4,128,128]{1,2,0:T(8,128)S(1)} %bitcast.41), channel_id=1, source_target_pairs={{0,16},{1,17},{2,18},{3,19},{4,20},{5,21},{6,22},{7,23},{8,24},{9,... | collective-permute-start | bytes 786440 | tf_op jit(solution)/shard_map/ppermute | solution.py:171
  12.9 1.0 collective-permute-done.9
  14.6 2.9 %collective-permute-start.11 = (f32[2,128,128]{1,0,2:T(2,128)S(1)}, f32[2,128,128]{1,0,2:T(2,128)S(1)}, u32[]{:S(2)}, u32[]{:S(2)}) collective-permute-start(f32[2,128,128]{1,0,2:T(2,128)S(1)} %get-tuple-element.8), channel_id=1, source_target_pairs={{0,96},{1,97},{2,98},{3,99},{4,100},{5,101},{6,102},{7,103},{8,104... | collective-permute-start | bytes 393224 | tf_op jit(solution)/shard_map/ppermute | solution.py:171
  17.5 1.3 %collective-permute-start.12 = (f32[2,128,128]{1,0,2:T(2,128)S(1)}, f32[2,128,128]{1,0,2:T(2,128)S(1)}, u32[]{:S(2)}, u32[]{:S(2)}) collective-permute-start(f32[2,128,128]{1,0,2:T(2,128)S(1)} %get-tuple-element.9), channel_id=1, source_target_pairs={{0,64},{1,65},{2,66},{3,67},{4,68},{5,69},{6,70},{7,71},{8,72},{9,... | collective-permute-start | bytes 393224 | tf_op jit(solution)/shard_map/ppermute | solution.py:171
  18.8 1.3 %collective-permute-start.10 = (f32[2,128,128]{1,0,2:T(2,128)S(1)}, f32[2,128,128]{1,0,2:T(2,128)S(1)}, u32[]{:S(2)}, u32[]{:S(2)}) collective-permute-start(f32[2,128,128]{1,0,2:T(2,128)S(1)} %get-tuple-element.10), channel_id=1, source_target_pairs={{0,32},{1,33},{2,34},{3,35},{4,36},{5,37},{6,38},{7,39},{8,40},{9,... | collective-permute-start | bytes 393224 | tf_op jit(solution)/shard_map/ppermute | solution.py:171
  21.0 2.8 %collective-permute-done.10 = f32[2,128,128]{1,0,2:T(2,128)S(1)} collective-permute-done((f32[2,128,128]{1,0,2:T(2,128)S(1)}, f32[2,128,128]{1,0,2:T(2,128)S(1)}, u32[]{:S(2)}, u32[]{:S(2)}) %collective-permute-start.10) | collective-permute-done | bytes 131104 | tf_op jit(solution)/shard_map/ppermute | solution.py:171
  24.7 6.3 %collective-permute-start.13 = (f32[256,128]{0,1:T(8,128)S(1)}, f32[256,128]{0,1:T(8,128)S(1)}, u32[]{:S(2)}, u32[]{:S(2)}) collective-permute-start(f32[256,128]{0,1:T(8,128)S(1)} %bitcast.46), channel_id=1, source_target_pairs={{0,0},{1,16},{2,32},{3,48},{4,64},{5,80},{6,96},{7,112},{8,1},{9,1... | collective-permute-start | bytes 393224 | tf_op jit(solution)/shard_map/ppermute | solution.py:171
  31.0 2.1 %collective-permute-done.13 = f32[256,128]{0,1:T(8,128)S(1)} collective-permute-done((f32[256,128]{0,1:T(8,128)S(1)}, f32[256,128]{0,1:T(8,128)S(1)}, u32[]{:S(2)}, u32[]{:S(2)}) %collective-permute-start.13) | collective-permute-done | bytes 131104 | tf_op jit(solution)/shard_map/ppermute | solution.py:171
  34.6 1.9 %collective-permute-start = (f32[128,128]{1,0:T(8,128)S(1)}, f32[128,128]{1,0:T(8,128)S(1)}, u32[]{:S(2)}, u32[]{:S(2)}) collective-permute-start(f32[128,128]{1,0:T(8,128)S(1)} %get-tuple-element.7), channel_id=1, source_target_pairs={{0,16},{1,17},{16,0},{17,1}} | collective-permute-start | bytes 196616 | tf_op jit(solution)/shard_map/ppermute | solution.py:171
  36.5 1.2 collective-permute-done
  37.7 6.3 %collective-permute-start.1 = (f32[2,128,128]{2,1,0:T(8,128)S(1)}, f32[2,128,128]{2,1,0:T(8,128)S(1)}, u32[]{:S(2)}, u32[]{:S(2)}) collective-permute-start(f32[2,128,128]{2,1,0:T(8,128)S(1)} %maximum_select_fusion.1), channel_id=1, source_target_pairs={{0,1},{1,0},{16,17},{17,16}} | collective-permute-start | bytes 393224 | tf_op jit(solution)/shard_map/ppermute | solution.py:171
  44.1 3.7 %collective-permute-done.1 = f32[2,128,128]{2,1,0:T(8,128)S(1)} collective-permute-done((f32[2,128,128]{2,1,0:T(8,128)S(1)}, f32[2,128,128]{2,1,0:T(8,128)S(1)}, u32[]{:S(2)}, u32[]{:S(2)}) %collective-permute-start.1) | collective-permute-done | bytes 131104 | tf_op jit(solution)/shard_map/ppermute | solution.py:171
  47.8 1.3 %collective-permute-start.4 = (f32[3,128,128]{2,1,0:T(8,128)S(1)}, f32[3,128,128]{2,1,0:T(8,128)S(1)}, u32[]{:S(2)}, u32[]{:S(2)}) collective-permute-start(f32[3,128,128]{2,1,0:T(8,128)S(1)} %pad_maximum_fusion), channel_id=1, source_target_pairs={{0,8},{1,9},{16,24},{17,25}} | collective-permute-start | bytes 589832 | tf_op jit(solution)/shard_map/ppermute | solution.py:171
  49.1 1.3 %collective-permute-start.3 = (f32[3,128,128]{2,1,0:T(8,128)S(1)}, f32[3,128,128]{2,1,0:T(8,128)S(1)}, u32[]{:S(2)}, u32[]{:S(2)}) collective-permute-start(f32[3,128,128]{2,1,0:T(8,128)S(1)} %pad_maximum_fusion), channel_id=1, source_target_pairs={{0,12},{1,13},{16,28},{17,29}} | collective-permute-start | bytes 589832 | tf_op jit(solution)/shard_map/ppermute | solution.py:171
  50.4 1.3 %collective-permute-start.2 = (f32[3,128,128]{2,1,0:T(8,128)S(1)}, f32[3,128,128]{2,1,0:T(8,128)S(1)}, u32[]{:S(2)}, u32[]{:S(2)}) collective-permute-start(f32[3,128,128]{2,1,0:T(8,128)S(1)} %pad_maximum_fusion), channel_id=1, source_target_pairs={{0,4},{1,5},{16,20},{17,21}} | collective-permute-start | bytes 589832 | tf_op jit(solution)/shard_map/ppermute | solution.py:171
  51.7 1.1 collective-permute-done.4
  52.9 1.3 %collective-permute-done.3 = f32[3,128,128]{2,1,0:T(8,128)S(1)} collective-permute-done((f32[3,128,128]{2,1,0:T(8,128)S(1)}, f32[3,128,128]{2,1,0:T(8,128)S(1)}, u32[]{:S(2)}, u32[]{:S(2)}) %collective-permute-start.3) | collective-permute-done | bytes 196640 | tf_op jit(solution)/shard_map/ppermute | solution.py:171
  54.2 2.9 %collective-permute-done.2 = f32[3,128,128]{2,1,0:T(8,128)S(1)} collective-permute-done((f32[3,128,128]{2,1,0:T(8,128)S(1)}, f32[3,128,128]{2,1,0:T(8,128)S(1)}, u32[]{:S(2)}, u32[]{:S(2)}) %collective-permute-start.2) | collective-permute-done | bytes 196640 | tf_op jit(solution)/shard_map/ppermute | solution.py:171
  57.1 1.3 %collective-permute-start.7 = (f32[3,128,128]{2,1,0:T(8,128)S(1)}, f32[3,128,128]{2,1,0:T(8,128)S(1)}, u32[]{:S(2)}, u32[]{:S(2)}) collective-permute-start(f32[3,128,128]{2,1,0:T(8,128)S(1)} %add_select_fusion.1), channel_id=1, source_target_pairs={{0,64},{1,65},{4,68},{5,69},{8,72},{9,73},{12,76},{13,77},{16,80},... | collective-permute-start | bytes 589832 | tf_op jit(solution)/shard_map/ppermute | solution.py:171
  58.4 1.3 %collective-permute-start.6 = (f32[3,128,128]{2,1,0:T(8,128)S(1)}, f32[3,128,128]{2,1,0:T(8,128)S(1)}, u32[]{:S(2)}, u32[]{:S(2)}) collective-permute-start(f32[3,128,128]{2,1,0:T(8,128)S(1)} %add_select_fusion.1), channel_id=1, source_target_pairs={{0,96},{1,97},{4,100},{5,101},{8,104},{9,105},{12,108},{13,109},{1... | collective-permute-start | bytes 589832 | tf_op jit(solution)/shard_map/ppermute | solution.py:171
  59.7 1.3 %collective-permute-start.5 = (f32[3,128,128]{2,1,0:T(8,128)S(1)}, f32[3,128,128]{2,1,0:T(8,128)S(1)}, u32[]{:S(2)}, u32[]{:S(2)}) collective-permute-start(f32[3,128,128]{2,1,0:T(8,128)S(1)} %add_select_fusion.1), channel_id=1, source_target_pairs={{0,32},{1,33},{4,36},{5,37},{8,40},{9,41},{12,44},{13,45},{16,48},... | collective-permute-start | bytes 589832 | tf_op jit(solution)/shard_map/ppermute | solution.py:171
  61.5 1.3 %collective-permute-done.6 = f32[3,128,128]{2,1,0:T(8,128)S(1)} collective-permute-done((f32[3,128,128]{2,1,0:T(8,128)S(1)}, f32[3,128,128]{2,1,0:T(8,128)S(1)}, u32[]{:S(2)}, u32[]{:S(2)}) %collective-permute-start.6) | collective-permute-done | bytes 196640 | tf_op jit(solution)/shard_map/ppermute | solution.py:171
  62.8 2.9 %collective-permute-done.5 = f32[3,128,128]{2,1,0:T(8,128)S(1)} collective-permute-done((f32[3,128,128]{2,1,0:T(8,128)S(1)}, f32[3,128,128]{2,1,0:T(8,128)S(1)}, u32[]{:S(2)}, u32[]{:S(2)}) %collective-permute-start.5) | collective-permute-done | bytes 196640 | tf_op jit(solution)/shard_map/ppermute | solution.py:171
  65.8 1.5 %collective-permute-start.8 = (f32[3,128,128]{2,1,0:T(8,128)S(1)}, f32[3,128,128]{2,1,0:T(8,128)S(1)}, u32[]{:S(2)}, u32[]{:S(2)}) collective-permute-start(f32[3,128,128]{2,1,0:T(8,128)S(1)} %add_select_fusion), channel_id=1, source_target_pairs={{0,3},{1,2},{4,7},{5,6},{8,11},{9,10},{12,15},{13,14},{16,19},{17,... | collective-permute-start | bytes 589832 | tf_op jit(solution)/shard_map/ppermute | solution.py:171
  67.4 2.9 %collective-permute-done.8 = f32[3,128,128]{2,1,0:T(8,128)S(1)} collective-permute-done((f32[3,128,128]{2,1,0:T(8,128)S(1)}, f32[3,128,128]{2,1,0:T(8,128)S(1)}, u32[]{:S(2)}, u32[]{:S(2)}) %collective-permute-start.8) | collective-permute-done | bytes 196640 | tf_op jit(solution)/shard_map/ppermute | solution.py:171
  71.0 14.2 %head.1 = (f32[2,128,256]{2,1,0:T(8,128)}, f32[256,256]{1,0:T(8,128)}) custom-call(f32[3,128,128]{2,1,0:T(8,128)} %broadcast_select_fusion.diag_ref), custom_call_target="tpu_custom_call" | custom-call | flops 100000000 | bytes 1000000 | tf_op jit(solution)/shard_map/head/pallas_call | solution.py:85
  85.2 1.3 %copy_bitcast_fusion.col_ref = f32[256,1024]{1,0:T(8,128)S(1)} fusion(f32[8,256,128]{2,1,0:T(8,128)} %all-gather.5.cloned.1.call-done), kind=kLoop, calls=%fused_computation | loop fusion | bytes 2097152 | tf_op jit(solution)/shard_map/reshape | solution.py:202
  86.6 9.5 %all-gather.3.cloned.1.call-done.row_ref = f32[2048,256]{1,0:T(8,128)} async-done(((f32[128,256]{1,0:T(8,128)}), f32[2048,256]{1,0:T(8,128)}) %all-gather.3.cloned.1.call-update) | async-done | bytes 2097168 | tf_op jit(solution)/shard_map/all_gather | solution.py:208
  96.1 3.4 %copy-done = f32[2048,1024]{1,0:T(8,128)S(1)} copy-done((f32[2048,1024]{1,0:T(8,128)S(1)}, f32[2048,1024]{1,0:T(8,128)}, u32[]{:S(2)}) %copy-start) | copy-done | bytes 8388632
  99.5 1.6 %copy-done.1 = f32[2048,256]{1,0:T(8,128)S(1)} copy-done((f32[2048,256]{1,0:T(8,128)S(1)}, f32[2048,256]{1,0:T(8,128)}, u32[]{:S(2)}) %copy-start.1) | copy-done | bytes 2097176
  103.0 13.9 %update.1 = (f32[2048,1024]{1,0:T(8,128)}, f32[2048,256]{1,0:T(8,128)}) custom-call(s32[2]{0:T(128)S(1)} %pad_add_fusion.where_ref, f32[2,128,256]{2,1,0:T(8,128)S(1)} %copy-done.2, f32[256,256]{1,0:T(8,128)S(1)} %copy-done.3, f32[2048,256]{1,0:T(8,128)S(1)} %copy-done.1, f32[256,1024]{1,0:T(8,128)S(1)} %copy_bitcast_fusion.col_ref, f32[2048,1024]{1,0:T(8,128)S(1)} %copy-done), custom_call_target="tpu_custom_call" | custom-call | tf_op jit(solution)/shard_map/update/pallas_call | solution.py:149
  (34 shorter events, 8.5 us)
Async XLA Ops:
  7.2 78.1 %all-gather.5.cloned.1.call-start = ((), (), s32[]{:S(2)}) async-start(), calls=%async_computation.1 | async-start | bytes 1179648 | tf_op jit(solution)/shard_map/all_gather | solution.py:201
  9.4 4.5 %collective-permute-start.9 = (f32[4,128,128]{1,2,0:T(8,128)S(1)}, f32[4,128,128]{1,2,0:T(8,128)S(1)}, u32[]{:S(2)}, u32[]{:S(2)}) collective-permute-start(f32[4,128,128]{1,2,0:T(8,128)S(1)} %bitcast.41), channel_id=1, source_target_pairs={{0,16},{1,17},{2,18},{3,19},{4,20},{5,21},{6,22},{7,23},{8,24},{9,... | collective-permute-start | bytes 786440 | tf_op jit(solution)/shard_map/ppermute | solution.py:171
  14.6 5.5 %collective-permute-start.11 = (f32[2,128,128]{1,0,2:T(2,128)S(1)}, f32[2,128,128]{1,0,2:T(2,128)S(1)}, u32[]{:S(2)}, u32[]{:S(2)}) collective-permute-start(f32[2,128,128]{1,0,2:T(2,128)S(1)} %get-tuple-element.8), channel_id=1, source_target_pairs={{0,96},{1,97},{2,98},{3,99},{4,100},{5,101},{6,102},{7,103},{8,104... | collective-permute-start | bytes 393224 | tf_op jit(solution)/shard_map/ppermute | solution.py:171
  17.5 3.4 %collective-permute-start.12 = (f32[2,128,128]{1,0,2:T(2,128)S(1)}, f32[2,128,128]{1,0,2:T(2,128)S(1)}, u32[]{:S(2)}, u32[]{:S(2)}) collective-permute-start(f32[2,128,128]{1,0,2:T(2,128)S(1)} %get-tuple-element.9), channel_id=1, source_target_pairs={{0,64},{1,65},{2,66},{3,67},{4,68},{5,69},{6,70},{7,71},{8,72},{9,... | collective-permute-start | bytes 393224 | tf_op jit(solution)/shard_map/ppermute | solution.py:171
  18.8 4.9 %collective-permute-start.10 = (f32[2,128,128]{1,0,2:T(2,128)S(1)}, f32[2,128,128]{1,0,2:T(2,128)S(1)}, u32[]{:S(2)}, u32[]{:S(2)}) collective-permute-start(f32[2,128,128]{1,0,2:T(2,128)S(1)} %get-tuple-element.10), channel_id=1, source_target_pairs={{0,32},{1,33},{2,34},{3,35},{4,36},{5,37},{6,38},{7,39},{8,40},{9,... | collective-permute-start | bytes 393224 | tf_op jit(solution)/shard_map/ppermute | solution.py:171
  24.7 71.4 %all-gather.3.cloned.1.call-start = ((), (), s32[]{:S(2)}) async-start(), calls=%async_computation | async-start | bytes 2228224 | tf_op jit(solution)/shard_map/all_gather | solution.py:208
  24.7 8.3 %collective-permute-start.13 = (f32[256,128]{0,1:T(8,128)S(1)}, f32[256,128]{0,1:T(8,128)S(1)}, u32[]{:S(2)}, u32[]{:S(2)}) collective-permute-start(f32[256,128]{0,1:T(8,128)S(1)} %bitcast.46), channel_id=1, source_target_pairs={{0,0},{1,16},{2,32},{3,48},{4,64},{5,80},{6,96},{7,112},{8,1},{9,1... | collective-permute-start | bytes 393224 | tf_op jit(solution)/shard_map/ppermute | solution.py:171
  33.0 0.6 copy-start.4
  34.6 3.1 %collective-permute-start = (f32[128,128]{1,0:T(8,128)S(1)}, f32[128,128]{1,0:T(8,128)S(1)}, u32[]{:S(2)}, u32[]{:S(2)}) collective-permute-start(f32[128,128]{1,0:T(8,128)S(1)} %get-tuple-element.7), channel_id=1, source_target_pairs={{0,16},{1,17},{16,0},{17,1}} | collective-permute-start | bytes 196616 | tf_op jit(solution)/shard_map/ppermute | solution.py:171
  37.7 10.0 %collective-permute-start.1 = (f32[2,128,128]{2,1,0:T(8,128)S(1)}, f32[2,128,128]{2,1,0:T(8,128)S(1)}, u32[]{:S(2)}, u32[]{:S(2)}) collective-permute-start(f32[2,128,128]{2,1,0:T(8,128)S(1)} %maximum_select_fusion.1), channel_id=1, source_target_pairs={{0,1},{1,0},{16,17},{17,16}} | collective-permute-start | bytes 393224 | tf_op jit(solution)/shard_map/ppermute | solution.py:171
  47.8 5.1 %collective-permute-start.4 = (f32[3,128,128]{2,1,0:T(8,128)S(1)}, f32[3,128,128]{2,1,0:T(8,128)S(1)}, u32[]{:S(2)}, u32[]{:S(2)}) collective-permute-start(f32[3,128,128]{2,1,0:T(8,128)S(1)} %pad_maximum_fusion), channel_id=1, source_target_pairs={{0,8},{1,9},{16,24},{17,25}} | collective-permute-start | bytes 589832 | tf_op jit(solution)/shard_map/ppermute | solution.py:171
  49.1 5.1 %collective-permute-start.3 = (f32[3,128,128]{2,1,0:T(8,128)S(1)}, f32[3,128,128]{2,1,0:T(8,128)S(1)}, u32[]{:S(2)}, u32[]{:S(2)}) collective-permute-start(f32[3,128,128]{2,1,0:T(8,128)S(1)} %pad_maximum_fusion), channel_id=1, source_target_pairs={{0,12},{1,13},{16,28},{17,29}} | collective-permute-start | bytes 589832 | tf_op jit(solution)/shard_map/ppermute | solution.py:171
  50.4 6.7 %collective-permute-start.2 = (f32[3,128,128]{2,1,0:T(8,128)S(1)}, f32[3,128,128]{2,1,0:T(8,128)S(1)}, u32[]{:S(2)}, u32[]{:S(2)}) collective-permute-start(f32[3,128,128]{2,1,0:T(8,128)S(1)} %pad_maximum_fusion), channel_id=1, source_target_pairs={{0,4},{1,5},{16,20},{17,21}} | collective-permute-start | bytes 589832 | tf_op jit(solution)/shard_map/ppermute | solution.py:171
  57.1 4.4 %collective-permute-start.7 = (f32[3,128,128]{2,1,0:T(8,128)S(1)}, f32[3,128,128]{2,1,0:T(8,128)S(1)}, u32[]{:S(2)}, u32[]{:S(2)}) collective-permute-start(f32[3,128,128]{2,1,0:T(8,128)S(1)} %add_select_fusion.1), channel_id=1, source_target_pairs={{0,64},{1,65},{4,68},{5,69},{8,72},{9,73},{12,76},{13,77},{16,80},... | collective-permute-start | bytes 589832 | tf_op jit(solution)/shard_map/ppermute | solution.py:171
  58.4 4.4 %collective-permute-start.6 = (f32[3,128,128]{2,1,0:T(8,128)S(1)}, f32[3,128,128]{2,1,0:T(8,128)S(1)}, u32[]{:S(2)}, u32[]{:S(2)}) collective-permute-start(f32[3,128,128]{2,1,0:T(8,128)S(1)} %add_select_fusion.1), channel_id=1, source_target_pairs={{0,96},{1,97},{4,100},{5,101},{8,104},{9,105},{12,108},{13,109},{1... | collective-permute-start | bytes 589832 | tf_op jit(solution)/shard_map/ppermute | solution.py:171
  59.7 6.0 %collective-permute-start.5 = (f32[3,128,128]{2,1,0:T(8,128)S(1)}, f32[3,128,128]{2,1,0:T(8,128)S(1)}, u32[]{:S(2)}, u32[]{:S(2)}) collective-permute-start(f32[3,128,128]{2,1,0:T(8,128)S(1)} %add_select_fusion.1), channel_id=1, source_target_pairs={{0,32},{1,33},{4,36},{5,37},{8,40},{9,41},{12,44},{13,45},{16,48},... | collective-permute-start | bytes 589832 | tf_op jit(solution)/shard_map/ppermute | solution.py:171
  65.8 4.5 %collective-permute-start.8 = (f32[3,128,128]{2,1,0:T(8,128)S(1)}, f32[3,128,128]{2,1,0:T(8,128)S(1)}, u32[]{:S(2)}, u32[]{:S(2)}) collective-permute-start(f32[3,128,128]{2,1,0:T(8,128)S(1)} %add_select_fusion), channel_id=1, source_target_pairs={{0,3},{1,2},{4,7},{5,6},{8,11},{9,10},{12,15},{13,14},{16,19},{17,... | collective-permute-start | bytes 589832 | tf_op jit(solution)/shard_map/ppermute | solution.py:171
  96.1 3.4 %copy-start = (f32[2048,1024]{1,0:T(8,128)S(1)}, f32[2048,1024]{1,0:T(8,128)}, u32[]{:S(2)}) copy-start(f32[2048,1024]{1,0:T(8,128)} %a_ref.1) | copy-start | bytes 25165828
  99.5 1.6 %copy-start.1 = (f32[2048,256]{1,0:T(8,128)S(1)}, f32[2048,256]{1,0:T(8,128)}, u32[]{:S(2)}) copy-start(f32[2048,256]{1,0:T(8,128)} %all-gather.3.cloned.1.call-done.row_ref) | copy-start | bytes 6291460
  101.1 0.9 copy-start.2
  102.0 0.9 copy-start.3
Sparse Core Ops, SparseCore 0:
  24.8 25.6 all-gather.4
  52.7 43.4 all-gather.2

commit v2 on v1

v2 whole, which is shorter than its diff:
```python
import functools

import jax
import jax.numpy as jnp
from jax import lax
from jax.experimental import pallas as pl
from jax.experimental.pallas import tpu as pltpu
from jax.sharding import PartitionSpec as P

BLOCK = 128
WIDE = 2 * BLOCK
GROUP = 8
SHIFTS = (0, 1, 3, 2)
F32 = jnp.float32
BF16 = jnp.bfloat16
AXES = ("row", "col")
NT = (((1,), (1,)), ((), ()))
NN = (((1,), (0,)), ((), ()))


def exact(left, right, dims):
    return lax.dot_general(
        left, right, dims, precision=lax.Precision.HIGHEST, preferred_element_type=F32
    )


def eliminate(matrix):
    lane = lax.broadcasted_iota(jnp.int32, (8, BLOCK), 1)
    sub = lax.broadcasted_iota(jnp.int32, (8, BLOCK), 0)
    rows = [matrix[8 * i : 8 * i + 8, :] for i in range(BLOCK // 8)]
    for first in range(0, BLOCK, GROUP):
        at = first // 8
        cols = {}
        for j in range(GROUP):
            for i in range(at, BLOCK // 8):
                cols[j, i] = jnp.broadcast_to(rows[i][:, first + j : first + j + 1], (8, BLOCK))
        for j in range(GROUP):
            k = first + j
            s = k % 8
            here = lane == k
            pivot = 1.0 / cols[j, at][s : s + 1, :]
            row = jnp.where(here[:1], 1.0, rows[at][s : s + 1, :])
            heads = {m: cols[m, at][s : s + 1, :] for m in range(j + 1, GROUP)}
            for i in range(at, BLOCK // 8):
                factor = cols[j, i] * pivot
                if i == at:
                    factor = jnp.where(sub > s, factor, 0.0)
                    rows[i] = jnp.where(here & (sub > s), 0.0, rows[i]) - factor * row
                else:
                    rows[i] = jnp.where(here, 0.0, rows[i]) - factor * row
                for m in range(j + 1, GROUP):
                    cols[m, i] = cols[m, i] - factor * heads[m]
    return jnp.concatenate(rows, axis=0)


def factor_block(matrix):
    done = eliminate(matrix)
    r = lax.broadcasted_iota(jnp.int32, (BLOCK, BLOCK), 0)
    c = lax.broadcasted_iota(jnp.int32, (BLOCK, BLOCK), 1)
    pivots = jnp.sum(jnp.where(r == c, done, 0.0), axis=1, keepdims=True)
    scale = lax.rsqrt(pivots)
    scale = scale * (1.5 - 0.5 * pivots * scale * scale)
    upper = jnp.where(r <= c, done, 0.0) * scale
    inverse = jnp.where(r > c, done, jnp.where(r == c, 1.0, 0.0)) * scale
    return upper.T, inverse


def head_kernel(mine_ref, other_ref, lower_ref, inverse_ref):
    first = lax.axis_index("row") % 2 == 0
    zero = jnp.zeros((BLOCK, BLOCK), F32)
    l00, i00 = factor_block(jnp.where(first, mine_ref[0], other_ref[0]))
    l10 = exact(jnp.where(first, other_ref[0], mine_ref[0]), i00, NT)
    rest = jnp.where(first, other_ref[1], mine_ref[1]) - exact(l10, l10, NT)
    l11, i11 = factor_block(rest)
    i10 = -exact(i11, exact(l10, i00, NN), NN)
    lower_ref[0, :, :BLOCK] = l00
    lower_ref[0, :, BLOCK:] = zero
    lower_ref[1, :, :BLOCK] = l10
    lower_ref[1, :, BLOCK:] = l11
    inverse_ref[:BLOCK, :BLOCK] = i00
    inverse_ref[:BLOCK, BLOCK:] = zero
    inverse_ref[BLOCK:, :BLOCK] = i10
    inverse_ref[BLOCK:, BLOCK:] = i11


def head(mine, other):
    return pl.pallas_call(
        head_kernel,
        out_shape=(
            jax.ShapeDtypeStruct((2, BLOCK, WIDE), F32),
            jax.ShapeDtypeStruct((WIDE, WIDE), F32),
        ),
        cost_estimate=pl.CostEstimate(flops=10**8, bytes_accessed=10**6, transcendentals=0),
        name="head",
    )(mine, other)


def turn_kernel(in_ref, out_ref):
    for p in range(2):
        span = slice(p * BLOCK, (p + 1) * BLOCK)
        out_ref[:, span] = in_ref[span, :].T


def turn(block):
    return pl.pallas_call(
        turn_kernel, out_shape=jax.ShapeDtypeStruct((BLOCK, WIDE), F32), name="turn"
    )(block)


def split(x):
    high = x.astype(BF16)
    return high, (x - high.astype(F32)).astype(BF16)


def update_kernel(
    lower_ref, inverse_ref, row0_ref, row1_ref, row2_ref, row3_ref, tall_ref, beside_ref, a_ref, out_ref, factor_ref,
    a_buf, row_buf, factor_buf, col_buf, right_ref, a_sem, row_sem, col_sem, out_sem, factor_sem,
):
    my_row = lax.axis_index("row")
    my_col = lax.axis_index("col")
    x, y = my_col // 4, my_col % 4
    even = my_row % 2 == 0
    count, _, cols = a_ref.shape
    blocks = cols // BLOCK

    place = []
    for far in SHIFTS:
        for near in SHIFTS:
            dx = jnp.where(even, far, near)
            dy = jnp.where(even, near, far)
            place.append((x - dx + 4) % 4 * 4 + (y - dy + 4) % 4)

    def start(src, dst, sem):
        copy = pltpu.make_async_copy(src, dst, sem)
        copy.start()
        return copy

    col_in = []
    for b, d in enumerate(SHIFTS):
        depth = (my_row // 2 - d + 4) % 4 * 2
        col_in.append(start(tall_ref.at[b], col_buf.at[depth + my_row % 2], col_sem.at[b]))
        col_in.append(start(beside_ref.at[b], col_buf.at[depth + 1 - my_row % 2], col_sem.at[4 + b]))
    row_in = [
        start(ref, row_buf.at[a], row_sem.at[a])
        for a, ref in enumerate((row0_ref, row1_ref, row2_ref, row3_ref))
    ]
    a_in = [start(a_ref.at[place[t]], a_buf.at[t], a_sem.at[t]) for t in range(count)]

    high, low = split(inverse_ref[...])
    by_left = jnp.concatenate([high, high, low], axis=1)
    by_right = jnp.concatenate([high, low, high], axis=1)
    for copy in col_in:
        copy.wait()
    for b in range(0, blocks, 2):
        span = slice(b * BLOCK, (b + 2) * BLOCK)
        high, low = split(jnp.concatenate([col_buf[b], col_buf[b + 1]], axis=1))
        stack = jnp.concatenate([high, low, high], axis=0)
        part = lax.dot_general(by_left, stack, NN, preferred_element_type=F32)
        if b == 0:
            known = jnp.concatenate([lower_ref[jnp.minimum(my_col, 1)].T, part[:, BLOCK:]], axis=1)
            part = jnp.where(my_col < 2, known, part)
        high, low = split(part)
        right_ref[0:WIDE, span] = high
        right_ref[WIDE : 2 * WIDE, span] = low
        right_ref[2 * WIDE : 3 * WIDE, span] = high

    out = []
    for a in range(4):
        row_in[a].wait()
        high, low = split(row_buf[a].reshape(4 * BLOCK, WIDE))
        left = jnp.concatenate([high, high, low], axis=1)
        part = lax.dot_general(left, by_right, NT, preferred_element_type=F32)
        factor_buf[a] = part.reshape(4, BLOCK, WIDE)
        for s in range(4):
            t = 4 * a + s

            @pl.when((my_row < 2) & (place[t] == 0))
            def _():
                factor_buf[a, s] = lower_ref[jnp.minimum(my_row, 1)]

        for s in range(4):
            t = 4 * a + s
            out.append(start(factor_buf.at[a, s], factor_ref.at[place[t]], factor_sem.at[t]))
        high, low = split(factor_buf[a].reshape(4 * BLOCK, WIDE))
        left = jnp.concatenate([high, high, low], axis=1)
        for s in range(4):
            a_in[4 * a + s].wait()
        mine = slice(4 * a, 4 * a + 4)
        for n in range(0, cols, WIDE):
            span = slice(n, n + WIDE)
            part = lax.dot_general(left, right_ref[:, span], NN, preferred_element_type=F32)
            a_buf[mine, :, span] = a_buf[mine, :, span] - part.reshape(4, BLOCK, WIDE)
        for s in range(4):
            t = 4 * a + s
            out.append(start(a_buf.at[t], out_ref.at[place[t]], out_sem.at[t]))
    for copy in out:
        copy.wait()


def update(lower, inverse, row_parts, col_parts, stored):
    rows, cols = stored.shape
    count = rows // BLOCK
    here = pl.BlockSpec(memory_space=pltpu.VMEM)
    there = pl.BlockSpec(memory_space=pl.ANY)
    trailing, factor = pl.pallas_call(
        update_kernel,
        in_specs=[here] * 2 + [there] * 7,
        out_specs=[there] * 2,
        out_shape=(
            jax.ShapeDtypeStruct((count, BLOCK, cols), F32),
            jax.ShapeDtypeStruct((count, BLOCK, WIDE), F32),
        ),
        scratch_shapes=[
            pltpu.VMEM((count, BLOCK, cols), F32),
            pltpu.VMEM((4, 4, BLOCK, WIDE), F32),
            pltpu.VMEM((4, 4, BLOCK, WIDE), F32),
            pltpu.VMEM((cols // BLOCK, WIDE, BLOCK), F32),
            pltpu.VMEM((3 * WIDE, cols), BF16),
            pltpu.SemaphoreType.DMA((count,)),
            pltpu.SemaphoreType.DMA((4,)),
            pltpu.SemaphoreType.DMA((cols // BLOCK,)),
            pltpu.SemaphoreType.DMA((count,)),
            pltpu.SemaphoreType.DMA((count,)),
        ],
        compiler_params=pltpu.CompilerParams(vmem_limit_bytes=56 * 2**20),
        name="update",
    )(lower, inverse, *row_parts, *col_parts, stored.reshape(count, BLOCK, cols))
    return trailing.reshape(rows, cols), factor.reshape(rows, WIDE)


def on_device(stored, n_row, n_col):
    my_row = lax.axis_index("row")
    my_col = lax.axis_index("col")
    core = my_row % 2
    depth = my_row // 2

    def at(r, c):
        return r * n_col + c

    def send(x, pairs):
        return lax.ppermute(x, AXES, pairs)

    def near(phase, d):
        pairs = []
        for r in range(n_row):
            for c in range(n_col):
                x, y = divmod(c, 4)
                if (r % 2 == 0) == (phase == 1):
                    pairs.append((at(r, c), at(r, x * 4 + (y + d) % 4)))
                else:
                    pairs.append((at(r, c), at(r, (x + d) % 4 * 4 + y)))
        return pairs

    every_row, every_col = range(n_row), range(n_col)

    corner = stored[:BLOCK, :BLOCK]
    got = [send(corner, [(at(r, c), at(r + 2 * d, c)) for r in (0, 1) for c in (0, 1)]) for d in SHIFTS[1:]]
    strip = stored[:BLOCK].reshape(BLOCK, n_row // 2, 2, BLOCK)
    keep = lax.dynamic_index_in_dim(strip, core, 2, False).transpose(1, 0, 2)
    give = lax.dynamic_index_in_dim(strip, 1 - core, 2, False).transpose(1, 0, 2)
    other = send(give, [(at(r, c), at(1 - r, c)) for r in (0, 1) for c in every_col])
    both = jnp.where(core == 0, jnp.stack([keep, other], 1), jnp.stack([other, keep], 1))
    corner = jnp.where(depth == 0, corner, got[0] + got[1] + got[2])
    corner, both = lax.optimization_barrier((corner, both))

    got = [send(corner, [(at(r, c), at(r, c + 4 * d)) for r in every_row for c in (0, 1)]) for d in SHIFTS[1:]]
    parts = [
        send(both[d], [(at(r, c), at(r + 2 * d, c)) for r in (0, 1) for c in every_col])
        for d in SHIFTS[1:]
    ]
    corner = jnp.where(my_col < 2, corner, got[0] + got[1] + got[2])
    block = jnp.where(depth == 0, both[0], parts[0] + parts[1] + parts[2]).reshape(WIDE, BLOCK)
    corner, block = lax.optimization_barrier((corner, block))

    got = [
        send(corner, [(at(r, 4 * x + y), at(r, 4 * x + (y ^ e))) for r in every_row for x in range(4) for y in (0, 1)])
        for e in (1, 2, 3)
    ]
    block_row = send(block, [(at(r, c), at(c % n_row, 2 * r + c // n_row)) for r in every_row for c in every_col])
    y = my_col % 4
    left = jnp.where(y == 0, corner, jnp.where(y == 1, got[0], jnp.where(y == 2, got[1], got[2])))
    right = jnp.where(y == 1, corner, jnp.where(y == 0, got[0], jnp.where(y == 3, got[1], got[2])))
    mine = jnp.stack([left, right])
    mine, block_row, block = lax.optimization_barrier((mine, block_row, block))

    swap = [(at(r, c), at(r + 1 - 2 * (r % 2), c)) for r in every_row for c in every_col]
    other = send(mine, swap)
    turned = turn(block_row)
    line = [turned] + [send(turned, near(1, d)) for d in SHIFTS[1:]]
    tall = [block] + [
        send(block, [(at(r, c), at((r + 2 * d) % n_row, c)) for r in every_row for c in every_col])
        for d in SHIFTS[1:]
    ]
    line = jnp.stack(line)
    tall = jnp.stack(tall)
    mine, other, line, tall = lax.optimization_barrier((mine, other, line, tall))

    row_parts = [line] + [send(line, near(2, d)) for d in SHIFTS[1:]]
    beside = send(tall, swap)
    lower, inverse = head(mine, other)
    return update(lower, inverse, row_parts, [tall, beside], stored)


def solution(mesh):
    body = functools.partial(on_device, n_row=mesh.shape["row"], n_col=mesh.shape["col"])
    return jax.shard_map(
        body,
        mesh=mesh,
        in_specs=(P("row", "col"),),
        out_specs=(P("row", "col"), P("row", None)),
        check_vma=False,
    )
```

time: 124 us -> 96.8 us (0.78)
  waiting for transfers between devices: 34.1 us -> 13.5 us
  starting transfers between devices: 32.6 us -> 48.5 us
  between operations: 14.4 us -> 1.24 us
  local copies, waits for them, and re-layouts: 12.7 us -> 4.57 us
  Pallas kernels: 28.1 us -> 26.4 us
    ppermute x14 -> x25, starting transfers between devices: 32.6 us -> 48.5 us  [send(): return lax.ppermute(x, AXES, pairs)]
    ppermute x14 -> x25, waiting for transfers between devices: 24.5 us -> 13.5 us  [send(): return lax.ppermute(x, AXES, pairs)]
    all_gather x2 -> x0, waiting for transfers between devices: 9.53 us -> none  [the longest x1 9.53 us: on_device(): row_part = lax.all_gather(turned.T, 'col', axis=0, tiled=True)]
    unnamed x11 -> x18, local copies, waits for them, and re-layouts: 7.52 us -> 1.68 us
    pallas_call x1, Pallas kernels: 14.2 us -> 10.5 us  [head(): pl.pallas_call(head_kernel, out_shape=(jax.ShapeDtypeStruct((2, BLOCK, WI...]
    pallas_call x1 -> x2, Pallas kernels: 13.9 us -> 15.8 us  [the longest x1 14.2 us: update(): pl.pallas_call(update_kernel, in_specs=[here] * 2 + [there] * 7, out_spec...]
    reshape x1 -> x0, local copies, waits for them, and re-layouts: 1.34 us -> none  [on_device(): col_part = col_part.transpose(1, 0, 2).reshape(WIDE, n_row * BLOCK)]
  transfers between devices with their start and end apart: 16 -> 25, of which waited for: 14 -> 7; matrix products, arithmetic and copies ran while one was open for 3% -> 4% of each run, Pallas kernels for 12% -> 11%
where the time goes in v2:
time: 96.8 us; the launch traced here: 96.2 us
  starting transfers between devices  48.5 us (50%)
  Pallas kernels  26.4 us (27%)
  waiting for transfers between devices  13.5 us (14%)
  local copies, waits for them, and re-layouts  4.57 us (5%)
  other arithmetic  1.97 us (2%)
  between operations  1.24 us (1%)
    ppermute x25, starting transfers between devices, send(): return lax.ppermute(x, AXES, pairs)  48.5 us
    pallas_call x1, Pallas kernels, update(): pl.pallas_call(update_kernel, in_specs=[here] * 2 + [there] * 7, out_spec...  14.2 us
    ppermute x25, waiting for transfers between devices, send(): return lax.ppermute(x, AXES, pairs)  13.5 us
    pallas_call x1, Pallas kernels, head(): pl.pallas_call(head_kernel, out_shape=(jax.ShapeDtypeStruct((2, BLOCK, WI...  10.5 us
  transfers between devices with their start and end apart: 25, of which 7 were waited for; matrix products, arithmetic and copies ran while one was open for 4% of the time, Pallas kernels for 11%

profile of v2, /device:TPU:1, one launch (start us, length us, event | category | flops | bytes accessed | tf_op | source)
XLA Modules:
  0.0 96.2 jit_solution(4886487597915891231)
XLA Ops:
  1.5 6.3 %collective-permute-start.2 = (f32[128,128]{1,0:T(8,128)S(1)}, f32[128,128]{1,0:T(8,128)S(1)}, u32[]{:S(2)}, u32[]{:S(2)}) collective-permute-start(f32[128,128]{1,0:T(8,128)S(1)} %slice.18), channel_id=1, source_target_pairs={{0,64},{1,65},{16,80},{17,81}} | collective-permute-start | bytes 196616 | tf_op jit(solution)/shard_map/ppermute | solution.py:241
  7.8 1.3 %collective-permute-start.1 = (f32[128,128]{1,0:T(8,128)S(1)}, f32[128,128]{1,0:T(8,128)S(1)}, u32[]{:S(2)}, u32[]{:S(2)}) collective-permute-start(f32[128,128]{1,0:T(8,128)S(1)} %slice.18), channel_id=1, source_target_pairs={{0,96},{1,97},{16,112},{17,113}} | collective-permute-start | bytes 196616 | tf_op jit(solution)/shard_map/ppermute | solution.py:241
  9.1 1.3 %collective-permute-start = (f32[128,128]{1,0:T(8,128)S(1)}, f32[128,128]{1,0:T(8,128)S(1)}, u32[]{:S(2)}, u32[]{:S(2)}) collective-permute-start(f32[128,128]{1,0:T(8,128)S(1)} %slice.18), channel_id=1, source_target_pairs={{0,32},{1,33},{16,48},{17,49}} | collective-permute-start | bytes 196616 | tf_op jit(solution)/shard_map/ppermute | solution.py:241
  10.4 1.1 %slice.19 = f32[128,1024]{1,0:T(8,128)S(1)} slice(f32[2048,1024]{1,0:T(8,128)} %param.1), slice={[0:128], [0:1024]} | slice | bytes 1048576 | tf_op jit(solution)/shard_map/slice | solution.py:258
  12.5 2.9 %collective-permute-start.3 = (f32[4,128,128]{2,1,0:T(8,128)S(1)}, f32[4,128,128]{2,1,0:T(8,128)S(1)}, u32[]{:S(2)}, u32[]{:S(2)}) collective-permute-start(f32[4,128,128]{2,1,0:T(8,128)S(1)} %bitcast.45), channel_id=1, source_target_pairs={{0,16},{1,17},{2,18},{3,19},{4,20},{5,21},{6,22},{7,23},{8,24},{9,... | collective-permute-start | bytes 786440 | tf_op jit(solution)/shard_map/ppermute | solution.py:241
  16.5 1.3 %collective-permute-start.6 = (f32[128,128]{1,0:T(8,128)S(1)}, f32[128,128]{1,0:T(8,128)S(1)}, u32[]{:S(2)}, u32[]{:S(2)}) collective-permute-start(f32[128,128]{1,0:T(8,128)S(1)} %add_select_fusion.1), channel_id=1, source_target_pairs={{0,8},{1,9},{16,24},{17,25},{32,40},{33,41},{48,56},{49,57},{64,72... | collective-permute-start | bytes 196616 | tf_op jit(solution)/shard_map/ppermute | solution.py:241
  17.8 1.3 %collective-permute-start.5 = (f32[128,128]{1,0:T(8,128)S(1)}, f32[128,128]{1,0:T(8,128)S(1)}, u32[]{:S(2)}, u32[]{:S(2)}) collective-permute-start(f32[128,128]{1,0:T(8,128)S(1)} %add_select_fusion.1), channel_id=1, source_target_pairs={{0,12},{1,13},{16,28},{17,29},{32,44},{33,45},{48,60},{49,61},{64,... | collective-permute-start | bytes 196616 | tf_op jit(solution)/shard_map/ppermute | solution.py:241
  19.1 1.3 %collective-permute-start.4 = (f32[128,128]{1,0:T(8,128)S(1)}, f32[128,128]{1,0:T(8,128)S(1)}, u32[]{:S(2)}, u32[]{:S(2)}) collective-permute-start(f32[128,128]{1,0:T(8,128)S(1)} %add_select_fusion.1), channel_id=1, source_target_pairs={{0,4},{1,5},{16,20},{17,21},{32,36},{33,37},{48,52},{49,53},{64,68... | collective-permute-start | bytes 196616 | tf_op jit(solution)/shard_map/ppermute | solution.py:241
  20.5 1.3 %collective-permute-start.8 = (f32[2,128,128]{2,1,0:T(8,128)S(1)}, f32[2,128,128]{2,1,0:T(8,128)S(1)}, u32[]{:S(2)}, u32[]{:S(2)}) collective-permute-start(f32[2,128,128]{2,1,0:T(8,128)S(1)} %get-tuple-element.32), channel_id=1, source_target_pairs={{0,96},{1,97},{2,98},{3,99},{4,100},{5,101},{6,102},{7,103},{8,104... | collective-permute-start | bytes 393224 | tf_op jit(solution)/shard_map/ppermute | solution.py:241
  21.8 1.3 %collective-permute-start.9 = (f32[2,128,128]{2,1,0:T(8,128)S(1)}, f32[2,128,128]{2,1,0:T(8,128)S(1)}, u32[]{:S(2)}, u32[]{:S(2)}) collective-permute-start(f32[2,128,128]{2,1,0:T(8,128)S(1)} %get-tuple-element.33), channel_id=1, source_target_pairs={{0,64},{1,65},{2,66},{3,67},{4,68},{5,69},{6,70},{7,71},{8,72},{9,... | collective-permute-start | bytes 393224 | tf_op jit(solution)/shard_map/ppermute | solution.py:241
  23.1 1.3 %collective-permute-start.7 = (f32[2,128,128]{2,1,0:T(8,128)S(1)}, f32[2,128,128]{2,1,0:T(8,128)S(1)}, u32[]{:S(2)}, u32[]{:S(2)}) collective-permute-start(f32[2,128,128]{2,1,0:T(8,128)S(1)} %get-tuple-element.34), channel_id=1, source_target_pairs={{0,32},{1,33},{2,34},{3,35},{4,36},{5,37},{6,38},{7,39},{8,40},{9,... | collective-permute-start | bytes 393224 | tf_op jit(solution)/shard_map/ppermute | solution.py:241
  24.4 1.2 %collective-permute-done.9 = f32[2,128,128]{2,1,0:T(8,128)S(1)} collective-permute-done((f32[2,128,128]{2,1,0:T(8,128)S(1)}, f32[2,128,128]{2,1,0:T(8,128)S(1)}, u32[]{:S(2)}, u32[]{:S(2)}) %collective-permute-start.9) | collective-permute-done | bytes 131104 | tf_op jit(solution)/shard_map/ppermute | solution.py:241
  25.7 2.8 %collective-permute-done.7 = f32[2,128,128]{2,1,0:T(8,128)S(1)} collective-permute-done((f32[2,128,128]{2,1,0:T(8,128)S(1)}, f32[2,128,128]{2,1,0:T(8,128)S(1)}, u32[]{:S(2)}, u32[]{:S(2)}) %collective-permute-start.7) | collective-permute-done | bytes 131104 | tf_op jit(solution)/shard_map/ppermute | solution.py:241
  28.5 1.3 %collective-permute-start.12 = (f32[128,128]{1,0:T(8,128)S(1)}, f32[128,128]{1,0:T(8,128)S(1)}, u32[]{:S(2)}, u32[]{:S(2)}) collective-permute-start(f32[128,128]{1,0:T(8,128)S(1)} %add_select_fusion), channel_id=1, source_target_pairs={{0,3},{1,2},{4,7},{5,6},{8,11},{9,10},{12,15},{13,14},{16,19},{17,... | collective-permute-start | bytes 196616 | tf_op jit(solution)/shard_map/ppermute | solution.py:241
  29.8 1.3 %collective-permute-start.11 = (f32[128,128]{1,0:T(8,128)S(1)}, f32[128,128]{1,0:T(8,128)S(1)}, u32[]{:S(2)}, u32[]{:S(2)}) collective-permute-start(f32[128,128]{1,0:T(8,128)S(1)} %add_select_fusion), channel_id=1, source_target_pairs={{0,2},{1,3},{4,6},{5,7},{8,10},{9,11},{12,14},{13,15},{16,18},{17,... | collective-permute-start | bytes 196616 | tf_op jit(solution)/shard_map/ppermute | solution.py:241
  31.1 3.2 %collective-permute-start.10 = (f32[128,128]{1,0:T(8,128)S(1)}, f32[128,128]{1,0:T(8,128)S(1)}, u32[]{:S(2)}, u32[]{:S(2)}) collective-permute-start(f32[128,128]{1,0:T(8,128)S(1)} %add_select_fusion), channel_id=1, source_target_pairs={{0,1},{1,0},{4,5},{5,4},{8,9},{9,8},{12,13},{13,12},{16,17},{17,16... | collective-permute-start | bytes 196616 | tf_op jit(solution)/shard_map/ppermute | solution.py:241
  34.4 1.9 %collective-permute-start.13 = (f32[256,128]{1,0:T(8,128)S(1)}, f32[256,128]{1,0:T(8,128)S(1)}, u32[]{:S(2)}, u32[]{:S(2)}) collective-permute-start(f32[256,128]{1,0:T(8,128)S(1)} %bitcast.40), channel_id=1, source_target_pairs={{0,0},{1,16},{2,32},{3,48},{4,64},{5,80},{6,96},{7,112},{8,1},{9,1... | collective-permute-start | bytes 393224 | tf_op jit(solution)/shard_map/ppermute | solution.py:241
  37.2 5.9 %collective-permute-done.13.in_ref = f32[256,128]{1,0:T(8,128)S(1)} collective-permute-done((f32[256,128]{1,0:T(8,128)S(1)}, f32[256,128]{1,0:T(8,128)S(1)}, u32[]{:S(2)}, u32[]{:S(2)}) %collective-permute-start.13) | collective-permute-done | bytes 131104 | tf_op jit(solution)/shard_map/ppermute | solution.py:241
  43.7 1.6 %turn.1 = f32[128,256]{1,0:T(8,128)} custom-call(f32[256,128]{1,0:T(8,128)} %copy-done.7), custom_call_target="tpu_custom_call" | custom-call | tf_op jit(solution)/shard_map/turn/pallas_call | solution.py:105
  45.4 3.0 %collective-permute-start.17 = (f32[128,256]{1,0:T(8,128)}, f32[128,256]{1,0:T(8,128)S(1)}, u32[]{:S(2)}, u32[]{:S(2)}) collective-permute-start(f32[128,256]{1,0:T(8,128)} %turn.1), channel_id=1, source_target_pairs={{0,2},{1,3},{2,0},{3,1},{4,6},{5,7},{6,4},{7,5},{8,10},{9,11},{10,... | collective-permute-start | bytes 393224 | tf_op jit(solution)/shard_map/ppermute | solution.py:241
  48.4 1.1 %collective-permute-start.16 = (f32[128,256]{1,0:T(8,128)}, f32[128,256]{1,0:T(8,128)S(1)}, u32[]{:S(2)}, u32[]{:S(2)}) collective-permute-start(f32[128,256]{1,0:T(8,128)} %turn.1), channel_id=1, source_target_pairs={{0,3},{1,0},{2,1},{3,2},{4,7},{5,4},{6,5},{7,6},{8,11},{9,8},{10,9... | collective-permute-start | bytes 393224 | tf_op jit(solution)/shard_map/ppermute | solution.py:241
  49.9 1.0 collective-permute-start.20
  50.9 3.5 %collective-permute-start.19 = (f32[256,128]{1,0:T(8,128)S(1)}, f32[256,128]{1,0:T(8,128)S(1)}, u32[]{:S(2)}, u32[]{:S(2)}) collective-permute-start(f32[256,128]{1,0:T(8,128)S(1)} %bitcast.42), channel_id=1, source_target_pairs={{0,96},{1,97},{2,98},{3,99},{4,100},{5,101},{6,102},{7,103},{8,104... | collective-permute-start | bytes 393224 | tf_op jit(solution)/shard_map/ppermute | solution.py:241
  54.3 1.7 %collective-permute-start.18 = (f32[256,128]{1,0:T(8,128)S(1)}, f32[256,128]{1,0:T(8,128)S(1)}, u32[]{:S(2)}, u32[]{:S(2)}) collective-permute-start(f32[256,128]{1,0:T(8,128)S(1)} %bitcast.43), channel_id=1, source_target_pairs={{0,32},{1,33},{2,34},{3,35},{4,36},{5,37},{6,38},{7,39},{8,40},{9,... | collective-permute-start | bytes 393224 | tf_op jit(solution)/shard_map/ppermute | solution.py:241
  56.1 2.5 %collective-permute-start.14 = (f32[2,128,128]{2,1,0:T(8,128)S(1)}, f32[2,128,128]{2,1,0:T(8,128)S(1)}, u32[]{:S(2)}, u32[]{:S(2)}) collective-permute-start(f32[2,128,128]{2,1,0:T(8,128)S(1)} %pad_maximum_fusion.2.mine_ref), channel_id=1, source_target_pairs={{0,16},{1,17},{2,18},{3,19},{4,20},{5,21},{6,22},{7,23},{8,24},{9,... | collective-permute-start | bytes 393224 | tf_op jit(solution)/shard_map/ppermute | solution.py:241
  58.6 0.9 pad_maximum_fusion.row0_ref
  60.2 4.6 %collective-permute-start.24 = (f32[4,256,128]{2,1,0:T(8,128)S(1)}, f32[4,256,128]{2,1,0:T(8,128)S(1)}, u32[]{:S(2)}, u32[]{:S(2)}) collective-permute-start(f32[4,256,128]{2,1,0:T(8,128)S(1)} %pad_maximum_fusion.1.tall_ref), channel_id=1, source_target_pairs={{0,16},{1,17},{2,18},{3,19},{4,20},{5,21},{6,22},{7,23},{8,24},{9,... | collective-permute-start | bytes 1572872 | tf_op jit(solution)/shard_map/ppermute | solution.py:241
  64.8 1.2 %collective-permute-start.23 = (f32[4,128,256]{2,1,0:T(8,128)S(1)}, f32[4,128,256]{2,1,0:T(8,128)S(1)}, u32[]{:S(2)}, u32[]{:S(2)}) collective-permute-start(f32[4,128,256]{2,1,0:T(8,128)S(1)} %pad_maximum_fusion.row0_ref), channel_id=1, source_target_pairs={{0,8},{1,9},{2,10},{3,11},{4,12},{5,13},{6,14},{7,15},{8,0},{9,1},... | collective-permute-start | bytes 1572872 | tf_op jit(solution)/shard_map/ppermute | solution.py:241
  66.0 1.8 %collective-permute-start.22 = (f32[4,128,256]{2,1,0:T(8,128)S(1)}, f32[4,128,256]{2,1,0:T(8,128)S(1)}, u32[]{:S(2)}, u32[]{:S(2)}) collective-permute-start(f32[4,128,256]{2,1,0:T(8,128)S(1)} %pad_maximum_fusion.row0_ref), channel_id=1, source_target_pairs={{0,12},{1,13},{2,14},{3,15},{4,0},{5,1},{6,2},{7,3},{8,4},{9,5},{1... | collective-permute-start | bytes 1572872 | tf_op jit(solution)/shard_map/ppermute | solution.py:241
  68.3 10.5 %head.1 = (f32[2,128,256]{2,1,0:T(8,128)}, f32[256,256]{1,0:T(8,128)}) custom-call(f32[2,128,128]{2,1,0:T(8,128)} %copy-done.6, f32[2,128,128]{2,1,0:T(8,128)} %copy-done.8), custom_call_target="tpu_custom_call" | custom-call | flops 100000000 | bytes 1000000 | tf_op jit(solution)/shard_map/head/pallas_call | solution.py:87
  78.9 1.9 %collective-permute-done.22.row2_ref = f32[4,128,256]{2,1,0:T(8,128)S(1)} collective-permute-done((f32[4,128,256]{2,1,0:T(8,128)S(1)}, f32[4,128,256]{2,1,0:T(8,128)S(1)}, u32[]{:S(2)}, u32[]{:S(2)}) %collective-permute-start.22) | collective-permute-done | bytes 524320 | tf_op jit(solution)/shard_map/ppermute | solution.py:241
  81.8 14.2 %update.1 = (f32[16,128,1024]{2,1,0:T(8,128)}, f32[16,128,256]{2,1,0:T(8,128)}) custom-call(f32[2,128,256]{2,1,0:T(8,128)} %get-tuple-element.26.lower_ref, f32[256,256]{1,0:T(8,128)} %get-tuple-element.27.inverse_ref, f32[4,128,256]{2,1,0:T(8,128)} %copy-done, f32[4,128,256]{2,1,0:T(8,128)} %copy-done.5, f32[4,128,256]{2,1,0:T(8,128)} %copy-done.4, ...), custom_call_target="tpu_custom_call" | custom-call | tf_op jit(solution)/shard_map/update/pallas_call | solution.py:205
  (54 shorter events, 7.1 us)
Async XLA Ops:
  1.5 13.9 %collective-permute-start.2 = (f32[128,128]{1,0:T(8,128)S(1)}, f32[128,128]{1,0:T(8,128)S(1)}, u32[]{:S(2)}, u32[]{:S(2)}) collective-permute-start(f32[128,128]{1,0:T(8,128)S(1)} %slice.18), channel_id=1, source_target_pairs={{0,64},{1,65},{16,80},{17,81}} | collective-permute-start | bytes 196616 | tf_op jit(solution)/shard_map/ppermute | solution.py:241
  7.8 7.6 %collective-permute-start.1 = (f32[128,128]{1,0:T(8,128)S(1)}, f32[128,128]{1,0:T(8,128)S(1)}, u32[]{:S(2)}, u32[]{:S(2)}) collective-permute-start(f32[128,128]{1,0:T(8,128)S(1)} %slice.18), channel_id=1, source_target_pairs={{0,96},{1,97},{16,112},{17,113}} | collective-permute-start | bytes 196616 | tf_op jit(solution)/shard_map/ppermute | solution.py:241
  9.1 6.3 %collective-permute-start = (f32[128,128]{1,0:T(8,128)S(1)}, f32[128,128]{1,0:T(8,128)S(1)}, u32[]{:S(2)}, u32[]{:S(2)}) collective-permute-start(f32[128,128]{1,0:T(8,128)S(1)} %slice.18), channel_id=1, source_target_pairs={{0,32},{1,33},{16,48},{17,49}} | collective-permute-start | bytes 196616 | tf_op jit(solution)/shard_map/ppermute | solution.py:241
  12.5 4.0 %collective-permute-start.3 = (f32[4,128,128]{2,1,0:T(8,128)S(1)}, f32[4,128,128]{2,1,0:T(8,128)S(1)}, u32[]{:S(2)}, u32[]{:S(2)}) collective-permute-start(f32[4,128,128]{2,1,0:T(8,128)S(1)} %bitcast.45), channel_id=1, source_target_pairs={{0,16},{1,17},{2,18},{3,19},{4,20},{5,21},{6,22},{7,23},{8,24},{9,... | collective-permute-start | bytes 786440 | tf_op jit(solution)/shard_map/ppermute | solution.py:241
  16.5 6.6 %collective-permute-start.6 = (f32[128,128]{1,0:T(8,128)S(1)}, f32[128,128]{1,0:T(8,128)S(1)}, u32[]{:S(2)}, u32[]{:S(2)}) collective-permute-start(f32[128,128]{1,0:T(8,128)S(1)} %add_select_fusion.1), channel_id=1, source_target_pairs={{0,8},{1,9},{16,24},{17,25},{32,40},{33,41},{48,56},{49,57},{64,72... | collective-permute-start | bytes 196616 | tf_op jit(solution)/shard_map/ppermute | solution.py:241
  17.8 6.6 %collective-permute-start.5 = (f32[128,128]{1,0:T(8,128)S(1)}, f32[128,128]{1,0:T(8,128)S(1)}, u32[]{:S(2)}, u32[]{:S(2)}) collective-permute-start(f32[128,128]{1,0:T(8,128)S(1)} %add_select_fusion.1), channel_id=1, source_target_pairs={{0,12},{1,13},{16,28},{17,29},{32,44},{33,45},{48,60},{49,61},{64,... | collective-permute-start | bytes 196616 | tf_op jit(solution)/shard_map/ppermute | solution.py:241
  19.1 5.3 %collective-permute-start.4 = (f32[128,128]{1,0:T(8,128)S(1)}, f32[128,128]{1,0:T(8,128)S(1)}, u32[]{:S(2)}, u32[]{:S(2)}) collective-permute-start(f32[128,128]{1,0:T(8,128)S(1)} %add_select_fusion.1), channel_id=1, source_target_pairs={{0,4},{1,5},{16,20},{17,21},{32,36},{33,37},{48,52},{49,53},{64,68... | collective-permute-start | bytes 196616 | tf_op jit(solution)/shard_map/ppermute | solution.py:241
  20.5 4.0 %collective-permute-start.8 = (f32[2,128,128]{2,1,0:T(8,128)S(1)}, f32[2,128,128]{2,1,0:T(8,128)S(1)}, u32[]{:S(2)}, u32[]{:S(2)}) collective-permute-start(f32[2,128,128]{2,1,0:T(8,128)S(1)} %get-tuple-element.32), channel_id=1, source_target_pairs={{0,96},{1,97},{2,98},{3,99},{4,100},{5,101},{6,102},{7,103},{8,104... | collective-permute-start | bytes 393224 | tf_op jit(solution)/shard_map/ppermute | solution.py:241
  21.8 3.9 %collective-permute-start.9 = (f32[2,128,128]{2,1,0:T(8,128)S(1)}, f32[2,128,128]{2,1,0:T(8,128)S(1)}, u32[]{:S(2)}, u32[]{:S(2)}) collective-permute-start(f32[2,128,128]{2,1,0:T(8,128)S(1)} %get-tuple-element.33), channel_id=1, source_target_pairs={{0,64},{1,65},{2,66},{3,67},{4,68},{5,69},{6,70},{7,71},{8,72},{9,... | collective-permute-start | bytes 393224 | tf_op jit(solution)/shard_map/ppermute | solution.py:241
  23.1 5.4 %collective-permute-start.7 = (f32[2,128,128]{2,1,0:T(8,128)S(1)}, f32[2,128,128]{2,1,0:T(8,128)S(1)}, u32[]{:S(2)}, u32[]{:S(2)}) collective-permute-start(f32[2,128,128]{2,1,0:T(8,128)S(1)} %get-tuple-element.34), channel_id=1, source_target_pairs={{0,32},{1,33},{2,34},{3,35},{4,36},{5,37},{6,38},{7,39},{8,40},{9,... | collective-permute-start | bytes 393224 | tf_op jit(solution)/shard_map/ppermute | solution.py:241
  28.5 7.8 %collective-permute-start.12 = (f32[128,128]{1,0:T(8,128)S(1)}, f32[128,128]{1,0:T(8,128)S(1)}, u32[]{:S(2)}, u32[]{:S(2)}) collective-permute-start(f32[128,128]{1,0:T(8,128)S(1)} %add_select_fusion), channel_id=1, source_target_pairs={{0,3},{1,2},{4,7},{5,6},{8,11},{9,10},{12,15},{13,14},{16,19},{17,... | collective-permute-start | bytes 196616 | tf_op jit(solution)/shard_map/ppermute | solution.py:241
  29.8 6.5 %collective-permute-start.11 = (f32[128,128]{1,0:T(8,128)S(1)}, f32[128,128]{1,0:T(8,128)S(1)}, u32[]{:S(2)}, u32[]{:S(2)}) collective-permute-start(f32[128,128]{1,0:T(8,128)S(1)} %add_select_fusion), channel_id=1, source_target_pairs={{0,2},{1,3},{4,6},{5,7},{8,10},{9,11},{12,14},{13,15},{16,18},{17,... | collective-permute-start | bytes 196616 | tf_op jit(solution)/shard_map/ppermute | solution.py:241
  31.1 6.0 %collective-permute-start.10 = (f32[128,128]{1,0:T(8,128)S(1)}, f32[128,128]{1,0:T(8,128)S(1)}, u32[]{:S(2)}, u32[]{:S(2)}) collective-permute-start(f32[128,128]{1,0:T(8,128)S(1)} %add_select_fusion), channel_id=1, source_target_pairs={{0,1},{1,0},{4,5},{5,4},{8,9},{9,8},{12,13},{13,12},{16,17},{17,16... | collective-permute-start | bytes 196616 | tf_op jit(solution)/shard_map/ppermute | solution.py:241
  34.4 8.7 %collective-permute-start.13 = (f32[256,128]{1,0:T(8,128)S(1)}, f32[256,128]{1,0:T(8,128)S(1)}, u32[]{:S(2)}, u32[]{:S(2)}) collective-permute-start(f32[256,128]{1,0:T(8,128)S(1)} %bitcast.40), channel_id=1, source_target_pairs={{0,0},{1,16},{2,32},{3,48},{4,64},{5,80},{6,96},{7,112},{8,1},{9,1... | collective-permute-start | bytes 393224 | tf_op jit(solution)/shard_map/ppermute | solution.py:241
  37.2 31.2 %copy-start.6 = (f32[2,128,128]{2,1,0:T(8,128)}, f32[2,128,128]{2,1,0:T(8,128)S(1)}, u32[]{:S(2)}) copy-start(f32[2,128,128]{2,1,0:T(8,128)S(1)} %pad_maximum_fusion.2.mine_ref) | copy-start | bytes 393220
  45.4 9.0 %collective-permute-start.17 = (f32[128,256]{1,0:T(8,128)}, f32[128,256]{1,0:T(8,128)S(1)}, u32[]{:S(2)}, u32[]{:S(2)}) collective-permute-start(f32[128,256]{1,0:T(8,128)} %turn.1), channel_id=1, source_target_pairs={{0,2},{1,3},{2,0},{3,1},{4,6},{5,7},{6,4},{7,5},{8,10},{9,11},{10,... | collective-permute-start | bytes 393224 | tf_op jit(solution)/shard_map/ppermute | solution.py:241
  48.4 7.6 %collective-permute-start.16 = (f32[128,256]{1,0:T(8,128)}, f32[128,256]{1,0:T(8,128)S(1)}, u32[]{:S(2)}, u32[]{:S(2)}) collective-permute-start(f32[128,256]{1,0:T(8,128)} %turn.1), channel_id=1, source_target_pairs={{0,3},{1,0},{2,1},{3,2},{4,7},{5,4},{6,5},{7,6},{8,11},{9,8},{10,9... | collective-permute-start | bytes 393224 | tf_op jit(solution)/shard_map/ppermute | solution.py:241
  49.6 9.0 %collective-permute-start.15 = (f32[128,256]{1,0:T(8,128)}, f32[128,256]{1,0:T(8,128)S(1)}, u32[]{:S(2)}, u32[]{:S(2)}) collective-permute-start(f32[128,256]{1,0:T(8,128)} %turn.1), channel_id=1, source_target_pairs={{0,1},{1,2},{2,3},{3,0},{4,5},{5,6},{6,7},{7,4},{8,9},{9,10},{10,1... | collective-permute-start | bytes 393224 | tf_op jit(solution)/shard_map/ppermute | solution.py:241
  49.9 9.6 %collective-permute-start.20 = (f32[256,128]{1,0:T(8,128)S(1)}, f32[256,128]{1,0:T(8,128)S(1)}, u32[]{:S(2)}, u32[]{:S(2)}) collective-permute-start(f32[256,128]{1,0:T(8,128)S(1)} %bitcast.41), channel_id=1, source_target_pairs={{0,64},{1,65},{2,66},{3,67},{4,68},{5,69},{6,70},{7,71},{8,72},{9,... | collective-permute-start | bytes 393224 | tf_op jit(solution)/shard_map/ppermute | solution.py:241
  50.9 8.7 %collective-permute-start.19 = (f32[256,128]{1,0:T(8,128)S(1)}, f32[256,128]{1,0:T(8,128)S(1)}, u32[]{:S(2)}, u32[]{:S(2)}) collective-permute-start(f32[256,128]{1,0:T(8,128)S(1)} %bitcast.42), channel_id=1, source_target_pairs={{0,96},{1,97},{2,98},{3,99},{4,100},{5,101},{6,102},{7,103},{8,104... | collective-permute-start | bytes 393224 | tf_op jit(solution)/shard_map/ppermute | solution.py:241
  54.3 5.8 %collective-permute-start.18 = (f32[256,128]{1,0:T(8,128)S(1)}, f32[256,128]{1,0:T(8,128)S(1)}, u32[]{:S(2)}, u32[]{:S(2)}) collective-permute-start(f32[256,128]{1,0:T(8,128)S(1)} %bitcast.43), channel_id=1, source_target_pairs={{0,32},{1,33},{2,34},{3,35},{4,36},{5,37},{6,38},{7,39},{8,40},{9,... | collective-permute-start | bytes 393224 | tf_op jit(solution)/shard_map/ppermute | solution.py:241
  56.1 4.1 %collective-permute-start.14 = (f32[2,128,128]{2,1,0:T(8,128)S(1)}, f32[2,128,128]{2,1,0:T(8,128)S(1)}, u32[]{:S(2)}, u32[]{:S(2)}) collective-permute-start(f32[2,128,128]{2,1,0:T(8,128)S(1)} %pad_maximum_fusion.2.mine_ref), channel_id=1, source_target_pairs={{0,16},{1,17},{2,18},{3,19},{4,20},{5,21},{6,22},{7,23},{8,24},{9,... | collective-permute-start | bytes 393224 | tf_op jit(solution)/shard_map/ppermute | solution.py:241
  59.5 21.3 %copy-start = (f32[4,128,256]{2,1,0:T(8,128)}, f32[4,128,256]{2,1,0:T(8,128)S(1)}, u32[]{:S(2)}) copy-start(f32[4,128,256]{2,1,0:T(8,128)S(1)} %pad_maximum_fusion.row0_ref) | copy-start | bytes 1572868
  60.2 20.6 %copy-start.1 = (f32[4,256,128]{2,1,0:T(8,128)}, f32[4,256,128]{2,1,0:T(8,128)S(1)}, u32[]{:S(2)}) copy-start(f32[4,256,128]{2,1,0:T(8,128)S(1)} %pad_maximum_fusion.1.tall_ref) | copy-start | bytes 1572868
  60.2 8.1 %copy-start.8 = (f32[2,128,128]{2,1,0:T(8,128)}, f32[2,128,128]{2,1,0:T(8,128)S(1)}, u32[]{:S(2)}) copy-start(f32[2,128,128]{2,1,0:T(8,128)S(1)} %collective-permute-done.14.other_ref) | copy-start | bytes 393220
  60.2 18.6 %collective-permute-start.24 = (f32[4,256,128]{2,1,0:T(8,128)S(1)}, f32[4,256,128]{2,1,0:T(8,128)S(1)}, u32[]{:S(2)}, u32[]{:S(2)}) collective-permute-start(f32[4,256,128]{2,1,0:T(8,128)S(1)} %pad_maximum_fusion.1.tall_ref), channel_id=1, source_target_pairs={{0,16},{1,17},{2,18},{3,19},{4,20},{5,21},{6,22},{7,23},{8,24},{9,... | collective-permute-start | bytes 1572872 | tf_op jit(solution)/shard_map/ppermute | solution.py:241
  64.8 14.1 %collective-permute-start.23 = (f32[4,128,256]{2,1,0:T(8,128)S(1)}, f32[4,128,256]{2,1,0:T(8,128)S(1)}, u32[]{:S(2)}, u32[]{:S(2)}) collective-permute-start(f32[4,128,256]{2,1,0:T(8,128)S(1)} %pad_maximum_fusion.row0_ref), channel_id=1, source_target_pairs={{0,8},{1,9},{2,10},{3,11},{4,12},{5,13},{6,14},{7,15},{8,0},{9,1},... | collective-permute-start | bytes 1572872 | tf_op jit(solution)/shard_map/ppermute | solution.py:241
  66.0 14.8 %collective-permute-start.22 = (f32[4,128,256]{2,1,0:T(8,128)S(1)}, f32[4,128,256]{2,1,0:T(8,128)S(1)}, u32[]{:S(2)}, u32[]{:S(2)}) collective-permute-start(f32[4,128,256]{2,1,0:T(8,128)S(1)} %pad_maximum_fusion.row0_ref), channel_id=1, source_target_pairs={{0,12},{1,13},{2,14},{3,15},{4,0},{5,1},{6,2},{7,3},{8,4},{9,5},{1... | collective-permute-start | bytes 1572872 | tf_op jit(solution)/shard_map/ppermute | solution.py:241
  67.8 13.0 %collective-permute-start.21 = (f32[4,128,256]{2,1,0:T(8,128)S(1)}, f32[4,128,256]{2,1,0:T(8,128)S(1)}, u32[]{:S(2)}, u32[]{:S(2)}) collective-permute-start(f32[4,128,256]{2,1,0:T(8,128)S(1)} %pad_maximum_fusion.row0_ref), channel_id=1, source_target_pairs={{0,4},{1,5},{2,6},{3,7},{4,8},{5,9},{6,10},{7,11},{8,12},{9,13},{1... | collective-permute-start | bytes 1572872 | tf_op jit(solution)/shard_map/ppermute | solution.py:241
  78.9 2.0 %copy-start.2 = (f32[4,256,128]{2,1,0:T(8,128)}, f32[4,256,128]{2,1,0:T(8,128)S(1)}, u32[]{:S(2)}) copy-start(f32[4,256,128]{2,1,0:T(8,128)S(1)} %collective-permute-done.24.beside_ref) | copy-start | bytes 1572868
  78.9 2.0 %copy-start.3 = (f32[4,128,256]{2,1,0:T(8,128)}, f32[4,128,256]{2,1,0:T(8,128)S(1)}, u32[]{:S(2)}) copy-start(f32[4,128,256]{2,1,0:T(8,128)S(1)} %collective-permute-done.23.row3_ref) | copy-start | bytes 1572868
  80.8 1.0 %copy-start.5 = (f32[4,128,256]{2,1,0:T(8,128)}, f32[4,128,256]{2,1,0:T(8,128)S(1)}, u32[]{:S(2)}) copy-start(f32[4,128,256]{2,1,0:T(8,128)S(1)} %collective-permute-done.21.row1_ref) | copy-start | bytes 1572868
  (2 other events, 1.5 us)

commit v3 on v2

--- a/solution.py
+++ b/solution.py
@@ -68,9 +68,9 @@
 def head_kernel(mine_ref, other_ref, lower_ref, inverse_ref):
     first = lax.axis_index("row") % 2 == 0
     zero = jnp.zeros((BLOCK, BLOCK), F32)
-    l00, i00 = factor_block(jnp.where(first, mine_ref[0], other_ref[0]))
-    l10 = exact(jnp.where(first, other_ref[0], mine_ref[0]), i00, NT)
-    rest = jnp.where(first, other_ref[1], mine_ref[1]) - exact(l10, l10, NT)
+    l00, i00 = factor_block(jnp.where(first, mine_ref[:, :BLOCK], other_ref[:, :BLOCK]))
+    l10 = exact(jnp.where(first, mine_ref[:, BLOCK:], other_ref[:, BLOCK:]), i00, NT)
+    rest = jnp.where(first, other_ref[:, BLOCK:], mine_ref[:, BLOCK:]) - exact(l10, l10, NT)
     l11, i11 = factor_block(rest)
     i10 = -exact(i11, exact(l10, i00, NN), NN)
     lower_ref[0, :, :BLOCK] = l00
@@ -91,20 +91,71 @@
             jax.ShapeDtypeStruct((WIDE, WIDE), F32),
         ),
         cost_estimate=pl.CostEstimate(flops=10**8, bytes_accessed=10**6, transcendentals=0),
+        compiler_params=pltpu.CompilerParams(vmem_limit_bytes=20 * 2**20),
         name="head",
     )(mine, other)
 
 
-def turn_kernel(in_ref, out_ref):
-    for p in range(2):
-        span = slice(p * BLOCK, (p + 1) * BLOCK)
-        out_ref[:, span] = in_ref[span, :].T
-
-
-def turn(block):
+def hold_kernel(stored_ref, held_ref, sem):
+    copy = pltpu.make_async_copy(stored_ref, held_ref, sem)
+    copy.start()
+    copy.wait()
+
+
+def hold(stored):
     return pl.pallas_call(
-        turn_kernel, out_shape=jax.ShapeDtypeStruct((BLOCK, WIDE), F32), name="turn"
-    )(block)
+        hold_kernel,
+        in_specs=[pl.BlockSpec(memory_space=pltpu.HBM)],
+        out_specs=pl.BlockSpec(memory_space=pltpu.VMEM),
+        out_shape=pltpu.VMEM(stored.shape, F32),
+        scratch_shapes=[pltpu.SemaphoreType.DMA(())],
+        compiler_params=pltpu.CompilerParams(vmem_limit_bytes=46 * 2**20),
+        cost_estimate=pl.CostEstimate(flops=0, bytes_accessed=2**23, transcendentals=0),
+        name="hold",
+    )(stored)
+
+
+def open_kernel(stored_ref, strip_ref, keep_ref, give_ref, sem):
+    copy = pltpu.make_async_copy(stored_ref.at[pl.ds(0, BLOCK)], strip_ref, sem)
+    copy.start()
+    first = lax.axis_index("row") % 2 == 0
+    last = keep_ref.shape[0] - 1
+    copy.wait()
+    keep_ref[last] = strip_ref[:, :BLOCK]
+    give_ref[last] = strip_ref[:, :BLOCK]
+    for b in range(last):
+        even = strip_ref[:, 2 * b * BLOCK : (2 * b + 1) * BLOCK]
+        odd = strip_ref[:, (2 * b + 1) * BLOCK : (2 * b + 2) * BLOCK]
+        keep_ref[b] = jnp.where(first, even, odd).T
+        give_ref[b] = jnp.where(first, odd, even).T
+
+
+def open_strip(stored):
+    cols = stored.shape[1]
+    part = jax.ShapeDtypeStruct((cols // WIDE + 1, BLOCK, BLOCK), F32)
+    return pl.pallas_call(
+        open_kernel,
+        in_specs=[pl.BlockSpec(memory_space=pl.ANY)],
+        out_shape=(jax.ShapeDtypeStruct((BLOCK, cols), F32), part, part),
+        scratch_shapes=[pltpu.SemaphoreType.DMA(())],
+        name="open",
+    )(stored)
+
+
+def pack_kernel(keep_ref, other_ref, *out_refs):
+    first = lax.axis_index("row") % 2 == 0
+    last = keep_ref.shape[0] - 1
+    for b, out_ref in enumerate(out_refs):
+        for n, t in enumerate((b, last)):
+            out_ref[:, 2 * n * BLOCK : (2 * n + 1) * BLOCK] = jnp.where(first, keep_ref[t], other_ref[t])
+            out_ref[:, (2 * n + 1) * BLOCK : (2 * n + 2) * BLOCK] = jnp.where(first, other_ref[t], keep_ref[t])
+
+
+def pack(keep, other):
+    count = keep.shape[0] - 1
+    return pl.pallas_call(
+        pack_kernel, out_shape=(jax.ShapeDtypeStruct((BLOCK, 2 * WIDE), F32),) * count, name="pack"
+    )(keep, other)
 
 
 def split(x):
@@ -114,7 +165,7 @@
 
 def update_kernel(
     lower_ref, inverse_ref, row0_ref, row1_ref, row2_ref, row3_ref, tall_ref, beside_ref, a_ref, out_ref, factor_ref,
-    a_buf, row_buf, factor_buf, col_buf, right_ref, a_sem, row_sem, col_sem, out_sem, factor_sem,
+    a_buf, row_buf, factor_buf, col_buf, right_ref, row_sem, col_sem, out_sem, factor_sem,
 ):
     my_row = lax.axis_index("row")
     my_col = lax.axis_index("col")
@@ -135,16 +186,15 @@
         copy.start()
         return copy
 
-    col_in = []
-    for b, d in enumerate(SHIFTS):
-        depth = (my_row // 2 - d + 4) % 4 * 2
-        col_in.append(start(tall_ref.at[b], col_buf.at[depth + my_row % 2], col_sem.at[b]))
-        col_in.append(start(beside_ref.at[b], col_buf.at[depth + 1 - my_row % 2], col_sem.at[4 + b]))
+    core = my_row % 2
+    col_in = [
+        start(tall_ref, col_buf.at[core], col_sem.at[0]),
+        start(beside_ref, col_buf.at[1 - core], col_sem.at[1]),
+    ]
     row_in = [
         start(ref, row_buf.at[a], row_sem.at[a])
         for a, ref in enumerate((row0_ref, row1_ref, row2_ref, row3_ref))
     ]
-    a_in = [start(a_ref.at[place[t]], a_buf.at[t], a_sem.at[t]) for t in range(count)]
 
     high, low = split(inverse_ref[...])
     by_left = jnp.concatenate([high, high, low], axis=1)
@@ -153,7 +203,7 @@
         copy.wait()
     for b in range(0, blocks, 2):
         span = slice(b * BLOCK, (b + 2) * BLOCK)
-        high, low = split(jnp.concatenate([col_buf[b], col_buf[b + 1]], axis=1))
+        high, low = split(jnp.concatenate([col_buf[0, :, span], col_buf[1, :, span]], axis=0))
         stack = jnp.concatenate([high, low, high], axis=0)
         part = lax.dot_general(by_left, stack, NN, preferred_element_type=F32)
         if b == 0:
@@ -183,13 +233,12 @@
             out.append(start(factor_buf.at[a, s], factor_ref.at[place[t]], factor_sem.at[t]))
         high, low = split(factor_buf[a].reshape(4 * BLOCK, WIDE))
         left = jnp.concatenate([high, high, low], axis=1)
-        for s in range(4):
-            a_in[4 * a + s].wait()
-        mine = slice(4 * a, 4 * a + 4)
         for n in range(0, cols, WIDE):
             span = slice(n, n + WIDE)
             part = lax.dot_general(left, right_ref[:, span], NN, preferred_element_type=F32)
-            a_buf[mine, :, span] = a_buf[mine, :, span] - part.reshape(4, BLOCK, WIDE)
+            for s in range(4):
+                t = 4 * a + s
+                a_buf[t, :, span] = a_ref[place[t], :, span] - part[s * BLOCK : (s + 1) * BLOCK]
         for s in range(4):
             t = 4 * a + s
             out.append(start(a_buf.at[t], out_ref.at[place[t]], out_sem.at[t]))
@@ -197,14 +246,14 @@
         copy.wait()
 
 
-def update(lower, inverse, row_parts, col_parts, stored):
-    rows, cols = stored.shape
-    count = rows // BLOCK
+def update(lower, inverse, row_parts, col_parts, held):
+    count, _, cols = held.shape
+    rows = count * BLOCK
     here = pl.BlockSpec(memory_space=pltpu.VMEM)
-    there = pl.BlockSpec(memory_space=pl.ANY)
+    there = pl.BlockSpec(memory_space=pltpu.HBM)
     trailing, factor = pl.pallas_call(
         update_kernel,
-        in_specs=[here] * 2 + [there] * 7,
+        in_specs=[here] * 2 + [there] * 6 + [here],
         out_specs=[there] * 2,
         out_shape=(
             jax.ShapeDtypeStruct((count, BLOCK, cols), F32),
@@ -214,17 +263,16 @@
             pltpu.VMEM((count, BLOCK, cols), F32),
             pltpu.VMEM((4, 4, BLOCK, WIDE), F32),
             pltpu.VMEM((4, 4, BLOCK, WIDE), F32),
-            pltpu.VMEM((cols // BLOCK, WIDE, BLOCK), F32),
+            pltpu.VMEM((2, BLOCK, cols), F32),
             pltpu.VMEM((3 * WIDE, cols), BF16),
-            pltpu.SemaphoreType.DMA((count,)),
             pltpu.SemaphoreType.DMA((4,)),
-            pltpu.SemaphoreType.DMA((cols // BLOCK,)),
+            pltpu.SemaphoreType.DMA((2,)),
             pltpu.SemaphoreType.DMA((count,)),
             pltpu.SemaphoreType.DMA((count,)),
         ],
-        compiler_params=pltpu.CompilerParams(vmem_limit_bytes=56 * 2**20),
+        compiler_params=pltpu.CompilerParams(vmem_limit_bytes=30 * 2**20),
         name="update",
-    )(lower, inverse, *row_parts, *col_parts, stored.reshape(count, BLOCK, cols))
+    )(lower, inverse, *row_parts, *col_parts, held)
     return trailing.reshape(rows, cols), factor.reshape(rows, WIDE)
 
 
@@ -253,52 +301,45 @@
 
     every_row, every_col = range(n_row), range(n_col)
 
-    corner = stored[:BLOCK, :BLOCK]
-    got = [send(corner, [(at(r, c), at(r + 2 * d, c)) for r in (0, 1) for c in (0, 1)]) for d in SHIFTS[1:]]
-    strip = stored[:BLOCK].reshape(BLOCK, n_row // 2, 2, BLOCK)
-    keep = lax.dynamic_index_in_dim(strip, core, 2, False).transpose(1, 0, 2)
-    give = lax.dynamic_index_in_dim(strip, 1 - core, 2, False).transpose(1, 0, 2)
+    strip, keep, give = open_strip(stored)
     other = send(give, [(at(r, c), at(1 - r, c)) for r in (0, 1) for c in every_col])
-    both = jnp.where(core == 0, jnp.stack([keep, other], 1), jnp.stack([other, keep], 1))
-    corner = jnp.where(depth == 0, corner, got[0] + got[1] + got[2])
-    corner, both = lax.optimization_barrier((corner, both))
-
-    got = [send(corner, [(at(r, c), at(r, c + 4 * d)) for r in every_row for c in (0, 1)]) for d in SHIFTS[1:]]
+    tall = send(strip, [(at(r, c), at(r + 4, c)) for r in (0, 1) for c in every_col])
+    messages = pack(keep, other)
+
     parts = [
-        send(both[d], [(at(r, c), at(r + 2 * d, c)) for r in (0, 1) for c in every_col])
-        for d in SHIFTS[1:]
+        send(
+            message,
+            [(at(r, c), at(c % n_row, 2 * (2 * b + r) + c // n_row)) for r in (0, 1) for c in every_col],
+        )
+        for b, message in enumerate(messages)
     ]
-    corner = jnp.where(my_col < 2, corner, got[0] + got[1] + got[2])
-    block = jnp.where(depth == 0, both[0], parts[0] + parts[1] + parts[2]).reshape(WIDE, BLOCK)
-    corner, block = lax.optimization_barrier((corner, block))
-
-    got = [
-        send(corner, [(at(r, 4 * x + y), at(r, 4 * x + (y ^ e))) for r in every_row for x in range(4) for y in (0, 1)])
-        for e in (1, 2, 3)
-    ]
-    block_row = send(block, [(at(r, c), at(c % n_row, 2 * r + c // n_row)) for r in every_row for c in every_col])
-    y = my_col % 4
-    left = jnp.where(y == 0, corner, jnp.where(y == 1, got[0], jnp.where(y == 2, got[1], got[2])))
-    right = jnp.where(y == 1, corner, jnp.where(y == 0, got[0], jnp.where(y == 3, got[1], got[2])))
-    mine = jnp.stack([left, right])
-    mine, block_row, block = lax.optimization_barrier((mine, block_row, block))
-
+    total = parts[0] + parts[1] + parts[2] + parts[3]
+    block, corner = total[:, :WIDE], total[:, WIDE:]
+    block, corner = lax.optimization_barrier((block, corner))
+
+    near_y = [4 * x + y for x in range(4) for y in (0, 2)]
+    got = send(corner, [(at(r, c), at(r + 4, c)) for r in (0, 1) for c in near_y])
+    line = [block] + [send(block, near(1, d)) for d in SHIFTS[1:]]
+    corner = jnp.where(depth == 0, corner, got)
+    got = send(corner, [(at(r, c), at((r + 6) % n_row, c)) for r in (0, 1, 4, 5) for c in near_y])
+    corner = jnp.where(depth % 2 == 0, corner, got)
+    got = send(corner, [(at(r, c), at(r, c + 1)) for r in every_row for c in near_y])
+    corner = jnp.where(my_col % 2 == 0, corner, got)
+    line = jnp.stack(line)
+    corner, line, tall = lax.optimization_barrier((corner, line, tall))
+
+    row_parts = [line] + [send(line, near(2, d)) for d in SHIFTS[1:]]
+    tall = jnp.where(depth == 0, strip, tall)
+    got_tall = send(tall, [(at(r, c), at(r + 2, c)) for r in (0, 1, 4, 5) for c in every_col])
     swap = [(at(r, c), at(r + 1 - 2 * (r % 2), c)) for r in every_row for c in every_col]
-    other = send(mine, swap)
-    turned = turn(block_row)
-    line = [turned] + [send(turned, near(1, d)) for d in SHIFTS[1:]]
-    tall = [block] + [
-        send(block, [(at(r, c), at((r + 2 * d) % n_row, c)) for r in every_row for c in every_col])
-        for d in SHIFTS[1:]
-    ]
-    line = jnp.stack(line)
-    tall = jnp.stack(tall)
-    mine, other, line, tall = lax.optimization_barrier((mine, other, line, tall))
-
-    row_parts = [line] + [send(line, near(2, d)) for d in SHIFTS[1:]]
+    other = send(corner, swap)
+    lower, inverse = head(corner, other)
+    inverse, got_tall, tall, stored = lax.optimization_barrier((inverse, got_tall, tall, stored))
+
+    tall = jnp.where(depth % 2 == 0, tall, got_tall)
     beside = send(tall, swap)
-    lower, inverse = head(mine, other)
-    return update(lower, inverse, row_parts, [tall, beside], stored)
+    held = hold(stored.reshape(-1, BLOCK, stored.shape[1]))
+    return update(lower, inverse, row_parts, [tall, beside], held)
 
 
 def solution(mesh):

time: 96.8 us -> 85.8 us (0.89)
  starting transfers between devices: 48.5 us -> 35.4 us
  waiting for transfers between devices: 13.5 us -> 21.4 us
  local copies, waits for them, and re-layouts: 4.57 us -> 0.73 us
    ppermute x25 -> x18, starting transfers between devices: 48.5 us -> 35.4 us  [send(): return lax.ppermute(x, AXES, pairs)]
    ppermute x25 -> x18, waiting for transfers between devices: 13.5 us -> 21.4 us  [send(): return lax.ppermute(x, AXES, pairs)]
    slice x2 -> x1, local copies, waits for them, and re-layouts: 1.93 us -> 0.02 us  [on_device(): block, corner = (total[:, :WIDE], total[:, WIDE:])]
    pallas_call x1, Pallas kernels: 10.5 us -> 8.89 us  [head(): pl.pallas_call(head_kernel, out_shape=(jax.ShapeDtypeStruct((2, BLOCK, WI...]
    pallas_call x2 -> x4, Pallas kernels: 15.8 us -> 16.6 us  [the longest x1 8.99 us: update(): pl.pallas_call(update_kernel, in_specs=[here] * 2 + [there] * 6 + [here],...]
  transfers between devices with their start and end apart: 25 -> 18, of which waited for: 7 -> 8; matrix products, arithmetic and copies ran while one was open for 4% -> 0% of each run, Pallas kernels for 11% -> 14%
where the time goes in v3:
time: 85.8 us; the launch traced here: 85.3 us
  starting transfers between devices  35.4 us (41%)
  Pallas kernels  25.5 us (30%)
  waiting for transfers between devices  21.4 us (25%)
  other arithmetic  1.33 us (2%)
  between operations  1.04 us (1%)
    ppermute x18, starting transfers between devices, send(): return lax.ppermute(x, AXES, pairs)  35.4 us
    ppermute x18, waiting for transfers between devices, send(): return lax.ppermute(x, AXES, pairs)  21.4 us
    pallas_call x1, Pallas kernels, update(): pl.pallas_call(update_kernel, in_specs=[here] * 2 + [there] * 6 + [here],...  8.99 us
    pallas_call x1, Pallas kernels, head(): pl.pallas_call(head_kernel, out_shape=(jax.ShapeDtypeStruct((2, BLOCK, WI...  8.89 us
    pallas_call x1, Pallas kernels, hold(): pl.pallas_call(hold_kernel, in_specs=[pl.BlockSpec(memory_space=pltpu.HBM...  3.39 us
    pallas_call x1, Pallas kernels, pack(): pl.pallas_call(pack_kernel, out_shape=(jax.ShapeDtypeStruct((BLOCK, 2 * W...  2.12 us
    pallas_call x1, Pallas kernels, open_strip(): pl.pallas_call(open_kernel, in_specs=[pl.BlockSpec(memory_space=pl.ANY)],...  2.08 us
  transfers between devices with their start and end apart: 18, of which 8 were waited for; matrix products, arithmetic and copies ran while one was open for 0% of the time, Pallas kernels for 14%

profile of v3, /device:TPU:1, one launch (start us, length us, event | category | flops | bytes accessed | tf_op | source)
XLA Modules:
  0.0 85.3 jit_solution(5096760909885313835)
XLA Ops:
  0.6 2.1 %open.1 = (f32[128,1024]{1,0:T(8,128)}, f32[5,128,128]{2,1,0:T(8,128)}, f32[5,128,128]{2,1,0:T(8,128)}) custom-call(f32[2048,1024]{1,0:T(8,128)} %stored_ref.1), custom_call_target="tpu_custom_call" | custom-call | tf_op jit(solution)/shard_map/open/pallas_call | solution.py:136
  2.7 3.3 %collective-permute-start = (f32[5,128,128]{2,1,0:T(8,128)}, f32[5,128,128]{2,1,0:T(8,128)S(1)}, u32[]{:S(2)}, u32[]{:S(2)}) collective-permute-start(f32[5,128,128]{2,1,0:T(8,128)} %get-tuple-element.23), channel_id=1, source_target_pairs={{0,16},{1,17},{2,18},{3,19},{4,20},{5,21},{6,22},{7,23},{8,24},{9,... | collective-permute-start | bytes 983048 | tf_op jit(solution)/shard_map/ppermute | solution.py:289
  6.1 1.4 %collective-permute-done.other_ref = f32[5,128,128]{2,1,0:T(8,128)S(1)} collective-permute-done((f32[5,128,128]{2,1,0:T(8,128)}, f32[5,128,128]{2,1,0:T(8,128)S(1)}, u32[]{:S(2)}, u32[]{:S(2)}) %collective-permute-start) | collective-permute-done | bytes 327712 | tf_op jit(solution)/shard_map/ppermute | solution.py:289
  7.5 0.7 copy-done
  8.2 2.1 %pack.1 = (f32[128,512]{1,0:T(8,128)}, f32[128,512]{1,0:T(8,128)}, f32[128,512]{1,0:T(8,128)}, f32[128,512]{1,0:T(8,128)}) custom-call(f32[5,128,128]{2,1,0:T(8,128)} %get-tuple-element.22.keep_ref, f32[5,128,128]{2,1,0:T(8,128)} %copy-done), custom_call_target="tpu_custom_call" | custom-call | tf_op jit(solution)/shard_map/pack/pallas_call | solution.py:156
  10.3 5.2 %collective-permute-start.1 = (f32[128,512]{1,0:T(8,128)}, f32[128,512]{1,0:T(8,128)S(1)}, u32[]{:S(2)}, u32[]{:S(2)}) collective-permute-start(f32[128,512]{1,0:T(8,128)} %get-tuple-element.24), channel_id=1, source_target_pairs={{0,0},{1,16},{2,32},{3,48},{4,64},{5,80},{6,96},{7,112},{8,1},{9,1... | collective-permute-start | bytes 786440 | tf_op jit(solution)/shard_map/ppermute | solution.py:289
  15.5 3.6 %collective-permute-start.2 = (f32[128,512]{1,0:T(8,128)}, f32[128,512]{1,0:T(8,128)S(1)}, u32[]{:S(2)}, u32[]{:S(2)}) collective-permute-start(f32[128,512]{1,0:T(8,128)} %get-tuple-element.25), channel_id=1, source_target_pairs={{0,4},{1,20},{2,36},{3,52},{4,68},{5,84},{6,100},{7,116},{8,5},{9,... | collective-permute-start | bytes 786440 | tf_op jit(solution)/shard_map/ppermute | solution.py:289
  19.1 1.5 %collective-permute-start.3 = (f32[128,512]{1,0:T(8,128)}, f32[128,512]{1,0:T(8,128)S(1)}, u32[]{:S(2)}, u32[]{:S(2)}) collective-permute-start(f32[128,512]{1,0:T(8,128)} %get-tuple-element.26), channel_id=1, source_target_pairs={{0,8},{1,24},{2,40},{3,56},{4,72},{5,88},{6,104},{7,120},{8,9},{9,... | collective-permute-start | bytes 786440 | tf_op jit(solution)/shard_map/ppermute | solution.py:289
  20.6 2.8 %collective-permute-start.4 = (f32[128,512]{1,0:T(8,128)}, f32[128,512]{1,0:T(8,128)S(1)}, u32[]{:S(2)}, u32[]{:S(2)}) collective-permute-start(f32[128,512]{1,0:T(8,128)} %get-tuple-element.27), channel_id=1, source_target_pairs={{0,12},{1,28},{2,44},{3,60},{4,76},{5,92},{6,108},{7,124},{8,13},{... | collective-permute-start | bytes 786440 | tf_op jit(solution)/shard_map/ppermute | solution.py:289
  23.4 3.0 %collective-permute-done.1 = f32[128,512]{1,0:T(8,128)S(1)} collective-permute-done((f32[128,512]{1,0:T(8,128)}, f32[128,512]{1,0:T(8,128)S(1)}, u32[]{:S(2)}, u32[]{:S(2)}) %collective-permute-start.1) | collective-permute-done | bytes 262176 | tf_op jit(solution)/shard_map/ppermute | solution.py:289
  26.4 3.4 %collective-permute-done.3 = f32[128,512]{1,0:T(8,128)S(1)} collective-permute-done((f32[128,512]{1,0:T(8,128)}, f32[128,512]{1,0:T(8,128)S(1)}, u32[]{:S(2)}, u32[]{:S(2)}) %collective-permute-start.3) | collective-permute-done | bytes 262176 | tf_op jit(solution)/shard_map/ppermute | solution.py:289
  29.8 3.8 %collective-permute-done.4 = f32[128,512]{1,0:T(8,128)S(1)} collective-permute-done((f32[128,512]{1,0:T(8,128)}, f32[128,512]{1,0:T(8,128)S(1)}, u32[]{:S(2)}, u32[]{:S(2)}) %collective-permute-start.4) | collective-permute-done | bytes 262176 | tf_op jit(solution)/shard_map/ppermute | solution.py:289
  33.6 0.1 add_add_fusion
  33.7 1.3 %collective-permute-start.5 = (f32[128,256]{1,0:T(8,128)S(1)}, f32[128,256]{1,0:T(8,128)S(1)}, u32[]{:S(2)}, u32[]{:S(2)}) collective-permute-start(f32[128,256]{1,0:T(8,128)S(1)} %get-tuple-element.28), channel_id=1, source_target_pairs={{0,64},{2,66},{4,68},{6,70},{8,72},{10,74},{12,76},{14,78},{16,80}... | collective-permute-start | bytes 393224 | tf_op jit(solution)/shard_map/ppermute | solution.py:289
  35.0 3.0 %collective-permute-done.5 = f32[128,256]{1,0:T(8,128)S(1)} collective-permute-done((f32[128,256]{1,0:T(8,128)S(1)}, f32[128,256]{1,0:T(8,128)S(1)}, u32[]{:S(2)}, u32[]{:S(2)}) %collective-permute-start.5) | collective-permute-done | bytes 131104 | tf_op jit(solution)/shard_map/ppermute | solution.py:289
  38.0 1.3 %collective-permute-start.6 = (f32[128,256]{1,0:T(8,128)S(1)}, f32[128,256]{1,0:T(8,128)S(1)}, u32[]{:S(2)}, u32[]{:S(2)}) collective-permute-start(f32[128,256]{1,0:T(8,128)S(1)} %broadcast_select_fusion.2), channel_id=1, source_target_pairs={{0,96},{2,98},{4,100},{6,102},{8,104},{10,106},{12,108},{14,110},{... | collective-permute-start | bytes 393224 | tf_op jit(solution)/shard_map/ppermute | solution.py:289
  39.3 5.6 %collective-permute-start.11 = (f32[128,1024]{1,0:T(8,128)}, f32[128,1024]{1,0:T(8,128)S(1)}, u32[]{:S(2)}, u32[]{:S(2)}) collective-permute-start(f32[128,1024]{1,0:T(8,128)} %get-tuple-element.30), channel_id=1, source_target_pairs={{0,64},{1,65},{2,66},{3,67},{4,68},{5,69},{6,70},{7,71},{8,72},{9,... | collective-permute-start | bytes 1572872 | tf_op jit(solution)/shard_map/ppermute | solution.py:289
  45.0 1.3 %collective-permute-start.10 = (f32[128,256]{1,0:T(8,128)S(1)}, f32[128,256]{1,0:T(8,128)S(1)}, u32[]{:S(2)}, u32[]{:S(2)}) collective-permute-start(f32[128,256]{1,0:T(8,128)S(1)} %get-tuple-element.29), channel_id=1, source_target_pairs={{0,2},{1,3},{2,0},{3,1},{4,6},{5,7},{6,4},{7,5},{8,10},{9,11},{10,... | collective-permute-start | bytes 393224 | tf_op jit(solution)/shard_map/ppermute | solution.py:289
  46.3 1.5 %collective-permute-start.8 = (f32[128,256]{1,0:T(8,128)S(1)}, f32[128,256]{1,0:T(8,128)S(1)}, u32[]{:S(2)}, u32[]{:S(2)}) collective-permute-start(f32[128,256]{1,0:T(8,128)S(1)} %get-tuple-element.29), channel_id=1, source_target_pairs={{0,1},{1,2},{2,3},{3,0},{4,5},{5,6},{6,7},{7,4},{8,9},{9,10},{10,1... | collective-permute-start | bytes 393224 | tf_op jit(solution)/shard_map/ppermute | solution.py:289
  47.8 1.3 %collective-permute-start.7 = (f32[128,256]{1,0:T(8,128)S(1)}, f32[128,256]{1,0:T(8,128)S(1)}, u32[]{:S(2)}, u32[]{:S(2)}) collective-permute-start(f32[128,256]{1,0:T(8,128)S(1)} %broadcast_select_fusion.3), channel_id=1, source_target_pairs={{0,1},{2,3},{4,5},{6,7},{8,9},{10,11},{12,13},{14,15},{16,17},{18,... | collective-permute-start | bytes 393224 | tf_op jit(solution)/shard_map/ppermute | solution.py:289
  49.1 1.4 %collective-permute-done.10 = f32[128,256]{1,0:T(8,128)S(1)} collective-permute-done((f32[128,256]{1,0:T(8,128)S(1)}, f32[128,256]{1,0:T(8,128)S(1)}, u32[]{:S(2)}, u32[]{:S(2)}) %collective-permute-start.10) | collective-permute-done | bytes 131104 | tf_op jit(solution)/shard_map/ppermute | solution.py:289
  50.5 1.6 %collective-permute-done.8 = f32[128,256]{1,0:T(8,128)S(1)} collective-permute-done((f32[128,256]{1,0:T(8,128)S(1)}, f32[128,256]{1,0:T(8,128)S(1)}, u32[]{:S(2)}, u32[]{:S(2)}) %collective-permute-start.8) | collective-permute-done | bytes 131104 | tf_op jit(solution)/shard_map/ppermute | solution.py:289
  52.2 3.7 %collective-permute-done.11 = f32[128,1024]{1,0:T(8,128)S(1)} collective-permute-done((f32[128,1024]{1,0:T(8,128)}, f32[128,1024]{1,0:T(8,128)S(1)}, u32[]{:S(2)}, u32[]{:S(2)}) %collective-permute-start.11) | collective-permute-done | bytes 524320 | tf_op jit(solution)/shard_map/ppermute | solution.py:289
  55.8 1.1 %broadcast_select_fusion.1 = f32[128,1024]{1,0:T(8,128)S(1)} fusion(f32[128,1024]{1,0:T(8,128)} %get-tuple-element.30, f32[128,1024]{1,0:T(8,128)S(1)} %collective-permute-done.11, pred[]{:T(512)S(6)} %eq.17), kind=kLoop, calls=%fused_computation.3 | loop fusion | flops 131072 | bytes 1572865 | tf_op jit(solution)/shard_map/jit(_where)/select_n | solution.py:332
  57.0 1.3 %collective-permute-start.13 = (f32[128,1024]{1,0:T(8,128)S(1)}, f32[128,1024]{1,0:T(8,128)S(1)}, u32[]{:S(2)}, u32[]{:S(2)}) collective-permute-start(f32[128,1024]{1,0:T(8,128)S(1)} %broadcast_select_fusion.1), channel_id=1, source_target_pairs={{0,32},{1,33},{2,34},{3,35},{4,36},{5,37},{6,38},{7,39},{8,40},{9,... | collective-permute-start | bytes 1572872 | tf_op jit(solution)/shard_map/ppermute | solution.py:289
  58.3 1.6 %collective-permute-start.12 = (f32[128,256]{1,0:T(8,128)S(1)}, f32[128,256]{1,0:T(8,128)S(1)}, u32[]{:S(2)}, u32[]{:S(2)}) collective-permute-start(f32[128,256]{1,0:T(8,128)S(1)} %broadcast_select_fusion.4.mine_ref), channel_id=1, source_target_pairs={{0,16},{1,17},{2,18},{3,19},{4,20},{5,21},{6,22},{7,23},{8,24},{9,... | collective-permute-start | bytes 393224 | tf_op jit(solution)/shard_map/ppermute | solution.py:289
  59.9 1.2 %collective-permute-start.15 = (f32[4,128,256]{2,1,0:T(8,128)S(1)}, f32[4,128,256]{2,1,0:T(8,128)S(1)}, u32[]{:S(2)}, u32[]{:S(2)}) collective-permute-start(f32[4,128,256]{2,1,0:T(8,128)S(1)} %pad_maximum_fusion.row0_ref), channel_id=1, source_target_pairs={{0,12},{1,13},{2,14},{3,15},{4,0},{5,1},{6,2},{7,3},{8,4},{9,5},{1... | collective-permute-start | bytes 1572872 | tf_op jit(solution)/shard_map/ppermute | solution.py:289
  61.1 0.3 collective-permute-start.14
  61.4 8.9 %head.1 = (f32[2,128,256]{2,1,0:T(8,128)S(1)}, f32[256,256]{1,0:T(8,128)S(1)}) custom-call(f32[128,256]{1,0:T(8,128)S(1)} %broadcast_select_fusion.4.mine_ref, f32[128,256]{1,0:T(8,128)S(1)} %collective-permute-done.12.other_ref), custom_call_target="tpu_custom_call" | custom-call | flops 100000000 | bytes 1000000 | tf_op jit(solution)/shard_map/head/pallas_call | solution.py:87
  70.4 2.4 %collective-permute-start.17 = (f32[128,1024]{1,0:T(8,128)S(1)}, f32[128,1024]{1,0:T(8,128)S(1)}, u32[]{:S(2)}, u32[]{:S(2)}) collective-permute-start(f32[128,1024]{1,0:T(8,128)S(1)} %broadcast_select_fusion.tall_ref), channel_id=1, source_target_pairs={{0,16},{1,17},{2,18},{3,19},{4,20},{5,21},{6,22},{7,23},{8,24},{9,... | collective-permute-start | bytes 1572872 | tf_op jit(solution)/shard_map/ppermute | solution.py:289
  72.7 3.4 %hold.1.a_ref = f32[16,128,1024]{2,1,0:T(8,128)S(1)} custom-call(f32[16,128,1024]{2,1,0:T(8,128)} %bitcast.7), custom_call_target="tpu_custom_call" | custom-call | bytes 8388608 | tf_op jit(solution)/shard_map/hold/pallas_call | solution.py:106
  76.2 9.0 %update.1 = (f32[16,128,1024]{2,1,0:T(8,128)}, f32[16,128,256]{2,1,0:T(8,128)}) custom-call(f32[2,128,256]{2,1,0:T(8,128)S(1)} %get-tuple-element.32.lower_ref, f32[256,256]{1,0:T(8,128)S(1)} %get-tuple-element.35.inverse_ref, f32[4,128,256]{2,1,0:T(8,128)S(1)} %pad_maximum_fusion.row0_ref, f32[4,128,256]{2,1,0:T(8,128)S(1)} %collective-permute-done.14.row1_ref, ...), custom_call_target="tpu_custom_call" | custom-call | tf_op jit(solution)/shard_map/update/pallas_call | solution.py:254
  (19 shorter events, 0.2 us)
Async XLA Ops:
  2.7 4.8 %collective-permute-start = (f32[5,128,128]{2,1,0:T(8,128)}, f32[5,128,128]{2,1,0:T(8,128)S(1)}, u32[]{:S(2)}, u32[]{:S(2)}) collective-permute-start(f32[5,128,128]{2,1,0:T(8,128)} %get-tuple-element.23), channel_id=1, source_target_pairs={{0,16},{1,17},{2,18},{3,19},{4,20},{5,21},{6,22},{7,23},{8,24},{9,... | collective-permute-start | bytes 983048 | tf_op jit(solution)/shard_map/ppermute | solution.py:289
  7.5 0.7 copy-start
  10.3 16.0 %collective-permute-start.1 = (f32[128,512]{1,0:T(8,128)}, f32[128,512]{1,0:T(8,128)S(1)}, u32[]{:S(2)}, u32[]{:S(2)}) collective-permute-start(f32[128,512]{1,0:T(8,128)} %get-tuple-element.24), channel_id=1, source_target_pairs={{0,0},{1,16},{2,32},{3,48},{4,64},{5,80},{6,96},{7,112},{8,1},{9,1... | collective-permute-start | bytes 786440 | tf_op jit(solution)/shard_map/ppermute | solution.py:289
  15.5 10.9 %collective-permute-start.2 = (f32[128,512]{1,0:T(8,128)}, f32[128,512]{1,0:T(8,128)S(1)}, u32[]{:S(2)}, u32[]{:S(2)}) collective-permute-start(f32[128,512]{1,0:T(8,128)} %get-tuple-element.25), channel_id=1, source_target_pairs={{0,4},{1,20},{2,36},{3,52},{4,68},{5,84},{6,100},{7,116},{8,5},{9,... | collective-permute-start | bytes 786440 | tf_op jit(solution)/shard_map/ppermute | solution.py:289
  19.1 10.6 %collective-permute-start.3 = (f32[128,512]{1,0:T(8,128)}, f32[128,512]{1,0:T(8,128)S(1)}, u32[]{:S(2)}, u32[]{:S(2)}) collective-permute-start(f32[128,512]{1,0:T(8,128)} %get-tuple-element.26), channel_id=1, source_target_pairs={{0,8},{1,24},{2,40},{3,56},{4,72},{5,88},{6,104},{7,120},{8,9},{9,... | collective-permute-start | bytes 786440 | tf_op jit(solution)/shard_map/ppermute | solution.py:289
  20.6 13.0 %collective-permute-start.4 = (f32[128,512]{1,0:T(8,128)}, f32[128,512]{1,0:T(8,128)S(1)}, u32[]{:S(2)}, u32[]{:S(2)}) collective-permute-start(f32[128,512]{1,0:T(8,128)} %get-tuple-element.27), channel_id=1, source_target_pairs={{0,12},{1,28},{2,44},{3,60},{4,76},{5,92},{6,108},{7,124},{8,13},{... | collective-permute-start | bytes 786440 | tf_op jit(solution)/shard_map/ppermute | solution.py:289
  33.7 4.3 %collective-permute-start.5 = (f32[128,256]{1,0:T(8,128)S(1)}, f32[128,256]{1,0:T(8,128)S(1)}, u32[]{:S(2)}, u32[]{:S(2)}) collective-permute-start(f32[128,256]{1,0:T(8,128)S(1)} %get-tuple-element.28), channel_id=1, source_target_pairs={{0,64},{2,66},{4,68},{6,70},{8,72},{10,74},{12,76},{14,78},{16,80}... | collective-permute-start | bytes 393224 | tf_op jit(solution)/shard_map/ppermute | solution.py:289
  38.0 9.7 %collective-permute-start.6 = (f32[128,256]{1,0:T(8,128)S(1)}, f32[128,256]{1,0:T(8,128)S(1)}, u32[]{:S(2)}, u32[]{:S(2)}) collective-permute-start(f32[128,256]{1,0:T(8,128)S(1)} %broadcast_select_fusion.2), channel_id=1, source_target_pairs={{0,96},{2,98},{4,100},{6,102},{8,104},{10,106},{12,108},{14,110},{... | collective-permute-start | bytes 393224 | tf_op jit(solution)/shard_map/ppermute | solution.py:289
  39.3 16.5 %collective-permute-start.11 = (f32[128,1024]{1,0:T(8,128)}, f32[128,1024]{1,0:T(8,128)S(1)}, u32[]{:S(2)}, u32[]{:S(2)}) collective-permute-start(f32[128,1024]{1,0:T(8,128)} %get-tuple-element.30), channel_id=1, source_target_pairs={{0,64},{1,65},{2,66},{3,67},{4,68},{5,69},{6,70},{7,71},{8,72},{9,... | collective-permute-start | bytes 1572872 | tf_op jit(solution)/shard_map/ppermute | solution.py:289
  45.0 5.5 %collective-permute-start.10 = (f32[128,256]{1,0:T(8,128)S(1)}, f32[128,256]{1,0:T(8,128)S(1)}, u32[]{:S(2)}, u32[]{:S(2)}) collective-permute-start(f32[128,256]{1,0:T(8,128)S(1)} %get-tuple-element.29), channel_id=1, source_target_pairs={{0,2},{1,3},{2,0},{3,1},{4,6},{5,7},{6,4},{7,5},{8,10},{9,11},{10,... | collective-permute-start | bytes 393224 | tf_op jit(solution)/shard_map/ppermute | solution.py:289
  46.3 4.2 %collective-permute-start.9 = (f32[128,256]{1,0:T(8,128)S(1)}, f32[128,256]{1,0:T(8,128)S(1)}, u32[]{:S(2)}, u32[]{:S(2)}) collective-permute-start(f32[128,256]{1,0:T(8,128)S(1)} %get-tuple-element.29), channel_id=1, source_target_pairs={{0,3},{1,0},{2,1},{3,2},{4,7},{5,4},{6,5},{7,6},{8,11},{9,8},{10,9... | collective-permute-start | bytes 393224 | tf_op jit(solution)/shard_map/ppermute | solution.py:289
  46.3 5.8 %collective-permute-start.8 = (f32[128,256]{1,0:T(8,128)S(1)}, f32[128,256]{1,0:T(8,128)S(1)}, u32[]{:S(2)}, u32[]{:S(2)}) collective-permute-start(f32[128,256]{1,0:T(8,128)S(1)} %get-tuple-element.29), channel_id=1, source_target_pairs={{0,1},{1,2},{2,3},{3,0},{4,5},{5,6},{6,7},{7,4},{8,9},{9,10},{10,1... | collective-permute-start | bytes 393224 | tf_op jit(solution)/shard_map/ppermute | solution.py:289
  47.8 4.4 %collective-permute-start.7 = (f32[128,256]{1,0:T(8,128)S(1)}, f32[128,256]{1,0:T(8,128)S(1)}, u32[]{:S(2)}, u32[]{:S(2)}) collective-permute-start(f32[128,256]{1,0:T(8,128)S(1)} %broadcast_select_fusion.3), channel_id=1, source_target_pairs={{0,1},{2,3},{4,5},{6,7},{8,9},{10,11},{12,13},{14,15},{16,17},{18,... | collective-permute-start | bytes 393224 | tf_op jit(solution)/shard_map/ppermute | solution.py:289
  57.0 13.3 %collective-permute-start.13 = (f32[128,1024]{1,0:T(8,128)S(1)}, f32[128,1024]{1,0:T(8,128)S(1)}, u32[]{:S(2)}, u32[]{:S(2)}) collective-permute-start(f32[128,1024]{1,0:T(8,128)S(1)} %broadcast_select_fusion.1), channel_id=1, source_target_pairs={{0,32},{1,33},{2,34},{3,35},{4,36},{5,37},{6,38},{7,39},{8,40},{9,... | collective-permute-start | bytes 1572872 | tf_op jit(solution)/shard_map/ppermute | solution.py:289
  58.3 3.1 %collective-permute-start.12 = (f32[128,256]{1,0:T(8,128)S(1)}, f32[128,256]{1,0:T(8,128)S(1)}, u32[]{:S(2)}, u32[]{:S(2)}) collective-permute-start(f32[128,256]{1,0:T(8,128)S(1)} %broadcast_select_fusion.4.mine_ref), channel_id=1, source_target_pairs={{0,16},{1,17},{2,18},{3,19},{4,20},{5,21},{6,22},{7,23},{8,24},{9,... | collective-permute-start | bytes 393224 | tf_op jit(solution)/shard_map/ppermute | solution.py:289
  59.9 16.2 %collective-permute-start.16 = (f32[4,128,256]{2,1,0:T(8,128)S(1)}, f32[4,128,256]{2,1,0:T(8,128)S(1)}, u32[]{:S(2)}, u32[]{:S(2)}) collective-permute-start(f32[4,128,256]{2,1,0:T(8,128)S(1)} %pad_maximum_fusion.row0_ref), channel_id=1, source_target_pairs={{0,8},{1,9},{2,10},{3,11},{4,12},{5,13},{6,14},{7,15},{8,0},{9,1},... | collective-permute-start | bytes 1572872 | tf_op jit(solution)/shard_map/ppermute | solution.py:289
  59.9 16.2 %collective-permute-start.15 = (f32[4,128,256]{2,1,0:T(8,128)S(1)}, f32[4,128,256]{2,1,0:T(8,128)S(1)}, u32[]{:S(2)}, u32[]{:S(2)}) collective-permute-start(f32[4,128,256]{2,1,0:T(8,128)S(1)} %pad_maximum_fusion.row0_ref), channel_id=1, source_target_pairs={{0,12},{1,13},{2,14},{3,15},{4,0},{5,1},{6,2},{7,3},{8,4},{9,5},{1... | collective-permute-start | bytes 1572872 | tf_op jit(solution)/shard_map/ppermute | solution.py:289
  61.1 15.1 %collective-permute-start.14 = (f32[4,128,256]{2,1,0:T(8,128)S(1)}, f32[4,128,256]{2,1,0:T(8,128)S(1)}, u32[]{:S(2)}, u32[]{:S(2)}) collective-permute-start(f32[4,128,256]{2,1,0:T(8,128)S(1)} %pad_maximum_fusion.row0_ref), channel_id=1, source_target_pairs={{0,4},{1,5},{2,6},{3,7},{4,8},{5,9},{6,10},{7,11},{8,12},{9,13},{1... | collective-permute-start | bytes 1572872 | tf_op jit(solution)/shard_map/ppermute | solution.py:289
  70.4 5.8 %collective-permute-start.17 = (f32[128,1024]{1,0:T(8,128)S(1)}, f32[128,1024]{1,0:T(8,128)S(1)}, u32[]{:S(2)}, u32[]{:S(2)}) collective-permute-start(f32[128,1024]{1,0:T(8,128)S(1)} %broadcast_select_fusion.tall_ref), channel_id=1, source_target_pairs={{0,16},{1,17},{2,18},{3,19},{4,20},{5,21},{6,22},{7,23},{8,24},{9,... | collective-permute-start | bytes 1572872 | tf_op jit(solution)/shard_map/ppermute | solution.py:289

commit v4 on v3

--- a/solution.py
+++ b/solution.py
@@ -115,15 +115,13 @@
     )(stored)
 
 
-def open_kernel(stored_ref, strip_ref, keep_ref, give_ref, sem):
+def open_kernel(stored_ref, strip_ref, corner_ref, keep_ref, give_ref, sem):
     copy = pltpu.make_async_copy(stored_ref.at[pl.ds(0, BLOCK)], strip_ref, sem)
     copy.start()
     first = lax.axis_index("row") % 2 == 0
-    last = keep_ref.shape[0] - 1
     copy.wait()
-    keep_ref[last] = strip_ref[:, :BLOCK]
-    give_ref[last] = strip_ref[:, :BLOCK]
-    for b in range(last):
+    corner_ref[...] = strip_ref[:, :BLOCK]
+    for b in range(keep_ref.shape[0]):
         even = strip_ref[:, 2 * b * BLOCK : (2 * b + 1) * BLOCK]
         odd = strip_ref[:, (2 * b + 1) * BLOCK : (2 * b + 2) * BLOCK]
         keep_ref[b] = jnp.where(first, even, odd).T
@@ -132,30 +130,34 @@
 
 def open_strip(stored):
     cols = stored.shape[1]
-    part = jax.ShapeDtypeStruct((cols // WIDE + 1, BLOCK, BLOCK), F32)
+    one = jax.ShapeDtypeStruct((BLOCK, BLOCK), F32)
+    part = jax.ShapeDtypeStruct((cols // WIDE, BLOCK, BLOCK), F32)
     return pl.pallas_call(
         open_kernel,
         in_specs=[pl.BlockSpec(memory_space=pl.ANY)],
-        out_shape=(jax.ShapeDtypeStruct((BLOCK, cols), F32), part, part),
+        out_shape=(jax.ShapeDtypeStruct((BLOCK, cols), F32), one, part, part),
         scratch_shapes=[pltpu.SemaphoreType.DMA(())],
         name="open",
     )(stored)
 
 
-def pack_kernel(keep_ref, other_ref, *out_refs):
+def pack_kernel(keep_ref, other_ref, corner_ref, beside_ref, *out_refs):
     first = lax.axis_index("row") % 2 == 0
-    last = keep_ref.shape[0] - 1
+    upper = jnp.where(first, corner_ref[...], beside_ref[...])
+    lower = jnp.where(first, beside_ref[...], corner_ref[...])
     for b, out_ref in enumerate(out_refs):
-        for n, t in enumerate((b, last)):
-            out_ref[:, 2 * n * BLOCK : (2 * n + 1) * BLOCK] = jnp.where(first, keep_ref[t], other_ref[t])
-            out_ref[:, (2 * n + 1) * BLOCK : (2 * n + 2) * BLOCK] = jnp.where(first, other_ref[t], keep_ref[t])
-
-
-def pack(keep, other):
-    count = keep.shape[0] - 1
+        out_ref[:, :BLOCK] = jnp.where(first, keep_ref[b], other_ref[b])
+        out_ref[:, BLOCK:WIDE] = jnp.where(first, other_ref[b], keep_ref[b])
+        out_ref[:, WIDE : WIDE + BLOCK] = upper
+        out_ref[:, WIDE + BLOCK :] = lower
+
+
+def pack(keep, other, corner, beside):
     return pl.pallas_call(
-        pack_kernel, out_shape=(jax.ShapeDtypeStruct((BLOCK, 2 * WIDE), F32),) * count, name="pack"
-    )(keep, other)
+        pack_kernel,
+        out_shape=(jax.ShapeDtypeStruct((BLOCK, 2 * WIDE), F32),) * keep.shape[0],
+        name="pack",
+    )(keep, other, corner, beside)
 
 
 def split(x):
@@ -301,10 +303,13 @@
 
     every_row, every_col = range(n_row), range(n_col)
 
-    strip, keep, give = open_strip(stored)
+    strip, corner, keep, give = open_strip(stored)
     other = send(give, [(at(r, c), at(1 - r, c)) for r in (0, 1) for c in every_col])
+    got = send(corner, [(at(r, c), at(r, c + 4)) for r in (0, 1) for c in (0, 1)])
+    corner = jnp.where(my_col < 4, corner, got)
+    got = send(corner, [(at(r, c), at(1 - r, c)) for r in (0, 1) for c in (0, 1, 4, 5)])
     tall = send(strip, [(at(r, c), at(r + 4, c)) for r in (0, 1) for c in every_col])
-    messages = pack(keep, other)
+    messages = pack(keep, other, corner, got)
 
     parts = [
         send(
@@ -318,19 +323,18 @@
     block, corner = lax.optimization_barrier((block, corner))
 
     near_y = [4 * x + y for x in range(4) for y in (0, 2)]
-    got = send(corner, [(at(r, c), at(r + 4, c)) for r in (0, 1) for c in near_y])
+    got = send(corner, [(at(r, c), at((r + 6) % n_row, c)) for r in (0, 1, 4, 5) for c in near_y])
     line = [block] + [send(block, near(1, d)) for d in SHIFTS[1:]]
-    corner = jnp.where(depth == 0, corner, got)
-    got = send(corner, [(at(r, c), at((r + 6) % n_row, c)) for r in (0, 1, 4, 5) for c in near_y])
     corner = jnp.where(depth % 2 == 0, corner, got)
+    corner, tall = lax.optimization_barrier((corner, tall))
+    tall = jnp.where(depth == 0, strip, tall)
+    got_tall = send(tall, [(at(r, c), at(r + 2, c)) for r in (0, 1, 4, 5) for c in every_col])
     got = send(corner, [(at(r, c), at(r, c + 1)) for r in every_row for c in near_y])
     corner = jnp.where(my_col % 2 == 0, corner, got)
     line = jnp.stack(line)
-    corner, line, tall = lax.optimization_barrier((corner, line, tall))
+    corner, line = lax.optimization_barrier((corner, line))
 
     row_parts = [line] + [send(line, near(2, d)) for d in SHIFTS[1:]]
-    tall = jnp.where(depth == 0, strip, tall)
-    got_tall = send(tall, [(at(r, c), at(r + 2, c)) for r in (0, 1, 4, 5) for c in every_col])
     swap = [(at(r, c), at(r + 1 - 2 * (r % 2), c)) for r in every_row for c in every_col]
     other = send(corner, swap)
     lower, inverse = head(corner, other)

time: 85.8 us -> 80.1 us (0.934)
  waiting for transfers between devices: 21.4 us -> 14 us
    ppermute x18 -> x19, waiting for transfers between devices: 21.4 us -> 14 us  [send(): return lax.ppermute(x, AXES, pairs)]
    ppermute x18 -> x19, starting transfers between devices: 35.4 us -> 36.1 us  [send(): return lax.ppermute(x, AXES, pairs)]
  transfers between devices with their start and end apart: 18 -> 19, of which waited for: 8 -> 7; matrix products, arithmetic and copies ran while one was open for 0% -> 3% of each run, Pallas kernels for 14% -> 15%
where the time goes in v4:
time: 80.1 us; the launch traced here: 79.5 us
  starting transfers between devices  36.1 us (45%)
  Pallas kernels  25.4 us (32%)
  waiting for transfers between devices  14 us (17%)
  other arithmetic  2.17 us (3%)
  between operations  1.07 us (1%)
    ppermute x19, starting transfers between devices, send(): return lax.ppermute(x, AXES, pairs)  36.1 us
    ppermute x19, waiting for transfers between devices, send(): return lax.ppermute(x, AXES, pairs)  14 us
    pallas_call x1, Pallas kernels, update(): pl.pallas_call(update_kernel, in_specs=[here] * 2 + [there] * 6 + [here],...  8.98 us
    pallas_call x1, Pallas kernels, head(): pl.pallas_call(head_kernel, out_shape=(jax.ShapeDtypeStruct((2, BLOCK, WI...  8.89 us
    pallas_call x1, Pallas kernels, hold(): pl.pallas_call(hold_kernel, in_specs=[pl.BlockSpec(memory_space=pltpu.HBM...  3.39 us
    pallas_call x1, Pallas kernels, pack(): pl.pallas_call(pack_kernel, out_shape=(jax.ShapeDtypeStruct((BLOCK, 2 * W...  2.12 us
    pallas_call x1, Pallas kernels, open_strip(): pl.pallas_call(open_kernel, in_specs=[pl.BlockSpec(memory_space=pl.ANY)],...  2.04 us
  transfers between devices with their start and end apart: 19, of which 7 were waited for; matrix products, arithmetic and copies ran while one was open for 3% of the time, Pallas kernels for 15%

profile of v4, /device:TPU:1, one launch (start us, length us, event | category | flops | bytes accessed | tf_op | source)
XLA Modules:
  0.0 79.5 jit_solution(2512854359874095356)
XLA Ops:
  0.6 2.0 %open.1 = (f32[128,1024]{1,0:T(8,128)}, f32[128,128]{1,0:T(8,128)}, f32[4,128,128]{2,1,0:T(8,128)}, f32[4,128,128]{2,1,0:T(8,128)}) custom-call(f32[2048,1024]{1,0:T(8,128)} %stored_ref.1), custom_call_target="tpu_custom_call" | custom-call | tf_op jit(solution)/shard_map/open/pallas_call | solution.py:135
  2.7 3.9 %collective-permute-start.1 = (f32[128,128]{1,0:T(8,128)}, f32[128,128]{1,0:T(8,128)S(1)}, u32[]{:S(2)}, u32[]{:S(2)}) collective-permute-start(f32[128,128]{1,0:T(8,128)} %get-tuple-element.26), channel_id=1, source_target_pairs={{0,4},{1,5},{16,20},{17,21}} | collective-permute-start | bytes 196616 | tf_op jit(solution)/shard_map/ppermute | solution.py:291
  6.6 2.9 %collective-permute-start = (f32[4,128,128]{2,1,0:T(8,128)}, f32[4,128,128]{2,1,0:T(8,128)S(1)}, u32[]{:S(2)}, u32[]{:S(2)}) collective-permute-start(f32[4,128,128]{2,1,0:T(8,128)} %get-tuple-element.25), channel_id=1, source_target_pairs={{0,16},{1,17},{2,18},{3,19},{4,20},{5,21},{6,22},{7,23},{8,24},{9,... | collective-permute-start | bytes 786440 | tf_op jit(solution)/shard_map/ppermute | solution.py:291
  9.5 0.9 %broadcast_select_fusion.4.corner_ref = f32[128,128]{1,0:T(8,128)S(1)} fusion(f32[128,128]{1,0:T(8,128)} %get-tuple-element.26, f32[128,128]{1,0:T(8,128)S(1)} %collective-permute-done.1, pred[]{:T(512)S(6)} %lt.17), kind=kLoop, calls=%fused_computation.6 | loop fusion | flops 16384 | bytes 196609 | tf_op jit(solution)/shard_map/jit(_where)/select_n | solution.py:309
  10.4 2.2 %collective-permute-start.2 = (f32[128,128]{1,0:T(8,128)S(1)}, f32[128,128]{1,0:T(8,128)S(1)}, u32[]{:S(2)}, u32[]{:S(2)}) collective-permute-start(f32[128,128]{1,0:T(8,128)S(1)} %broadcast_select_fusion.4.corner_ref), channel_id=1, source_target_pairs={{0,16},{1,17},{4,20},{5,21},{16,0},{17,1},{20,4},{21,5}} | collective-permute-start | bytes 196616 | tf_op jit(solution)/shard_map/ppermute | solution.py:291
  12.6 1.0 %collective-permute-done.2.beside_ref = f32[128,128]{1,0:T(8,128)S(1)} collective-permute-done((f32[128,128]{1,0:T(8,128)S(1)}, f32[128,128]{1,0:T(8,128)S(1)}, u32[]{:S(2)}, u32[]{:S(2)}) %collective-permute-start.2) | collective-permute-done | bytes 65568 | tf_op jit(solution)/shard_map/ppermute | solution.py:291
  13.5 0.6 copy-done.2
  14.3 2.1 %pack.1 = (f32[128,512]{1,0:T(8,128)}, f32[128,512]{1,0:T(8,128)}, f32[128,512]{1,0:T(8,128)}, f32[128,512]{1,0:T(8,128)}) custom-call(f32[4,128,128]{2,1,0:T(8,128)} %get-tuple-element.24.keep_ref, f32[4,128,128]{2,1,0:T(8,128)} %copy-done.1, f32[128,128]{1,0:T(8,128)} %copy-done, f32[128,128]{1,0:T(8,128)} %copy-done.2), custom_call_target="tpu_custom_call" | custom-call | tf_op jit(solution)/shard_map/pack/pallas_call | solution.py:156
  16.4 1.9 %collective-permute-start.3 = (f32[128,512]{1,0:T(8,128)}, f32[128,512]{1,0:T(8,128)S(1)}, u32[]{:S(2)}, u32[]{:S(2)}) collective-permute-start(f32[128,512]{1,0:T(8,128)} %get-tuple-element.27), channel_id=1, source_target_pairs={{0,0},{1,16},{2,32},{3,48},{4,64},{5,80},{6,96},{7,112},{8,1},{9,1... | collective-permute-start | bytes 786440 | tf_op jit(solution)/shard_map/ppermute | solution.py:291
  18.3 3.0 %collective-permute-start.4 = (f32[128,512]{1,0:T(8,128)}, f32[128,512]{1,0:T(8,128)S(1)}, u32[]{:S(2)}, u32[]{:S(2)}) collective-permute-start(f32[128,512]{1,0:T(8,128)} %get-tuple-element.28), channel_id=1, source_target_pairs={{0,4},{1,20},{2,36},{3,52},{4,68},{5,84},{6,100},{7,116},{8,5},{9,... | collective-permute-start | bytes 786440 | tf_op jit(solution)/shard_map/ppermute | solution.py:291
  21.3 1.3 %collective-permute-start.5 = (f32[128,512]{1,0:T(8,128)}, f32[128,512]{1,0:T(8,128)S(1)}, u32[]{:S(2)}, u32[]{:S(2)}) collective-permute-start(f32[128,512]{1,0:T(8,128)} %get-tuple-element.29), channel_id=1, source_target_pairs={{0,8},{1,24},{2,40},{3,56},{4,72},{5,88},{6,104},{7,120},{8,9},{9,... | collective-permute-start | bytes 786440 | tf_op jit(solution)/shard_map/ppermute | solution.py:291
  22.6 2.6 %collective-permute-start.6 = (f32[128,512]{1,0:T(8,128)}, f32[128,512]{1,0:T(8,128)S(1)}, u32[]{:S(2)}, u32[]{:S(2)}) collective-permute-start(f32[128,512]{1,0:T(8,128)} %get-tuple-element.30), channel_id=1, source_target_pairs={{0,12},{1,28},{2,44},{3,60},{4,76},{5,92},{6,108},{7,124},{8,13},{... | collective-permute-start | bytes 786440 | tf_op jit(solution)/shard_map/ppermute | solution.py:291
  25.2 1.3 %collective-permute-start.8 = (f32[128,1024]{1,0:T(8,128)}, f32[128,1024]{1,0:T(8,128)S(1)}, u32[]{:S(2)}, u32[]{:S(2)}) collective-permute-start(f32[128,1024]{1,0:T(8,128)} %get-tuple-element.32), channel_id=1, source_target_pairs={{0,64},{1,65},{2,66},{3,67},{4,68},{5,69},{6,70},{7,71},{8,72},{9,... | collective-permute-start | bytes 1572872 | tf_op jit(solution)/shard_map/ppermute | solution.py:291
  26.6 4.8 %collective-permute-done.3 = f32[128,512]{1,0:T(8,128)S(1)} collective-permute-done((f32[128,512]{1,0:T(8,128)}, f32[128,512]{1,0:T(8,128)S(1)}, u32[]{:S(2)}, u32[]{:S(2)}) %collective-permute-start.3) | collective-permute-done | bytes 262176 | tf_op jit(solution)/shard_map/ppermute | solution.py:291
  31.4 1.9 %collective-permute-done.5 = f32[128,512]{1,0:T(8,128)S(1)} collective-permute-done((f32[128,512]{1,0:T(8,128)}, f32[128,512]{1,0:T(8,128)S(1)}, u32[]{:S(2)}, u32[]{:S(2)}) %collective-permute-start.5) | collective-permute-done | bytes 262176 | tf_op jit(solution)/shard_map/ppermute | solution.py:291
  33.4 3.1 %collective-permute-done.6 = f32[128,512]{1,0:T(8,128)S(1)} collective-permute-done((f32[128,512]{1,0:T(8,128)}, f32[128,512]{1,0:T(8,128)S(1)}, u32[]{:S(2)}, u32[]{:S(2)}) %collective-permute-start.6) | collective-permute-done | bytes 262176 | tf_op jit(solution)/shard_map/ppermute | solution.py:291
  36.5 1.3 %collective-permute-start.7 = (f32[128,256]{1,0:T(8,128)S(1)}, f32[128,256]{1,0:T(8,128)S(1)}, u32[]{:S(2)}, u32[]{:S(2)}) collective-permute-start(f32[128,256]{1,0:T(8,128)S(1)} %get-tuple-element.31), channel_id=1, source_target_pairs={{0,96},{2,98},{4,100},{6,102},{8,104},{10,106},{12,108},{14,110},{... | collective-permute-start | bytes 393224 | tf_op jit(solution)/shard_map/ppermute | solution.py:291
  37.9 4.4 %collective-permute-start.12 = (f32[128,256]{1,0:T(8,128)S(1)}, f32[128,256]{1,0:T(8,128)S(1)}, u32[]{:S(2)}, u32[]{:S(2)}) collective-permute-start(f32[128,256]{1,0:T(8,128)S(1)} %get-tuple-element.34), channel_id=1, source_target_pairs={{0,2},{1,3},{2,0},{3,1},{4,6},{5,7},{6,4},{7,5},{8,10},{9,11},{10,... | collective-permute-start | bytes 393224 | tf_op jit(solution)/shard_map/ppermute | solution.py:291
  42.3 0.8 %collective-permute-start.11 = (f32[128,256]{1,0:T(8,128)S(1)}, f32[128,256]{1,0:T(8,128)S(1)}, u32[]{:S(2)}, u32[]{:S(2)}) collective-permute-start(f32[128,256]{1,0:T(8,128)S(1)} %get-tuple-element.34), channel_id=1, source_target_pairs={{0,3},{1,0},{2,1},{3,2},{4,7},{5,4},{6,5},{7,6},{8,11},{9,8},{10,9... | collective-permute-start | bytes 393224 | tf_op jit(solution)/shard_map/ppermute | solution.py:291
  43.1 0.7 collective-permute-start.10
  43.8 1.1 %broadcast_select_fusion.1 = f32[128,1024]{1,0:T(8,128)S(1)} fusion(f32[128,1024]{1,0:T(8,128)} %get-tuple-element.32, f32[128,1024]{1,0:T(8,128)S(1)} %collective-permute-done.8, pred[]{:T(512)S(6)} %eq.16), kind=kLoop, calls=%fused_computation.3 | loop fusion | flops 131072 | bytes 1572865 | tf_op jit(solution)/shard_map/jit(_where)/select_n | solution.py:330
  44.9 1.3 %collective-permute-start.14 = (f32[128,1024]{1,0:T(8,128)S(1)}, f32[128,1024]{1,0:T(8,128)S(1)}, u32[]{:S(2)}, u32[]{:S(2)}) collective-permute-start(f32[128,1024]{1,0:T(8,128)S(1)} %broadcast_select_fusion.1), channel_id=1, source_target_pairs={{0,32},{1,33},{2,34},{3,35},{4,36},{5,37},{6,38},{7,39},{8,40},{9,... | collective-permute-start | bytes 1572872 | tf_op jit(solution)/shard_map/ppermute | solution.py:291
  46.2 1.3 %collective-permute-start.9 = (f32[128,256]{1,0:T(8,128)S(1)}, f32[128,256]{1,0:T(8,128)S(1)}, u32[]{:S(2)}, u32[]{:S(2)}) collective-permute-start(f32[128,256]{1,0:T(8,128)S(1)} %broadcast_select_fusion.2), channel_id=1, source_target_pairs={{0,1},{2,3},{4,5},{6,7},{8,9},{10,11},{12,13},{14,15},{16,17},{18,... | collective-permute-start | bytes 393224 | tf_op jit(solution)/shard_map/ppermute | solution.py:291
  47.7 0.7 collective-permute-done.10
  48.4 2.3 %collective-permute-done.9 = f32[128,256]{1,0:T(8,128)S(1)} collective-permute-done((f32[128,256]{1,0:T(8,128)S(1)}, f32[128,256]{1,0:T(8,128)S(1)}, u32[]{:S(2)}, u32[]{:S(2)}) %collective-permute-start.9) | collective-permute-done | bytes 131104 | tf_op jit(solution)/shard_map/ppermute | solution.py:291
  50.8 0.6 collective-permute-start.13
  51.3 3.0 %collective-permute-start.17 = (f32[4,128,256]{2,1,0:T(8,128)S(1)}, f32[4,128,256]{2,1,0:T(8,128)S(1)}, u32[]{:S(2)}, u32[]{:S(2)}) collective-permute-start(f32[4,128,256]{2,1,0:T(8,128)S(1)} %pad_maximum_fusion.row0_ref), channel_id=1, source_target_pairs={{0,8},{1,9},{2,10},{3,11},{4,12},{5,13},{6,14},{7,15},{8,0},{9,1},... | collective-permute-start | bytes 1572872 | tf_op jit(solution)/shard_map/ppermute | solution.py:291
  54.3 1.6 %collective-permute-start.16 = (f32[4,128,256]{2,1,0:T(8,128)S(1)}, f32[4,128,256]{2,1,0:T(8,128)S(1)}, u32[]{:S(2)}, u32[]{:S(2)}) collective-permute-start(f32[4,128,256]{2,1,0:T(8,128)S(1)} %pad_maximum_fusion.row0_ref), channel_id=1, source_target_pairs={{0,12},{1,13},{2,14},{3,15},{4,0},{5,1},{6,2},{7,3},{8,4},{9,5},{1... | collective-permute-start | bytes 1572872 | tf_op jit(solution)/shard_map/ppermute | solution.py:291
  55.9 8.9 %head.1 = (f32[2,128,256]{2,1,0:T(8,128)S(1)}, f32[256,256]{1,0:T(8,128)S(1)}) custom-call(f32[128,256]{1,0:T(8,128)S(1)} %broadcast_select_fusion.3.mine_ref, f32[128,256]{1,0:T(8,128)S(1)} %collective-permute-done.13.other_ref), custom_call_target="tpu_custom_call" | custom-call | flops 100000000 | bytes 1000000 | tf_op jit(solution)/shard_map/head/pallas_call | solution.py:87
  64.9 2.0 %collective-permute-start.18 = (f32[128,1024]{1,0:T(8,128)S(1)}, f32[128,1024]{1,0:T(8,128)S(1)}, u32[]{:S(2)}, u32[]{:S(2)}) collective-permute-start(f32[128,1024]{1,0:T(8,128)S(1)} %broadcast_select_fusion.tall_ref), channel_id=1, source_target_pairs={{0,16},{1,17},{2,18},{3,19},{4,20},{5,21},{6,22},{7,23},{8,24},{9,... | collective-permute-start | bytes 1572872 | tf_op jit(solution)/shard_map/ppermute | solution.py:291
  66.9 3.4 %hold.1.a_ref = f32[16,128,1024]{2,1,0:T(8,128)S(1)} custom-call(f32[16,128,1024]{2,1,0:T(8,128)} %bitcast.7), custom_call_target="tpu_custom_call" | custom-call | bytes 8388608 | tf_op jit(solution)/shard_map/hold/pallas_call | solution.py:106
  70.3 9.0 %update.1 = (f32[16,128,1024]{2,1,0:T(8,128)}, f32[16,128,256]{2,1,0:T(8,128)}) custom-call(f32[2,128,256]{2,1,0:T(8,128)S(1)} %get-tuple-element.36.lower_ref, f32[256,256]{1,0:T(8,128)S(1)} %get-tuple-element.39.inverse_ref, f32[4,128,256]{2,1,0:T(8,128)S(1)} %pad_maximum_fusion.row0_ref, f32[4,128,256]{2,1,0:T(8,128)S(1)} %collective-permute-done.15.row1_ref, ...), custom_call_target="tpu_custom_call" | custom-call | tf_op jit(solution)/shard_map/update/pallas_call | solution.py:256
  (25 shorter events, 0.5 us)
Async XLA Ops:
  2.7 6.8 %collective-permute-start.1 = (f32[128,128]{1,0:T(8,128)}, f32[128,128]{1,0:T(8,128)S(1)}, u32[]{:S(2)}, u32[]{:S(2)}) collective-permute-start(f32[128,128]{1,0:T(8,128)} %get-tuple-element.26), channel_id=1, source_target_pairs={{0,4},{1,5},{16,20},{17,21}} | collective-permute-start | bytes 196616 | tf_op jit(solution)/shard_map/ppermute | solution.py:291
  6.6 6.9 %collective-permute-start = (f32[4,128,128]{2,1,0:T(8,128)}, f32[4,128,128]{2,1,0:T(8,128)S(1)}, u32[]{:S(2)}, u32[]{:S(2)}) collective-permute-start(f32[4,128,128]{2,1,0:T(8,128)} %get-tuple-element.25), channel_id=1, source_target_pairs={{0,16},{1,17},{2,18},{3,19},{4,20},{5,21},{6,22},{7,23},{8,24},{9,... | collective-permute-start | bytes 786440 | tf_op jit(solution)/shard_map/ppermute | solution.py:291
  10.4 3.2 %copy-start = (f32[128,128]{1,0:T(8,128)}, f32[128,128]{1,0:T(8,128)S(1)}, u32[]{:S(2)}) copy-start(f32[128,128]{1,0:T(8,128)S(1)} %broadcast_select_fusion.4.corner_ref) | copy-start | bytes 196612
  10.4 3.1 %collective-permute-start.2 = (f32[128,128]{1,0:T(8,128)S(1)}, f32[128,128]{1,0:T(8,128)S(1)}, u32[]{:S(2)}, u32[]{:S(2)}) collective-permute-start(f32[128,128]{1,0:T(8,128)S(1)} %broadcast_select_fusion.4.corner_ref), channel_id=1, source_target_pairs={{0,16},{1,17},{4,20},{5,21},{16,0},{17,1},{20,4},{21,5}} | collective-permute-start | bytes 196616 | tf_op jit(solution)/shard_map/ppermute | solution.py:291
  13.5 0.6 copy-start.2
  13.5 0.7 copy-start.1
  16.4 15.0 %collective-permute-start.3 = (f32[128,512]{1,0:T(8,128)}, f32[128,512]{1,0:T(8,128)S(1)}, u32[]{:S(2)}, u32[]{:S(2)}) collective-permute-start(f32[128,512]{1,0:T(8,128)} %get-tuple-element.27), channel_id=1, source_target_pairs={{0,0},{1,16},{2,32},{3,48},{4,64},{5,80},{6,96},{7,112},{8,1},{9,1... | collective-permute-start | bytes 786440 | tf_op jit(solution)/shard_map/ppermute | solution.py:291
  18.3 13.1 %collective-permute-start.4 = (f32[128,512]{1,0:T(8,128)}, f32[128,512]{1,0:T(8,128)S(1)}, u32[]{:S(2)}, u32[]{:S(2)}) collective-permute-start(f32[128,512]{1,0:T(8,128)} %get-tuple-element.28), channel_id=1, source_target_pairs={{0,4},{1,20},{2,36},{3,52},{4,68},{5,84},{6,100},{7,116},{8,5},{9,... | collective-permute-start | bytes 786440 | tf_op jit(solution)/shard_map/ppermute | solution.py:291
  21.3 12.1 %collective-permute-start.5 = (f32[128,512]{1,0:T(8,128)}, f32[128,512]{1,0:T(8,128)S(1)}, u32[]{:S(2)}, u32[]{:S(2)}) collective-permute-start(f32[128,512]{1,0:T(8,128)} %get-tuple-element.29), channel_id=1, source_target_pairs={{0,8},{1,24},{2,40},{3,56},{4,72},{5,88},{6,104},{7,120},{8,9},{9,... | collective-permute-start | bytes 786440 | tf_op jit(solution)/shard_map/ppermute | solution.py:291
  22.6 13.8 %collective-permute-start.6 = (f32[128,512]{1,0:T(8,128)}, f32[128,512]{1,0:T(8,128)S(1)}, u32[]{:S(2)}, u32[]{:S(2)}) collective-permute-start(f32[128,512]{1,0:T(8,128)} %get-tuple-element.30), channel_id=1, source_target_pairs={{0,12},{1,28},{2,44},{3,60},{4,76},{5,92},{6,108},{7,124},{8,13},{... | collective-permute-start | bytes 786440 | tf_op jit(solution)/shard_map/ppermute | solution.py:291
  25.2 18.5 %collective-permute-start.8 = (f32[128,1024]{1,0:T(8,128)}, f32[128,1024]{1,0:T(8,128)S(1)}, u32[]{:S(2)}, u32[]{:S(2)}) collective-permute-start(f32[128,1024]{1,0:T(8,128)} %get-tuple-element.32), channel_id=1, source_target_pairs={{0,64},{1,65},{2,66},{3,67},{4,68},{5,69},{6,70},{7,71},{8,72},{9,... | collective-permute-start | bytes 1572872 | tf_op jit(solution)/shard_map/ppermute | solution.py:291
  36.5 7.2 %collective-permute-start.7 = (f32[128,256]{1,0:T(8,128)S(1)}, f32[128,256]{1,0:T(8,128)S(1)}, u32[]{:S(2)}, u32[]{:S(2)}) collective-permute-start(f32[128,256]{1,0:T(8,128)S(1)} %get-tuple-element.31), channel_id=1, source_target_pairs={{0,96},{2,98},{4,100},{6,102},{8,104},{10,106},{12,108},{14,110},{... | collective-permute-start | bytes 393224 | tf_op jit(solution)/shard_map/ppermute | solution.py:291
  37.9 9.7 %collective-permute-start.12 = (f32[128,256]{1,0:T(8,128)S(1)}, f32[128,256]{1,0:T(8,128)S(1)}, u32[]{:S(2)}, u32[]{:S(2)}) collective-permute-start(f32[128,256]{1,0:T(8,128)S(1)} %get-tuple-element.34), channel_id=1, source_target_pairs={{0,2},{1,3},{2,0},{3,1},{4,6},{5,7},{6,4},{7,5},{8,10},{9,11},{10,... | collective-permute-start | bytes 393224 | tf_op jit(solution)/shard_map/ppermute | solution.py:291
  42.3 5.4 %collective-permute-start.11 = (f32[128,256]{1,0:T(8,128)S(1)}, f32[128,256]{1,0:T(8,128)S(1)}, u32[]{:S(2)}, u32[]{:S(2)}) collective-permute-start(f32[128,256]{1,0:T(8,128)S(1)} %get-tuple-element.34), channel_id=1, source_target_pairs={{0,3},{1,0},{2,1},{3,2},{4,7},{5,4},{6,5},{7,6},{8,11},{9,8},{10,9... | collective-permute-start | bytes 393224 | tf_op jit(solution)/shard_map/ppermute | solution.py:291
  43.1 5.3 %collective-permute-start.10 = (f32[128,256]{1,0:T(8,128)S(1)}, f32[128,256]{1,0:T(8,128)S(1)}, u32[]{:S(2)}, u32[]{:S(2)}) collective-permute-start(f32[128,256]{1,0:T(8,128)S(1)} %get-tuple-element.34), channel_id=1, source_target_pairs={{0,1},{1,2},{2,3},{3,0},{4,5},{5,6},{6,7},{7,4},{8,9},{9,10},{10,1... | collective-permute-start | bytes 393224 | tf_op jit(solution)/shard_map/ppermute | solution.py:291
  44.9 19.9 %collective-permute-start.14 = (f32[128,1024]{1,0:T(8,128)S(1)}, f32[128,1024]{1,0:T(8,128)S(1)}, u32[]{:S(2)}, u32[]{:S(2)}) collective-permute-start(f32[128,1024]{1,0:T(8,128)S(1)} %broadcast_select_fusion.1), channel_id=1, source_target_pairs={{0,32},{1,33},{2,34},{3,35},{4,36},{5,37},{6,38},{7,39},{8,40},{9,... | collective-permute-start | bytes 1572872 | tf_op jit(solution)/shard_map/ppermute | solution.py:291
  46.2 4.5 %collective-permute-start.9 = (f32[128,256]{1,0:T(8,128)S(1)}, f32[128,256]{1,0:T(8,128)S(1)}, u32[]{:S(2)}, u32[]{:S(2)}) collective-permute-start(f32[128,256]{1,0:T(8,128)S(1)} %broadcast_select_fusion.2), channel_id=1, source_target_pairs={{0,1},{2,3},{4,5},{6,7},{8,9},{10,11},{12,13},{14,15},{16,17},{18,... | collective-permute-start | bytes 393224 | tf_op jit(solution)/shard_map/ppermute | solution.py:291
  50.8 5.1 %collective-permute-start.13 = (f32[128,256]{1,0:T(8,128)S(1)}, f32[128,256]{1,0:T(8,128)S(1)}, u32[]{:S(2)}, u32[]{:S(2)}) collective-permute-start(f32[128,256]{1,0:T(8,128)S(1)} %broadcast_select_fusion.3.mine_ref), channel_id=1, source_target_pairs={{0,16},{1,17},{2,18},{3,19},{4,20},{5,21},{6,22},{7,23},{8,24},{9,... | collective-permute-start | bytes 393224 | tf_op jit(solution)/shard_map/ppermute | solution.py:291
  51.3 19.0 %collective-permute-start.17 = (f32[4,128,256]{2,1,0:T(8,128)S(1)}, f32[4,128,256]{2,1,0:T(8,128)S(1)}, u32[]{:S(2)}, u32[]{:S(2)}) collective-permute-start(f32[4,128,256]{2,1,0:T(8,128)S(1)} %pad_maximum_fusion.row0_ref), channel_id=1, source_target_pairs={{0,8},{1,9},{2,10},{3,11},{4,12},{5,13},{6,14},{7,15},{8,0},{9,1},... | collective-permute-start | bytes 1572872 | tf_op jit(solution)/shard_map/ppermute | solution.py:291
  54.3 16.0 %collective-permute-start.16 = (f32[4,128,256]{2,1,0:T(8,128)S(1)}, f32[4,128,256]{2,1,0:T(8,128)S(1)}, u32[]{:S(2)}, u32[]{:S(2)}) collective-permute-start(f32[4,128,256]{2,1,0:T(8,128)S(1)} %pad_maximum_fusion.row0_ref), channel_id=1, source_target_pairs={{0,12},{1,13},{2,14},{3,15},{4,0},{5,1},{6,2},{7,3},{8,4},{9,5},{1... | collective-permute-start | bytes 1572872 | tf_op jit(solution)/shard_map/ppermute | solution.py:291
  55.9 14.4 %collective-permute-start.15 = (f32[4,128,256]{2,1,0:T(8,128)S(1)}, f32[4,128,256]{2,1,0:T(8,128)S(1)}, u32[]{:S(2)}, u32[]{:S(2)}) collective-permute-start(f32[4,128,256]{2,1,0:T(8,128)S(1)} %pad_maximum_fusion.row0_ref), channel_id=1, source_target_pairs={{0,4},{1,5},{2,6},{3,7},{4,8},{5,9},{6,10},{7,11},{8,12},{9,13},{1... | collective-permute-start | bytes 1572872 | tf_op jit(solution)/shard_map/ppermute | solution.py:291
  64.9 5.5 %collective-permute-start.18 = (f32[128,1024]{1,0:T(8,128)S(1)}, f32[128,1024]{1,0:T(8,128)S(1)}, u32[]{:S(2)}, u32[]{:S(2)}) collective-permute-start(f32[128,1024]{1,0:T(8,128)S(1)} %broadcast_select_fusion.tall_ref), channel_id=1, source_target_pairs={{0,16},{1,17},{2,18},{3,19},{4,20},{5,21},{6,22},{7,23},{8,24},{9,... | collective-permute-start | bytes 1572872 | tf_op jit(solution)/shard_map/ppermute | solution.py:291

commit v5 on v4

--- a/solution.py
+++ b/solution.py
@@ -308,7 +308,7 @@
     got = send(corner, [(at(r, c), at(r, c + 4)) for r in (0, 1) for c in (0, 1)])
     corner = jnp.where(my_col < 4, corner, got)
     got = send(corner, [(at(r, c), at(1 - r, c)) for r in (0, 1) for c in (0, 1, 4, 5)])
-    tall = send(strip, [(at(r, c), at(r + 4, c)) for r in (0, 1) for c in every_col])
+    tall = send(strip, [(at(r, c), at(r + 6, c)) for r in (0, 1) for c in every_col])
     messages = pack(keep, other, corner, got)
 
     parts = [
@@ -323,12 +323,12 @@
     block, corner = lax.optimization_barrier((block, corner))
 
     near_y = [4 * x + y for x in range(4) for y in (0, 2)]
-    got = send(corner, [(at(r, c), at((r + 6) % n_row, c)) for r in (0, 1, 4, 5) for c in near_y])
+    got = send(corner, [(at(r, c), at(r + 2, c)) for r in (0, 1, 4, 5) for c in near_y])
     line = [block] + [send(block, near(1, d)) for d in SHIFTS[1:]]
     corner = jnp.where(depth % 2 == 0, corner, got)
     corner, tall = lax.optimization_barrier((corner, tall))
     tall = jnp.where(depth == 0, strip, tall)
-    got_tall = send(tall, [(at(r, c), at(r + 2, c)) for r in (0, 1, 4, 5) for c in every_col])
+    got_tall = send(tall, [(at(r, c), at(t, c)) for r, t in ((0, 2), (1, 3), (6, 4), (7, 5)) for c in every_col])
     got = send(corner, [(at(r, c), at(r, c + 1)) for r in every_row for c in near_y])
     corner = jnp.where(my_col % 2 == 0, corner, got)
     line = jnp.stack(line)
@@ -340,7 +340,7 @@
     lower, inverse = head(corner, other)
     inverse, got_tall, tall, stored = lax.optimization_barrier((inverse, got_tall, tall, stored))
 
-    tall = jnp.where(depth % 2 == 0, tall, got_tall)
+    tall = jnp.where(depth % 3 == 0, tall, got_tall)
     beside = send(tall, swap)
     held = hold(stored.reshape(-1, BLOCK, stored.shape[1]))
     return update(lower, inverse, row_parts, [tall, beside], held)

time: 80.1 us -> 78.4 us (0.979)
  starting transfers between devices: 36.1 us -> 34.4 us
    ppermute x19, starting transfers between devices: 36.1 us -> 34.4 us  [send(): return lax.ppermute(x, AXES, pairs)]
  transfers between devices with their start and end apart: 19 -> 19, of which waited for: 7 -> 7; matrix products, arithmetic and copies ran while one was open for 3% -> 3% of each run, Pallas kernels for 15% -> 16%
where the time goes in v5:
time: 78.4 us; the launch traced here: 77.7 us
  starting transfers between devices  34.4 us (44%)
  Pallas kernels  25.4 us (32%)
  waiting for transfers between devices  13.9 us (18%)
  other arithmetic  2.17 us (3%)
  between operations  1.07 us (1%)
    ppermute x19, starting transfers between devices, send(): return lax.ppermute(x, AXES, pairs)  34.4 us
    ppermute x19, waiting for transfers between devices, send(): return lax.ppermute(x, AXES, pairs)  13.9 us
    pallas_call x1, Pallas kernels, update(): pl.pallas_call(update_kernel, in_specs=[here] * 2 + [there] * 6 + [here],...  8.98 us
    pallas_call x1, Pallas kernels, head(): pl.pallas_call(head_kernel, out_shape=(jax.ShapeDtypeStruct((2, BLOCK, WI...  8.89 us
    pallas_call x1, Pallas kernels, hold(): pl.pallas_call(hold_kernel, in_specs=[pl.BlockSpec(memory_space=pltpu.HBM...  3.39 us
    pallas_call x1, Pallas kernels, pack(): pl.pallas_call(pack_kernel, out_shape=(jax.ShapeDtypeStruct((BLOCK, 2 * W...  2.12 us
    pallas_call x1, Pallas kernels, open_strip(): pl.pallas_call(open_kernel, in_specs=[pl.BlockSpec(memory_space=pl.ANY)],...  2.04 us
  transfers between devices with their start and end apart: 19, of which 7 were waited for; matrix products, arithmetic and copies ran while one was open for 3% of the time, Pallas kernels for 16%

profile of v5, /device:TPU:1, one launch (start us, length us, event | category | flops | bytes accessed | tf_op | source)
XLA Modules:
  0.0 77.7 jit_solution(11762976882872775563)
XLA Ops:
  0.6 2.0 %open.1 = (f32[128,1024]{1,0:T(8,128)}, f32[128,128]{1,0:T(8,128)}, f32[4,128,128]{2,1,0:T(8,128)}, f32[4,128,128]{2,1,0:T(8,128)}) custom-call(f32[2048,1024]{1,0:T(8,128)} %stored_ref.1), custom_call_target="tpu_custom_call" | custom-call | tf_op jit(solution)/shard_map/open/pallas_call | solution.py:135
  2.7 3.9 %collective-permute-start.1 = (f32[128,128]{1,0:T(8,128)}, f32[128,128]{1,0:T(8,128)S(1)}, u32[]{:S(2)}, u32[]{:S(2)}) collective-permute-start(f32[128,128]{1,0:T(8,128)} %get-tuple-element.26), channel_id=1, source_target_pairs={{0,4},{1,5},{16,20},{17,21}} | collective-permute-start | bytes 196616 | tf_op jit(solution)/shard_map/ppermute | solution.py:291
  6.6 2.9 %collective-permute-start = (f32[4,128,128]{2,1,0:T(8,128)}, f32[4,128,128]{2,1,0:T(8,128)S(1)}, u32[]{:S(2)}, u32[]{:S(2)}) collective-permute-start(f32[4,128,128]{2,1,0:T(8,128)} %get-tuple-element.25), channel_id=1, source_target_pairs={{0,16},{1,17},{2,18},{3,19},{4,20},{5,21},{6,22},{7,23},{8,24},{9,... | collective-permute-start | bytes 786440 | tf_op jit(solution)/shard_map/ppermute | solution.py:291
  9.5 0.9 %broadcast_select_fusion.4.corner_ref = f32[128,128]{1,0:T(8,128)S(1)} fusion(f32[128,128]{1,0:T(8,128)} %get-tuple-element.26, f32[128,128]{1,0:T(8,128)S(1)} %collective-permute-done.1, pred[]{:T(512)S(6)} %lt.19), kind=kLoop, calls=%fused_computation.6 | loop fusion | flops 16384 | bytes 196609 | tf_op jit(solution)/shard_map/jit(_where)/select_n | solution.py:309
  10.4 2.2 %collective-permute-start.2 = (f32[128,128]{1,0:T(8,128)S(1)}, f32[128,128]{1,0:T(8,128)S(1)}, u32[]{:S(2)}, u32[]{:S(2)}) collective-permute-start(f32[128,128]{1,0:T(8,128)S(1)} %broadcast_select_fusion.4.corner_ref), channel_id=1, source_target_pairs={{0,16},{1,17},{4,20},{5,21},{16,0},{17,1},{20,4},{21,5}} | collective-permute-start | bytes 196616 | tf_op jit(solution)/shard_map/ppermute | solution.py:291
  12.6 1.0 %collective-permute-done.2.beside_ref = f32[128,128]{1,0:T(8,128)S(1)} collective-permute-done((f32[128,128]{1,0:T(8,128)S(1)}, f32[128,128]{1,0:T(8,128)S(1)}, u32[]{:S(2)}, u32[]{:S(2)}) %collective-permute-start.2) | collective-permute-done | bytes 65568 | tf_op jit(solution)/shard_map/ppermute | solution.py:291
  13.5 0.6 copy-done.2
  14.3 2.1 %pack.1 = (f32[128,512]{1,0:T(8,128)}, f32[128,512]{1,0:T(8,128)}, f32[128,512]{1,0:T(8,128)}, f32[128,512]{1,0:T(8,128)}) custom-call(f32[4,128,128]{2,1,0:T(8,128)} %get-tuple-element.24.keep_ref, f32[4,128,128]{2,1,0:T(8,128)} %copy-done.1, f32[128,128]{1,0:T(8,128)} %copy-done, f32[128,128]{1,0:T(8,128)} %copy-done.2), custom_call_target="tpu_custom_call" | custom-call | tf_op jit(solution)/shard_map/pack/pallas_call | solution.py:156
  16.4 1.9 %collective-permute-start.3 = (f32[128,512]{1,0:T(8,128)}, f32[128,512]{1,0:T(8,128)S(1)}, u32[]{:S(2)}, u32[]{:S(2)}) collective-permute-start(f32[128,512]{1,0:T(8,128)} %get-tuple-element.27), channel_id=1, source_target_pairs={{0,0},{1,16},{2,32},{3,48},{4,64},{5,80},{6,96},{7,112},{8,1},{9,1... | collective-permute-start | bytes 786440 | tf_op jit(solution)/shard_map/ppermute | solution.py:291
  18.3 3.0 %collective-permute-start.4 = (f32[128,512]{1,0:T(8,128)}, f32[128,512]{1,0:T(8,128)S(1)}, u32[]{:S(2)}, u32[]{:S(2)}) collective-permute-start(f32[128,512]{1,0:T(8,128)} %get-tuple-element.28), channel_id=1, source_target_pairs={{0,4},{1,20},{2,36},{3,52},{4,68},{5,84},{6,100},{7,116},{8,5},{9,... | collective-permute-start | bytes 786440 | tf_op jit(solution)/shard_map/ppermute | solution.py:291
  21.3 1.3 %collective-permute-start.5 = (f32[128,512]{1,0:T(8,128)}, f32[128,512]{1,0:T(8,128)S(1)}, u32[]{:S(2)}, u32[]{:S(2)}) collective-permute-start(f32[128,512]{1,0:T(8,128)} %get-tuple-element.29), channel_id=1, source_target_pairs={{0,8},{1,24},{2,40},{3,56},{4,72},{5,88},{6,104},{7,120},{8,9},{9,... | collective-permute-start | bytes 786440 | tf_op jit(solution)/shard_map/ppermute | solution.py:291
  22.6 2.6 %collective-permute-start.6 = (f32[128,512]{1,0:T(8,128)}, f32[128,512]{1,0:T(8,128)S(1)}, u32[]{:S(2)}, u32[]{:S(2)}) collective-permute-start(f32[128,512]{1,0:T(8,128)} %get-tuple-element.30), channel_id=1, source_target_pairs={{0,12},{1,28},{2,44},{3,60},{4,76},{5,92},{6,108},{7,124},{8,13},{... | collective-permute-start | bytes 786440 | tf_op jit(solution)/shard_map/ppermute | solution.py:291
  25.2 1.3 %collective-permute-start.8 = (f32[128,1024]{1,0:T(8,128)}, f32[128,1024]{1,0:T(8,128)S(1)}, u32[]{:S(2)}, u32[]{:S(2)}) collective-permute-start(f32[128,1024]{1,0:T(8,128)} %get-tuple-element.32), channel_id=1, source_target_pairs={{0,96},{1,97},{2,98},{3,99},{4,100},{5,101},{6,102},{7,103},{8,104... | collective-permute-start | bytes 1572872 | tf_op jit(solution)/shard_map/ppermute | solution.py:291
  26.6 4.8 %collective-permute-done.3 = f32[128,512]{1,0:T(8,128)S(1)} collective-permute-done((f32[128,512]{1,0:T(8,128)}, f32[128,512]{1,0:T(8,128)S(1)}, u32[]{:S(2)}, u32[]{:S(2)}) %collective-permute-start.3) | collective-permute-done | bytes 262176 | tf_op jit(solution)/shard_map/ppermute | solution.py:291
  31.4 1.9 %collective-permute-done.5 = f32[128,512]{1,0:T(8,128)S(1)} collective-permute-done((f32[128,512]{1,0:T(8,128)}, f32[128,512]{1,0:T(8,128)S(1)}, u32[]{:S(2)}, u32[]{:S(2)}) %collective-permute-start.5) | collective-permute-done | bytes 262176 | tf_op jit(solution)/shard_map/ppermute | solution.py:291
  33.4 3.0 %collective-permute-done.6 = f32[128,512]{1,0:T(8,128)S(1)} collective-permute-done((f32[128,512]{1,0:T(8,128)}, f32[128,512]{1,0:T(8,128)S(1)}, u32[]{:S(2)}, u32[]{:S(2)}) %collective-permute-start.6) | collective-permute-done | bytes 262176 | tf_op jit(solution)/shard_map/ppermute | solution.py:291
  36.5 1.3 %collective-permute-start.7 = (f32[128,256]{1,0:T(8,128)S(1)}, f32[128,256]{1,0:T(8,128)S(1)}, u32[]{:S(2)}, u32[]{:S(2)}) collective-permute-start(f32[128,256]{1,0:T(8,128)S(1)} %get-tuple-element.31), channel_id=1, source_target_pairs={{0,32},{2,34},{4,36},{6,38},{8,40},{10,42},{12,44},{14,46},{16,48}... | collective-permute-start | bytes 393224 | tf_op jit(solution)/shard_map/ppermute | solution.py:291
  37.9 1.1 %collective-permute-start.12 = (f32[128,256]{1,0:T(8,128)S(1)}, f32[128,256]{1,0:T(8,128)S(1)}, u32[]{:S(2)}, u32[]{:S(2)}) collective-permute-start(f32[128,256]{1,0:T(8,128)S(1)} %get-tuple-element.34), channel_id=1, source_target_pairs={{0,2},{1,3},{2,0},{3,1},{4,6},{5,7},{6,4},{7,5},{8,10},{9,11},{10,... | collective-permute-start | bytes 393224 | tf_op jit(solution)/shard_map/ppermute | solution.py:291
  39.0 4.1 %collective-permute-start.11 = (f32[128,256]{1,0:T(8,128)S(1)}, f32[128,256]{1,0:T(8,128)S(1)}, u32[]{:S(2)}, u32[]{:S(2)}) collective-permute-start(f32[128,256]{1,0:T(8,128)S(1)} %get-tuple-element.34), channel_id=1, source_target_pairs={{0,3},{1,0},{2,1},{3,2},{4,7},{5,4},{6,5},{7,6},{8,11},{9,8},{10,9... | collective-permute-start | bytes 393224 | tf_op jit(solution)/shard_map/ppermute | solution.py:291
  43.1 0.5 collective-permute-start.10
  43.6 1.1 %broadcast_select_fusion.1 = f32[128,1024]{1,0:T(8,128)S(1)} fusion(f32[128,1024]{1,0:T(8,128)} %get-tuple-element.32, f32[128,1024]{1,0:T(8,128)S(1)} %collective-permute-done.8, pred[]{:T(512)S(6)} %eq.18), kind=kLoop, calls=%fused_computation.3 | loop fusion | flops 131072 | bytes 1572865 | tf_op jit(solution)/shard_map/jit(_where)/select_n | solution.py:330
  44.7 1.3 %collective-permute-start.14 = (f32[128,1024]{1,0:T(8,128)S(1)}, f32[128,1024]{1,0:T(8,128)S(1)}, u32[]{:S(2)}, u32[]{:S(2)}) collective-permute-start(f32[128,1024]{1,0:T(8,128)S(1)} %broadcast_select_fusion.1), channel_id=1, source_target_pairs={{0,32},{1,33},{2,34},{3,35},{4,36},{5,37},{6,38},{7,39},{8,40},{9,... | collective-permute-start | bytes 1572872 | tf_op jit(solution)/shard_map/ppermute | solution.py:291
  46.0 1.3 %collective-permute-start.9 = (f32[128,256]{1,0:T(8,128)S(1)}, f32[128,256]{1,0:T(8,128)S(1)}, u32[]{:S(2)}, u32[]{:S(2)}) collective-permute-start(f32[128,256]{1,0:T(8,128)S(1)} %broadcast_select_fusion.2), channel_id=1, source_target_pairs={{0,1},{2,3},{4,5},{6,7},{8,9},{10,11},{12,13},{14,15},{16,17},{18,... | collective-permute-start | bytes 393224 | tf_op jit(solution)/shard_map/ppermute | solution.py:291
  47.4 0.3 collective-permute-done.11
  47.7 0.7 collective-permute-done.10
  48.4 2.0 %collective-permute-done.9 = f32[128,256]{1,0:T(8,128)S(1)} collective-permute-done((f32[128,256]{1,0:T(8,128)S(1)}, f32[128,256]{1,0:T(8,128)S(1)}, u32[]{:S(2)}, u32[]{:S(2)}) %collective-permute-start.9) | collective-permute-done | bytes 131104 | tf_op jit(solution)/shard_map/ppermute | solution.py:291
  50.5 0.7 collective-permute-start.13
  51.1 3.1 %collective-permute-start.17 = (f32[4,128,256]{2,1,0:T(8,128)S(1)}, f32[4,128,256]{2,1,0:T(8,128)S(1)}, u32[]{:S(2)}, u32[]{:S(2)}) collective-permute-start(f32[4,128,256]{2,1,0:T(8,128)S(1)} %pad_maximum_fusion.row0_ref), channel_id=1, source_target_pairs={{0,8},{1,9},{2,10},{3,11},{4,12},{5,13},{6,14},{7,15},{8,0},{9,1},... | collective-permute-start | bytes 1572872 | tf_op jit(solution)/shard_map/ppermute | solution.py:291
  54.3 1.4 %collective-permute-start.16 = (f32[4,128,256]{2,1,0:T(8,128)S(1)}, f32[4,128,256]{2,1,0:T(8,128)S(1)}, u32[]{:S(2)}, u32[]{:S(2)}) collective-permute-start(f32[4,128,256]{2,1,0:T(8,128)S(1)} %pad_maximum_fusion.row0_ref), channel_id=1, source_target_pairs={{0,12},{1,13},{2,14},{3,15},{4,0},{5,1},{6,2},{7,3},{8,4},{9,5},{1... | collective-permute-start | bytes 1572872 | tf_op jit(solution)/shard_map/ppermute | solution.py:291
  55.8 8.9 %head.1 = (f32[2,128,256]{2,1,0:T(8,128)S(1)}, f32[256,256]{1,0:T(8,128)S(1)}) custom-call(f32[128,256]{1,0:T(8,128)S(1)} %broadcast_select_fusion.3.mine_ref, f32[128,256]{1,0:T(8,128)S(1)} %collective-permute-done.13.other_ref), custom_call_target="tpu_custom_call" | custom-call | flops 100000000 | bytes 1000000 | tf_op jit(solution)/shard_map/head/pallas_call | solution.py:87
  65.1 3.4 %hold.1.a_ref = f32[16,128,1024]{2,1,0:T(8,128)S(1)} custom-call(f32[16,128,1024]{2,1,0:T(8,128)} %bitcast.7), custom_call_target="tpu_custom_call" | custom-call | bytes 8388608 | tf_op jit(solution)/shard_map/hold/pallas_call | solution.py:106
  68.5 9.0 %update.1 = (f32[16,128,1024]{2,1,0:T(8,128)}, f32[16,128,256]{2,1,0:T(8,128)}) custom-call(f32[2,128,256]{2,1,0:T(8,128)S(1)} %get-tuple-element.36.lower_ref, f32[256,256]{1,0:T(8,128)S(1)} %get-tuple-element.39.inverse_ref, f32[4,128,256]{2,1,0:T(8,128)S(1)} %pad_maximum_fusion.row0_ref, f32[4,128,256]{2,1,0:T(8,128)S(1)} %collective-permute-done.15.row1_ref, ...), custom_call_target="tpu_custom_call" | custom-call | tf_op jit(solution)/shard_map/update/pallas_call | solution.py:256
  (25 shorter events, 0.7 us)
Async XLA Ops:
  2.7 6.8 %collective-permute-start.1 = (f32[128,128]{1,0:T(8,128)}, f32[128,128]{1,0:T(8,128)S(1)}, u32[]{:S(2)}, u32[]{:S(2)}) collective-permute-start(f32[128,128]{1,0:T(8,128)} %get-tuple-element.26), channel_id=1, source_target_pairs={{0,4},{1,5},{16,20},{17,21}} | collective-permute-start | bytes 196616 | tf_op jit(solution)/shard_map/ppermute | solution.py:291
  6.6 6.9 %collective-permute-start = (f32[4,128,128]{2,1,0:T(8,128)}, f32[4,128,128]{2,1,0:T(8,128)S(1)}, u32[]{:S(2)}, u32[]{:S(2)}) collective-permute-start(f32[4,128,128]{2,1,0:T(8,128)} %get-tuple-element.25), channel_id=1, source_target_pairs={{0,16},{1,17},{2,18},{3,19},{4,20},{5,21},{6,22},{7,23},{8,24},{9,... | collective-permute-start | bytes 786440 | tf_op jit(solution)/shard_map/ppermute | solution.py:291
  10.4 3.2 %copy-start = (f32[128,128]{1,0:T(8,128)}, f32[128,128]{1,0:T(8,128)S(1)}, u32[]{:S(2)}) copy-start(f32[128,128]{1,0:T(8,128)S(1)} %broadcast_select_fusion.4.corner_ref) | copy-start | bytes 196612
  10.4 3.1 %collective-permute-start.2 = (f32[128,128]{1,0:T(8,128)S(1)}, f32[128,128]{1,0:T(8,128)S(1)}, u32[]{:S(2)}, u32[]{:S(2)}) collective-permute-start(f32[128,128]{1,0:T(8,128)S(1)} %broadcast_select_fusion.4.corner_ref), channel_id=1, source_target_pairs={{0,16},{1,17},{4,20},{5,21},{16,0},{17,1},{20,4},{21,5}} | collective-permute-start | bytes 196616 | tf_op jit(solution)/shard_map/ppermute | solution.py:291
  13.5 0.6 copy-start.2
  13.5 0.7 copy-start.1
  16.4 15.0 %collective-permute-start.3 = (f32[128,512]{1,0:T(8,128)}, f32[128,512]{1,0:T(8,128)S(1)}, u32[]{:S(2)}, u32[]{:S(2)}) collective-permute-start(f32[128,512]{1,0:T(8,128)} %get-tuple-element.27), channel_id=1, source_target_pairs={{0,0},{1,16},{2,32},{3,48},{4,64},{5,80},{6,96},{7,112},{8,1},{9,1... | collective-permute-start | bytes 786440 | tf_op jit(solution)/shard_map/ppermute | solution.py:291
  18.3 13.1 %collective-permute-start.4 = (f32[128,512]{1,0:T(8,128)}, f32[128,512]{1,0:T(8,128)S(1)}, u32[]{:S(2)}, u32[]{:S(2)}) collective-permute-start(f32[128,512]{1,0:T(8,128)} %get-tuple-element.28), channel_id=1, source_target_pairs={{0,4},{1,20},{2,36},{3,52},{4,68},{5,84},{6,100},{7,116},{8,5},{9,... | collective-permute-start | bytes 786440 | tf_op jit(solution)/shard_map/ppermute | solution.py:291
  21.3 12.1 %collective-permute-start.5 = (f32[128,512]{1,0:T(8,128)}, f32[128,512]{1,0:T(8,128)S(1)}, u32[]{:S(2)}, u32[]{:S(2)}) collective-permute-start(f32[128,512]{1,0:T(8,128)} %get-tuple-element.29), channel_id=1, source_target_pairs={{0,8},{1,24},{2,40},{3,56},{4,72},{5,88},{6,104},{7,120},{8,9},{9,... | collective-permute-start | bytes 786440 | tf_op jit(solution)/shard_map/ppermute | solution.py:291
  22.6 13.8 %collective-permute-start.6 = (f32[128,512]{1,0:T(8,128)}, f32[128,512]{1,0:T(8,128)S(1)}, u32[]{:S(2)}, u32[]{:S(2)}) collective-permute-start(f32[128,512]{1,0:T(8,128)} %get-tuple-element.30), channel_id=1, source_target_pairs={{0,12},{1,28},{2,44},{3,60},{4,76},{5,92},{6,108},{7,124},{8,13},{... | collective-permute-start | bytes 786440 | tf_op jit(solution)/shard_map/ppermute | solution.py:291
  25.2 18.3 %collective-permute-start.8 = (f32[128,1024]{1,0:T(8,128)}, f32[128,1024]{1,0:T(8,128)S(1)}, u32[]{:S(2)}, u32[]{:S(2)}) collective-permute-start(f32[128,1024]{1,0:T(8,128)} %get-tuple-element.32), channel_id=1, source_target_pairs={{0,96},{1,97},{2,98},{3,99},{4,100},{5,101},{6,102},{7,103},{8,104... | collective-permute-start | bytes 1572872 | tf_op jit(solution)/shard_map/ppermute | solution.py:291
  36.5 7.0 %collective-permute-start.7 = (f32[128,256]{1,0:T(8,128)S(1)}, f32[128,256]{1,0:T(8,128)S(1)}, u32[]{:S(2)}, u32[]{:S(2)}) collective-permute-start(f32[128,256]{1,0:T(8,128)S(1)} %get-tuple-element.31), channel_id=1, source_target_pairs={{0,32},{2,34},{4,36},{6,38},{8,40},{10,42},{12,44},{14,46},{16,48}... | collective-permute-start | bytes 393224 | tf_op jit(solution)/shard_map/ppermute | solution.py:291
  37.9 9.5 %collective-permute-start.12 = (f32[128,256]{1,0:T(8,128)S(1)}, f32[128,256]{1,0:T(8,128)S(1)}, u32[]{:S(2)}, u32[]{:S(2)}) collective-permute-start(f32[128,256]{1,0:T(8,128)S(1)} %get-tuple-element.34), channel_id=1, source_target_pairs={{0,2},{1,3},{2,0},{3,1},{4,6},{5,7},{6,4},{7,5},{8,10},{9,11},{10,... | collective-permute-start | bytes 393224 | tf_op jit(solution)/shard_map/ppermute | solution.py:291
  39.0 8.7 %collective-permute-start.11 = (f32[128,256]{1,0:T(8,128)S(1)}, f32[128,256]{1,0:T(8,128)S(1)}, u32[]{:S(2)}, u32[]{:S(2)}) collective-permute-start(f32[128,256]{1,0:T(8,128)S(1)} %get-tuple-element.34), channel_id=1, source_target_pairs={{0,3},{1,0},{2,1},{3,2},{4,7},{5,4},{6,5},{7,6},{8,11},{9,8},{10,9... | collective-permute-start | bytes 393224 | tf_op jit(solution)/shard_map/ppermute | solution.py:291
  43.1 5.3 %collective-permute-start.10 = (f32[128,256]{1,0:T(8,128)S(1)}, f32[128,256]{1,0:T(8,128)S(1)}, u32[]{:S(2)}, u32[]{:S(2)}) collective-permute-start(f32[128,256]{1,0:T(8,128)S(1)} %get-tuple-element.34), channel_id=1, source_target_pairs={{0,1},{1,2},{2,3},{3,0},{4,5},{5,6},{6,7},{7,4},{8,9},{9,10},{10,1... | collective-permute-start | bytes 393224 | tf_op jit(solution)/shard_map/ppermute | solution.py:291
  44.7 20.0 %collective-permute-start.14 = (f32[128,1024]{1,0:T(8,128)S(1)}, f32[128,1024]{1,0:T(8,128)S(1)}, u32[]{:S(2)}, u32[]{:S(2)}) collective-permute-start(f32[128,1024]{1,0:T(8,128)S(1)} %broadcast_select_fusion.1), channel_id=1, source_target_pairs={{0,32},{1,33},{2,34},{3,35},{4,36},{5,37},{6,38},{7,39},{8,40},{9,... | collective-permute-start | bytes 1572872 | tf_op jit(solution)/shard_map/ppermute | solution.py:291
  46.0 4.4 %collective-permute-start.9 = (f32[128,256]{1,0:T(8,128)S(1)}, f32[128,256]{1,0:T(8,128)S(1)}, u32[]{:S(2)}, u32[]{:S(2)}) collective-permute-start(f32[128,256]{1,0:T(8,128)S(1)} %broadcast_select_fusion.2), channel_id=1, source_target_pairs={{0,1},{2,3},{4,5},{6,7},{8,9},{10,11},{12,13},{14,15},{16,17},{18,... | collective-permute-start | bytes 393224 | tf_op jit(solution)/shard_map/ppermute | solution.py:291
  50.5 5.4 %collective-permute-start.13 = (f32[128,256]{1,0:T(8,128)S(1)}, f32[128,256]{1,0:T(8,128)S(1)}, u32[]{:S(2)}, u32[]{:S(2)}) collective-permute-start(f32[128,256]{1,0:T(8,128)S(1)} %broadcast_select_fusion.3.mine_ref), channel_id=1, source_target_pairs={{0,16},{1,17},{2,18},{3,19},{4,20},{5,21},{6,22},{7,23},{8,24},{9,... | collective-permute-start | bytes 393224 | tf_op jit(solution)/shard_map/ppermute | solution.py:291
  51.1 17.4 %collective-permute-start.17 = (f32[4,128,256]{2,1,0:T(8,128)S(1)}, f32[4,128,256]{2,1,0:T(8,128)S(1)}, u32[]{:S(2)}, u32[]{:S(2)}) collective-permute-start(f32[4,128,256]{2,1,0:T(8,128)S(1)} %pad_maximum_fusion.row0_ref), channel_id=1, source_target_pairs={{0,8},{1,9},{2,10},{3,11},{4,12},{5,13},{6,14},{7,15},{8,0},{9,1},... | collective-permute-start | bytes 1572872 | tf_op jit(solution)/shard_map/ppermute | solution.py:291
  54.3 14.2 %collective-permute-start.16 = (f32[4,128,256]{2,1,0:T(8,128)S(1)}, f32[4,128,256]{2,1,0:T(8,128)S(1)}, u32[]{:S(2)}, u32[]{:S(2)}) collective-permute-start(f32[4,128,256]{2,1,0:T(8,128)S(1)} %pad_maximum_fusion.row0_ref), channel_id=1, source_target_pairs={{0,12},{1,13},{2,14},{3,15},{4,0},{5,1},{6,2},{7,3},{8,4},{9,5},{1... | collective-permute-start | bytes 1572872 | tf_op jit(solution)/shard_map/ppermute | solution.py:291
  55.7 12.8 %collective-permute-start.15 = (f32[4,128,256]{2,1,0:T(8,128)S(1)}, f32[4,128,256]{2,1,0:T(8,128)S(1)}, u32[]{:S(2)}, u32[]{:S(2)}) collective-permute-start(f32[4,128,256]{2,1,0:T(8,128)S(1)} %pad_maximum_fusion.row0_ref), channel_id=1, source_target_pairs={{0,4},{1,5},{2,6},{3,7},{4,8},{5,9},{6,10},{7,11},{8,12},{9,13},{1... | collective-permute-start | bytes 1572872 | tf_op jit(solution)/shard_map/ppermute | solution.py:291
  64.8 3.7 %collective-permute-start.18 = (f32[128,1024]{1,0:T(8,128)S(1)}, f32[128,1024]{1,0:T(8,128)S(1)}, u32[]{:S(2)}, u32[]{:S(2)}) collective-permute-start(f32[128,1024]{1,0:T(8,128)S(1)} %broadcast_select_fusion.tall_ref), channel_id=1, source_target_pairs={{0,16},{1,17},{2,18},{3,19},{4,20},{5,21},{6,22},{7,23},{8,24},{9,... | collective-permute-start | bytes 1572872 | tf_op jit(solution)/shard_map/ppermute | solution.py:291

commit v6 on v5

--- a/solution.py
+++ b/solution.py
@@ -11,6 +11,7 @@
 WIDE = 2 * BLOCK
 GROUP = 8
 SHIFTS = (0, 1, 3, 2)
+ORDER = (0, 1, 2, 3)
 F32 = jnp.float32
 BF16 = jnp.bfloat16
 AXES = ("row", "col")
@@ -145,7 +146,9 @@
     first = lax.axis_index("row") % 2 == 0
     upper = jnp.where(first, corner_ref[...], beside_ref[...])
     lower = jnp.where(first, beside_ref[...], corner_ref[...])
-    for b, out_ref in enumerate(out_refs):
+    count = keep_ref.shape[0]
+    for shift, out_ref in zip(ORDER, out_refs, strict=True):
+        b = (lax.axis_index("col") // 4 + shift) % count
         out_ref[:, :BLOCK] = jnp.where(first, keep_ref[b], other_ref[b])
         out_ref[:, BLOCK:WIDE] = jnp.where(first, other_ref[b], keep_ref[b])
         out_ref[:, WIDE : WIDE + BLOCK] = upper
@@ -314,9 +317,13 @@
     parts = [
         send(
             message,
-            [(at(r, c), at(c % n_row, 2 * (2 * b + r) + c // n_row)) for r in (0, 1) for c in every_col],
+            [
+                (at(r, c), at(c % n_row, 2 * (2 * ((c // 4 + shift) % 4) + r) + c // n_row))
+                for r in (0, 1)
+                for c in every_col
+            ],
         )
-        for b, message in enumerate(messages)
+        for shift, message in zip(ORDER, messages, strict=True)
     ]
     total = parts[0] + parts[1] + parts[2] + parts[3]
     block, corner = total[:, :WIDE], total[:, WIDE:]

time: 78.4 us -> 77.8 us (level)
  transfers between devices with their start and end apart: 19 -> 19, of which waited for: 7 -> 6; matrix products, arithmetic and copies ran while one was open for 3% -> 3% of each run, Pallas kernels for 16% -> 16%
where the time goes in v6:
time: 77.8 us; the launch traced here: 77.2 us
  starting transfers between devices  33.8 us (43%)
  Pallas kernels  25.4 us (33%)
  waiting for transfers between devices  14 us (18%)
  other arithmetic  2.17 us (3%)
  between operations  1.09 us (1%)
    ppermute x19, starting transfers between devices, send(): return lax.ppermute(x, AXES, pairs)  33.8 us
    ppermute x19, waiting for transfers between devices, send(): return lax.ppermute(x, AXES, pairs)  14 us
    pallas_call x1, Pallas kernels, update(): pl.pallas_call(update_kernel, in_specs=[here] * 2 + [there] * 6 + [here],...  8.98 us
    pallas_call x1, Pallas kernels, head(): pl.pallas_call(head_kernel, out_shape=(jax.ShapeDtypeStruct((2, BLOCK, WI...  8.89 us
    pallas_call x1, Pallas kernels, hold(): pl.pallas_call(hold_kernel, in_specs=[pl.BlockSpec(memory_space=pltpu.HBM...  3.39 us
    pallas_call x1, Pallas kernels, pack(): pl.pallas_call(pack_kernel, out_shape=(jax.ShapeDtypeStruct((BLOCK, 2 * W...  2.13 us
    pallas_call x1, Pallas kernels, open_strip(): pl.pallas_call(open_kernel, in_specs=[pl.BlockSpec(memory_space=pl.ANY)],...  2.04 us
  transfers between devices with their start and end apart: 19, of which 6 were waited for; matrix products, arithmetic and copies ran while one was open for 3% of the time, Pallas kernels for 16%

profile of v6, /device:TPU:1, one launch (start us, length us, event | category | flops | bytes accessed | tf_op | source)
XLA Modules:
  0.0 77.2 jit_solution(7264096427910155233)
XLA Ops:
  0.6 2.0 %open.1 = (f32[128,1024]{1,0:T(8,128)}, f32[128,128]{1,0:T(8,128)}, f32[4,128,128]{2,1,0:T(8,128)}, f32[4,128,128]{2,1,0:T(8,128)}) custom-call(f32[2048,1024]{1,0:T(8,128)} %stored_ref.1), custom_call_target="tpu_custom_call" | custom-call | tf_op jit(solution)/shard_map/open/pallas_call | solution.py:136
  2.7 3.9 %collective-permute-start.1 = (f32[128,128]{1,0:T(8,128)}, f32[128,128]{1,0:T(8,128)S(1)}, u32[]{:S(2)}, u32[]{:S(2)}) collective-permute-start(f32[128,128]{1,0:T(8,128)} %get-tuple-element.26), channel_id=1, source_target_pairs={{0,4},{1,5},{16,20},{17,21}} | collective-permute-start | bytes 196616 | tf_op jit(solution)/shard_map/ppermute | solution.py:294
  6.6 2.9 %collective-permute-start = (f32[4,128,128]{2,1,0:T(8,128)}, f32[4,128,128]{2,1,0:T(8,128)S(1)}, u32[]{:S(2)}, u32[]{:S(2)}) collective-permute-start(f32[4,128,128]{2,1,0:T(8,128)} %get-tuple-element.25), channel_id=1, source_target_pairs={{0,16},{1,17},{2,18},{3,19},{4,20},{5,21},{6,22},{7,23},{8,24},{9,... | collective-permute-start | bytes 786440 | tf_op jit(solution)/shard_map/ppermute | solution.py:294
  9.5 0.9 %broadcast_select_fusion.4.corner_ref = f32[128,128]{1,0:T(8,128)S(1)} fusion(f32[128,128]{1,0:T(8,128)} %get-tuple-element.26, f32[128,128]{1,0:T(8,128)S(1)} %collective-permute-done.1, pred[]{:T(512)S(6)} %lt.19), kind=kLoop, calls=%fused_computation.6 | loop fusion | flops 16384 | bytes 196609 | tf_op jit(solution)/shard_map/jit(_where)/select_n | solution.py:312
  10.4 2.2 %collective-permute-start.2 = (f32[128,128]{1,0:T(8,128)S(1)}, f32[128,128]{1,0:T(8,128)S(1)}, u32[]{:S(2)}, u32[]{:S(2)}) collective-permute-start(f32[128,128]{1,0:T(8,128)S(1)} %broadcast_select_fusion.4.corner_ref), channel_id=1, source_target_pairs={{0,16},{1,17},{4,20},{5,21},{16,0},{17,1},{20,4},{21,5}} | collective-permute-start | bytes 196616 | tf_op jit(solution)/shard_map/ppermute | solution.py:294
  12.6 1.0 %collective-permute-done.2.beside_ref = f32[128,128]{1,0:T(8,128)S(1)} collective-permute-done((f32[128,128]{1,0:T(8,128)S(1)}, f32[128,128]{1,0:T(8,128)S(1)}, u32[]{:S(2)}, u32[]{:S(2)}) %collective-permute-start.2) | collective-permute-done | bytes 65568 | tf_op jit(solution)/shard_map/ppermute | solution.py:294
  13.5 0.6 copy-done.2
  14.3 2.1 %pack.1 = (f32[128,512]{1,0:T(8,128)}, f32[128,512]{1,0:T(8,128)}, f32[128,512]{1,0:T(8,128)}, f32[128,512]{1,0:T(8,128)}) custom-call(f32[4,128,128]{2,1,0:T(8,128)} %get-tuple-element.24.keep_ref, f32[4,128,128]{2,1,0:T(8,128)} %copy-done.1, f32[128,128]{1,0:T(8,128)} %copy-done, f32[128,128]{1,0:T(8,128)} %copy-done.2), custom_call_target="tpu_custom_call" | custom-call | tf_op jit(solution)/shard_map/pack/pallas_call | solution.py:159
  16.4 1.9 %collective-permute-start.3 = (f32[128,512]{1,0:T(8,128)}, f32[128,512]{1,0:T(8,128)S(1)}, u32[]{:S(2)}, u32[]{:S(2)}) collective-permute-start(f32[128,512]{1,0:T(8,128)} %get-tuple-element.27), channel_id=1, source_target_pairs={{0,0},{1,16},{2,32},{3,48},{4,68},{5,84},{6,100},{7,116},{8,9},{9,... | collective-permute-start | bytes 786440 | tf_op jit(solution)/shard_map/ppermute | solution.py:294
  18.3 2.2 %collective-permute-start.4 = (f32[128,512]{1,0:T(8,128)}, f32[128,512]{1,0:T(8,128)S(1)}, u32[]{:S(2)}, u32[]{:S(2)}) collective-permute-start(f32[128,512]{1,0:T(8,128)} %get-tuple-element.28), channel_id=1, source_target_pairs={{0,4},{1,20},{2,36},{3,52},{4,72},{5,88},{6,104},{7,120},{8,13},{9... | collective-permute-start | bytes 786440 | tf_op jit(solution)/shard_map/ppermute | solution.py:294
  20.5 1.3 %collective-permute-start.5 = (f32[128,512]{1,0:T(8,128)}, f32[128,512]{1,0:T(8,128)S(1)}, u32[]{:S(2)}, u32[]{:S(2)}) collective-permute-start(f32[128,512]{1,0:T(8,128)} %get-tuple-element.29), channel_id=1, source_target_pairs={{0,8},{1,24},{2,40},{3,56},{4,76},{5,92},{6,108},{7,124},{8,1},{9,... | collective-permute-start | bytes 786440 | tf_op jit(solution)/shard_map/ppermute | solution.py:294
  21.8 2.8 %collective-permute-start.6 = (f32[128,512]{1,0:T(8,128)}, f32[128,512]{1,0:T(8,128)S(1)}, u32[]{:S(2)}, u32[]{:S(2)}) collective-permute-start(f32[128,512]{1,0:T(8,128)} %get-tuple-element.30), channel_id=1, source_target_pairs={{0,12},{1,28},{2,44},{3,60},{4,64},{5,80},{6,96},{7,112},{8,5},{9,... | collective-permute-start | bytes 786440 | tf_op jit(solution)/shard_map/ppermute | solution.py:294
  24.6 1.3 %collective-permute-start.8 = (f32[128,1024]{1,0:T(8,128)}, f32[128,1024]{1,0:T(8,128)S(1)}, u32[]{:S(2)}, u32[]{:S(2)}) collective-permute-start(f32[128,1024]{1,0:T(8,128)} %get-tuple-element.32), channel_id=1, source_target_pairs={{0,96},{1,97},{2,98},{3,99},{4,100},{5,101},{6,102},{7,103},{8,104... | collective-permute-start | bytes 1572872 | tf_op jit(solution)/shard_map/ppermute | solution.py:294
  26.0 1.1 %collective-permute-done.3 = f32[128,512]{1,0:T(8,128)S(1)} collective-permute-done((f32[128,512]{1,0:T(8,128)}, f32[128,512]{1,0:T(8,128)S(1)}, u32[]{:S(2)}, u32[]{:S(2)}) %collective-permute-start.3) | collective-permute-done | bytes 262176 | tf_op jit(solution)/shard_map/ppermute | solution.py:294
  27.1 5.1 %collective-permute-done.5 = f32[128,512]{1,0:T(8,128)S(1)} collective-permute-done((f32[128,512]{1,0:T(8,128)}, f32[128,512]{1,0:T(8,128)S(1)}, u32[]{:S(2)}, u32[]{:S(2)}) %collective-permute-start.5) | collective-permute-done | bytes 262176 | tf_op jit(solution)/shard_map/ppermute | solution.py:294
  32.2 1.5 %collective-permute-done.6 = f32[128,512]{1,0:T(8,128)S(1)} collective-permute-done((f32[128,512]{1,0:T(8,128)}, f32[128,512]{1,0:T(8,128)S(1)}, u32[]{:S(2)}, u32[]{:S(2)}) %collective-permute-start.6) | collective-permute-done | bytes 262176 | tf_op jit(solution)/shard_map/ppermute | solution.py:294
  33.8 1.3 %collective-permute-start.7 = (f32[128,256]{1,0:T(8,128)S(1)}, f32[128,256]{1,0:T(8,128)S(1)}, u32[]{:S(2)}, u32[]{:S(2)}) collective-permute-start(f32[128,256]{1,0:T(8,128)S(1)} %get-tuple-element.31), channel_id=1, source_target_pairs={{0,32},{2,34},{4,36},{6,38},{8,40},{10,42},{12,44},{14,46},{16,48}... | collective-permute-start | bytes 393224 | tf_op jit(solution)/shard_map/ppermute | solution.py:294
  35.2 3.4 %collective-permute-start.12 = (f32[128,256]{1,0:T(8,128)S(1)}, f32[128,256]{1,0:T(8,128)S(1)}, u32[]{:S(2)}, u32[]{:S(2)}) collective-permute-start(f32[128,256]{1,0:T(8,128)S(1)} %get-tuple-element.34), channel_id=1, source_target_pairs={{0,2},{1,3},{2,0},{3,1},{4,6},{5,7},{6,4},{7,5},{8,10},{9,11},{10,... | collective-permute-start | bytes 393224 | tf_op jit(solution)/shard_map/ppermute | solution.py:294
  38.5 1.3 %collective-permute-start.11 = (f32[128,256]{1,0:T(8,128)S(1)}, f32[128,256]{1,0:T(8,128)S(1)}, u32[]{:S(2)}, u32[]{:S(2)}) collective-permute-start(f32[128,256]{1,0:T(8,128)S(1)} %get-tuple-element.34), channel_id=1, source_target_pairs={{0,3},{1,0},{2,1},{3,2},{4,7},{5,4},{6,5},{7,6},{8,11},{9,8},{10,9... | collective-permute-start | bytes 393224 | tf_op jit(solution)/shard_map/ppermute | solution.py:294
  39.8 0.5 collective-permute-start.10
  40.3 2.9 %collective-permute-done.8 = f32[128,1024]{1,0:T(8,128)S(1)} collective-permute-done((f32[128,1024]{1,0:T(8,128)}, f32[128,1024]{1,0:T(8,128)S(1)}, u32[]{:S(2)}, u32[]{:S(2)}) %collective-permute-start.8) | collective-permute-done | bytes 524320 | tf_op jit(solution)/shard_map/ppermute | solution.py:294
  43.3 1.1 %broadcast_select_fusion.1 = f32[128,1024]{1,0:T(8,128)S(1)} fusion(f32[128,1024]{1,0:T(8,128)} %get-tuple-element.32, f32[128,1024]{1,0:T(8,128)S(1)} %collective-permute-done.8, pred[]{:T(512)S(6)} %eq.18), kind=kLoop, calls=%fused_computation.3 | loop fusion | flops 131072 | bytes 1572865 | tf_op jit(solution)/shard_map/jit(_where)/select_n | solution.py:337
  44.4 1.3 %collective-permute-start.14 = (f32[128,1024]{1,0:T(8,128)S(1)}, f32[128,1024]{1,0:T(8,128)S(1)}, u32[]{:S(2)}, u32[]{:S(2)}) collective-permute-start(f32[128,1024]{1,0:T(8,128)S(1)} %broadcast_select_fusion.1), channel_id=1, source_target_pairs={{0,32},{1,33},{2,34},{3,35},{4,36},{5,37},{6,38},{7,39},{8,40},{9,... | collective-permute-start | bytes 1572872 | tf_op jit(solution)/shard_map/ppermute | solution.py:294
  45.7 1.3 %collective-permute-start.9 = (f32[128,256]{1,0:T(8,128)S(1)}, f32[128,256]{1,0:T(8,128)S(1)}, u32[]{:S(2)}, u32[]{:S(2)}) collective-permute-start(f32[128,256]{1,0:T(8,128)S(1)} %broadcast_select_fusion.2), channel_id=1, source_target_pairs={{0,1},{2,3},{4,5},{6,7},{8,9},{10,11},{12,13},{14,15},{16,17},{18,... | collective-permute-start | bytes 393224 | tf_op jit(solution)/shard_map/ppermute | solution.py:294
  47.1 2.3 %collective-permute-done.9 = f32[128,256]{1,0:T(8,128)S(1)} collective-permute-done((f32[128,256]{1,0:T(8,128)S(1)}, f32[128,256]{1,0:T(8,128)S(1)}, u32[]{:S(2)}, u32[]{:S(2)}) %collective-permute-start.9) | collective-permute-done | bytes 131104 | tf_op jit(solution)/shard_map/ppermute | solution.py:294
  49.4 1.4 %collective-permute-start.13 = (f32[128,256]{1,0:T(8,128)S(1)}, f32[128,256]{1,0:T(8,128)S(1)}, u32[]{:S(2)}, u32[]{:S(2)}) collective-permute-start(f32[128,256]{1,0:T(8,128)S(1)} %broadcast_select_fusion.3.mine_ref), channel_id=1, source_target_pairs={{0,16},{1,17},{2,18},{3,19},{4,20},{5,21},{6,22},{7,23},{8,24},{9,... | collective-permute-start | bytes 393224 | tf_op jit(solution)/shard_map/ppermute | solution.py:294
  50.8 0.5 collective-permute-start.17
  51.3 4.1 %collective-permute-start.16 = (f32[4,128,256]{2,1,0:T(8,128)S(1)}, f32[4,128,256]{2,1,0:T(8,128)S(1)}, u32[]{:S(2)}, u32[]{:S(2)}) collective-permute-start(f32[4,128,256]{2,1,0:T(8,128)S(1)} %pad_maximum_fusion.row0_ref), channel_id=1, source_target_pairs={{0,12},{1,13},{2,14},{3,15},{4,0},{5,1},{6,2},{7,3},{8,4},{9,5},{1... | collective-permute-start | bytes 1572872 | tf_op jit(solution)/shard_map/ppermute | solution.py:294
  55.4 8.9 %head.1 = (f32[2,128,256]{2,1,0:T(8,128)S(1)}, f32[256,256]{1,0:T(8,128)S(1)}) custom-call(f32[128,256]{1,0:T(8,128)S(1)} %broadcast_select_fusion.3.mine_ref, f32[128,256]{1,0:T(8,128)S(1)} %collective-permute-done.13.other_ref), custom_call_target="tpu_custom_call" | custom-call | flops 100000000 | bytes 1000000 | tf_op jit(solution)/shard_map/head/pallas_call | solution.py:88
  64.4 0.3 collective-permute-start.18
  64.7 3.4 %hold.1.a_ref = f32[16,128,1024]{2,1,0:T(8,128)S(1)} custom-call(f32[16,128,1024]{2,1,0:T(8,128)} %bitcast.7), custom_call_target="tpu_custom_call" | custom-call | bytes 8388608 | tf_op jit(solution)/shard_map/hold/pallas_call | solution.py:107
  68.1 9.0 %update.1 = (f32[16,128,1024]{2,1,0:T(8,128)}, f32[16,128,256]{2,1,0:T(8,128)}) custom-call(f32[2,128,256]{2,1,0:T(8,128)S(1)} %get-tuple-element.36.lower_ref, f32[256,256]{1,0:T(8,128)S(1)} %get-tuple-element.39.inverse_ref, f32[4,128,256]{2,1,0:T(8,128)S(1)} %pad_maximum_fusion.row0_ref, f32[4,128,256]{2,1,0:T(8,128)S(1)} %collective-permute-done.15.row1_ref, ...), custom_call_target="tpu_custom_call" | custom-call | tf_op jit(solution)/shard_map/update/pallas_call | solution.py:259
  (25 shorter events, 0.4 us)
Async XLA Ops:
  2.7 6.8 %collective-permute-start.1 = (f32[128,128]{1,0:T(8,128)}, f32[128,128]{1,0:T(8,128)S(1)}, u32[]{:S(2)}, u32[]{:S(2)}) collective-permute-start(f32[128,128]{1,0:T(8,128)} %get-tuple-element.26), channel_id=1, source_target_pairs={{0,4},{1,5},{16,20},{17,21}} | collective-permute-start | bytes 196616 | tf_op jit(solution)/shard_map/ppermute | solution.py:294
  6.6 6.9 %collective-permute-start = (f32[4,128,128]{2,1,0:T(8,128)}, f32[4,128,128]{2,1,0:T(8,128)S(1)}, u32[]{:S(2)}, u32[]{:S(2)}) collective-permute-start(f32[4,128,128]{2,1,0:T(8,128)} %get-tuple-element.25), channel_id=1, source_target_pairs={{0,16},{1,17},{2,18},{3,19},{4,20},{5,21},{6,22},{7,23},{8,24},{9,... | collective-permute-start | bytes 786440 | tf_op jit(solution)/shard_map/ppermute | solution.py:294
  10.4 3.2 %copy-start = (f32[128,128]{1,0:T(8,128)}, f32[128,128]{1,0:T(8,128)S(1)}, u32[]{:S(2)}) copy-start(f32[128,128]{1,0:T(8,128)S(1)} %broadcast_select_fusion.4.corner_ref) | copy-start | bytes 196612
  10.4 3.1 %collective-permute-start.2 = (f32[128,128]{1,0:T(8,128)S(1)}, f32[128,128]{1,0:T(8,128)S(1)}, u32[]{:S(2)}, u32[]{:S(2)}) collective-permute-start(f32[128,128]{1,0:T(8,128)S(1)} %broadcast_select_fusion.4.corner_ref), channel_id=1, source_target_pairs={{0,16},{1,17},{4,20},{5,21},{16,0},{17,1},{20,4},{21,5}} | collective-permute-start | bytes 196616 | tf_op jit(solution)/shard_map/ppermute | solution.py:294
  13.5 0.6 copy-start.2
  13.5 0.7 copy-start.1
  16.4 10.7 %collective-permute-start.3 = (f32[128,512]{1,0:T(8,128)}, f32[128,512]{1,0:T(8,128)S(1)}, u32[]{:S(2)}, u32[]{:S(2)}) collective-permute-start(f32[128,512]{1,0:T(8,128)} %get-tuple-element.27), channel_id=1, source_target_pairs={{0,0},{1,16},{2,32},{3,48},{4,68},{5,84},{6,100},{7,116},{8,9},{9,... | collective-permute-start | bytes 786440 | tf_op jit(solution)/shard_map/ppermute | solution.py:294
  18.3 8.8 %collective-permute-start.4 = (f32[128,512]{1,0:T(8,128)}, f32[128,512]{1,0:T(8,128)S(1)}, u32[]{:S(2)}, u32[]{:S(2)}) collective-permute-start(f32[128,512]{1,0:T(8,128)} %get-tuple-element.28), channel_id=1, source_target_pairs={{0,4},{1,20},{2,36},{3,52},{4,72},{5,88},{6,104},{7,120},{8,13},{9... | collective-permute-start | bytes 786440 | tf_op jit(solution)/shard_map/ppermute | solution.py:294
  20.5 11.7 %collective-permute-start.5 = (f32[128,512]{1,0:T(8,128)}, f32[128,512]{1,0:T(8,128)S(1)}, u32[]{:S(2)}, u32[]{:S(2)}) collective-permute-start(f32[128,512]{1,0:T(8,128)} %get-tuple-element.29), channel_id=1, source_target_pairs={{0,8},{1,24},{2,40},{3,56},{4,76},{5,92},{6,108},{7,124},{8,1},{9,... | collective-permute-start | bytes 786440 | tf_op jit(solution)/shard_map/ppermute | solution.py:294
  21.8 11.9 %collective-permute-start.6 = (f32[128,512]{1,0:T(8,128)}, f32[128,512]{1,0:T(8,128)S(1)}, u32[]{:S(2)}, u32[]{:S(2)}) collective-permute-start(f32[128,512]{1,0:T(8,128)} %get-tuple-element.30), channel_id=1, source_target_pairs={{0,12},{1,28},{2,44},{3,60},{4,64},{5,80},{6,96},{7,112},{8,5},{9,... | collective-permute-start | bytes 786440 | tf_op jit(solution)/shard_map/ppermute | solution.py:294
  24.6 18.6 %collective-permute-start.8 = (f32[128,1024]{1,0:T(8,128)}, f32[128,1024]{1,0:T(8,128)S(1)}, u32[]{:S(2)}, u32[]{:S(2)}) collective-permute-start(f32[128,1024]{1,0:T(8,128)} %get-tuple-element.32), channel_id=1, source_target_pairs={{0,96},{1,97},{2,98},{3,99},{4,100},{5,101},{6,102},{7,103},{8,104... | collective-permute-start | bytes 1572872 | tf_op jit(solution)/shard_map/ppermute | solution.py:294
  33.8 6.5 %collective-permute-start.7 = (f32[128,256]{1,0:T(8,128)S(1)}, f32[128,256]{1,0:T(8,128)S(1)}, u32[]{:S(2)}, u32[]{:S(2)}) collective-permute-start(f32[128,256]{1,0:T(8,128)S(1)} %get-tuple-element.31), channel_id=1, source_target_pairs={{0,32},{2,34},{4,36},{6,38},{8,40},{10,42},{12,44},{14,46},{16,48}... | collective-permute-start | bytes 393224 | tf_op jit(solution)/shard_map/ppermute | solution.py:294
  35.2 11.9 %collective-permute-start.12 = (f32[128,256]{1,0:T(8,128)S(1)}, f32[128,256]{1,0:T(8,128)S(1)}, u32[]{:S(2)}, u32[]{:S(2)}) collective-permute-start(f32[128,256]{1,0:T(8,128)S(1)} %get-tuple-element.34), channel_id=1, source_target_pairs={{0,2},{1,3},{2,0},{3,1},{4,6},{5,7},{6,4},{7,5},{8,10},{9,11},{10,... | collective-permute-start | bytes 393224 | tf_op jit(solution)/shard_map/ppermute | solution.py:294
  38.5 8.5 %collective-permute-start.11 = (f32[128,256]{1,0:T(8,128)S(1)}, f32[128,256]{1,0:T(8,128)S(1)}, u32[]{:S(2)}, u32[]{:S(2)}) collective-permute-start(f32[128,256]{1,0:T(8,128)S(1)} %get-tuple-element.34), channel_id=1, source_target_pairs={{0,3},{1,0},{2,1},{3,2},{4,7},{5,4},{6,5},{7,6},{8,11},{9,8},{10,9... | collective-permute-start | bytes 393224 | tf_op jit(solution)/shard_map/ppermute | solution.py:294
  39.8 7.2 %collective-permute-start.10 = (f32[128,256]{1,0:T(8,128)S(1)}, f32[128,256]{1,0:T(8,128)S(1)}, u32[]{:S(2)}, u32[]{:S(2)}) collective-permute-start(f32[128,256]{1,0:T(8,128)S(1)} %get-tuple-element.34), channel_id=1, source_target_pairs={{0,1},{1,2},{2,3},{3,0},{4,5},{5,6},{6,7},{7,4},{8,9},{9,10},{10,1... | collective-permute-start | bytes 393224 | tf_op jit(solution)/shard_map/ppermute | solution.py:294
  44.4 19.9 %collective-permute-start.14 = (f32[128,1024]{1,0:T(8,128)S(1)}, f32[128,1024]{1,0:T(8,128)S(1)}, u32[]{:S(2)}, u32[]{:S(2)}) collective-permute-start(f32[128,1024]{1,0:T(8,128)S(1)} %broadcast_select_fusion.1), channel_id=1, source_target_pairs={{0,32},{1,33},{2,34},{3,35},{4,36},{5,37},{6,38},{7,39},{8,40},{9,... | collective-permute-start | bytes 1572872 | tf_op jit(solution)/shard_map/ppermute | solution.py:294
  45.7 3.7 %collective-permute-start.9 = (f32[128,256]{1,0:T(8,128)S(1)}, f32[128,256]{1,0:T(8,128)S(1)}, u32[]{:S(2)}, u32[]{:S(2)}) collective-permute-start(f32[128,256]{1,0:T(8,128)S(1)} %broadcast_select_fusion.2), channel_id=1, source_target_pairs={{0,1},{2,3},{4,5},{6,7},{8,9},{10,11},{12,13},{14,15},{16,17},{18,... | collective-permute-start | bytes 393224 | tf_op jit(solution)/shard_map/ppermute | solution.py:294
  49.4 6.0 %collective-permute-start.13 = (f32[128,256]{1,0:T(8,128)S(1)}, f32[128,256]{1,0:T(8,128)S(1)}, u32[]{:S(2)}, u32[]{:S(2)}) collective-permute-start(f32[128,256]{1,0:T(8,128)S(1)} %broadcast_select_fusion.3.mine_ref), channel_id=1, source_target_pairs={{0,16},{1,17},{2,18},{3,19},{4,20},{5,21},{6,22},{7,23},{8,24},{9,... | collective-permute-start | bytes 393224 | tf_op jit(solution)/shard_map/ppermute | solution.py:294
  50.8 17.3 %collective-permute-start.17 = (f32[4,128,256]{2,1,0:T(8,128)S(1)}, f32[4,128,256]{2,1,0:T(8,128)S(1)}, u32[]{:S(2)}, u32[]{:S(2)}) collective-permute-start(f32[4,128,256]{2,1,0:T(8,128)S(1)} %pad_maximum_fusion.row0_ref), channel_id=1, source_target_pairs={{0,8},{1,9},{2,10},{3,11},{4,12},{5,13},{6,14},{7,15},{8,0},{9,1},... | collective-permute-start | bytes 1572872 | tf_op jit(solution)/shard_map/ppermute | solution.py:294
  51.3 16.8 %collective-permute-start.16 = (f32[4,128,256]{2,1,0:T(8,128)S(1)}, f32[4,128,256]{2,1,0:T(8,128)S(1)}, u32[]{:S(2)}, u32[]{:S(2)}) collective-permute-start(f32[4,128,256]{2,1,0:T(8,128)S(1)} %pad_maximum_fusion.row0_ref), channel_id=1, source_target_pairs={{0,12},{1,13},{2,14},{3,15},{4,0},{5,1},{6,2},{7,3},{8,4},{9,5},{1... | collective-permute-start | bytes 1572872 | tf_op jit(solution)/shard_map/ppermute | solution.py:294
  55.4 12.7 %collective-permute-start.15 = (f32[4,128,256]{2,1,0:T(8,128)S(1)}, f32[4,128,256]{2,1,0:T(8,128)S(1)}, u32[]{:S(2)}, u32[]{:S(2)}) collective-permute-start(f32[4,128,256]{2,1,0:T(8,128)S(1)} %pad_maximum_fusion.row0_ref), channel_id=1, source_target_pairs={{0,4},{1,5},{2,6},{3,7},{4,8},{5,9},{6,10},{7,11},{8,12},{9,13},{1... | collective-permute-start | bytes 1572872 | tf_op jit(solution)/shard_map/ppermute | solution.py:294
  64.4 3.7 %collective-permute-start.18 = (f32[128,1024]{1,0:T(8,128)S(1)}, f32[128,1024]{1,0:T(8,128)S(1)}, u32[]{:S(2)}, u32[]{:S(2)}) collective-permute-start(f32[128,1024]{1,0:T(8,128)S(1)} %broadcast_select_fusion.tall_ref), channel_id=1, source_target_pairs={{0,16},{1,17},{2,18},{3,19},{4,20},{5,21},{6,22},{7,23},{8,24},{9,... | collective-permute-start | bytes 1572872 | tf_op jit(solution)/shard_map/ppermute | solution.py:294

commit v7 on v6

--- a/solution.py
+++ b/solution.py
@@ -11,7 +11,7 @@
 WIDE = 2 * BLOCK
 GROUP = 8
 SHIFTS = (0, 1, 3, 2)
-ORDER = (0, 1, 2, 3)
+ORDER = (0, 1, 3, 2)
 F32 = jnp.float32
 BF16 = jnp.bfloat16
 AXES = ("row", "col")
@@ -238,8 +238,8 @@
             out.append(start(factor_buf.at[a, s], factor_ref.at[place[t]], factor_sem.at[t]))
         high, low = split(factor_buf[a].reshape(4 * BLOCK, WIDE))
         left = jnp.concatenate([high, high, low], axis=1)
-        for n in range(0, cols, WIDE):
-            span = slice(n, n + WIDE)
+        for n in range(0, cols, 2 * WIDE):
+            span = slice(n, n + 2 * WIDE)
             part = lax.dot_general(left, right_ref[:, span], NN, preferred_element_type=F32)
             for s in range(4):
                 t = 4 * a + s

time: 77.8 us -> 77.2 us (level)
  waiting for transfers between devices: 14 us -> 12 us
  starting transfers between devices: 33.8 us -> 34.7 us
    ppermute x19, waiting for transfers between devices: 14 us -> 12 us  [send(): return lax.ppermute(x, AXES, pairs)]
    ppermute x19, starting transfers between devices: 33.8 us -> 34.7 us  [send(): return lax.ppermute(x, AXES, pairs)]
  transfers between devices with their start and end apart: 19 -> 19, of which waited for: 6 -> 5; matrix products, arithmetic and copies ran while one was open for 3% -> 3% of each run, Pallas kernels for 16% -> 16%
where the time goes in v7:
time: 77.2 us; the launch traced here: 76.1 us
  starting transfers between devices  34.7 us (45%)
  Pallas kernels  25.4 us (33%)
  waiting for transfers between devices  12 us (16%)
  other arithmetic  2.17 us (3%)
  between operations  1.08 us (1%)
    ppermute x19, starting transfers between devices, send(): return lax.ppermute(x, AXES, pairs)  34.7 us
    ppermute x19, waiting for transfers between devices, send(): return lax.ppermute(x, AXES, pairs)  12 us
    pallas_call x1, Pallas kernels, update(): pl.pallas_call(update_kernel, in_specs=[here] * 2 + [there] * 6 + [here],...  8.98 us
    pallas_call x1, Pallas kernels, head(): pl.pallas_call(head_kernel, out_shape=(jax.ShapeDtypeStruct((2, BLOCK, WI...  8.89 us
    pallas_call x1, Pallas kernels, hold(): pl.pallas_call(hold_kernel, in_specs=[pl.BlockSpec(memory_space=pltpu.HBM...  3.39 us
    pallas_call x1, Pallas kernels, pack(): pl.pallas_call(pack_kernel, out_shape=(jax.ShapeDtypeStruct((BLOCK, 2 * W...  2.13 us
    pallas_call x1, Pallas kernels, open_strip(): pl.pallas_call(open_kernel, in_specs=[pl.BlockSpec(memory_space=pl.ANY)],...  2.04 us
  transfers between devices with their start and end apart: 19, of which 5 were waited for; matrix products, arithmetic and copies ran while one was open for 3% of the time, Pallas kernels for 16%

profile of v7, /device:TPU:1, one launch (start us, length us, event | category | flops | bytes accessed | tf_op | source)
XLA Modules:
  0.0 76.1 jit_solution(6172299344649350749)
XLA Ops:
  0.6 2.0 %open.1 = (f32[128,1024]{1,0:T(8,128)}, f32[128,128]{1,0:T(8,128)}, f32[4,128,128]{2,1,0:T(8,128)}, f32[4,128,128]{2,1,0:T(8,128)}) custom-call(f32[2048,1024]{1,0:T(8,128)} %stored_ref.1), custom_call_target="tpu_custom_call" | custom-call | tf_op jit(solution)/shard_map/open/pallas_call | solution.py:136
  2.7 3.9 %collective-permute-start.1 = (f32[128,128]{1,0:T(8,128)}, f32[128,128]{1,0:T(8,128)S(1)}, u32[]{:S(2)}, u32[]{:S(2)}) collective-permute-start(f32[128,128]{1,0:T(8,128)} %get-tuple-element.26), channel_id=1, source_target_pairs={{0,4},{1,5},{16,20},{17,21}} | collective-permute-start | bytes 196616 | tf_op jit(solution)/shard_map/ppermute | solution.py:294
  6.6 2.9 %collective-permute-start = (f32[4,128,128]{2,1,0:T(8,128)}, f32[4,128,128]{2,1,0:T(8,128)S(1)}, u32[]{:S(2)}, u32[]{:S(2)}) collective-permute-start(f32[4,128,128]{2,1,0:T(8,128)} %get-tuple-element.25), channel_id=1, source_target_pairs={{0,16},{1,17},{2,18},{3,19},{4,20},{5,21},{6,22},{7,23},{8,24},{9,... | collective-permute-start | bytes 786440 | tf_op jit(solution)/shard_map/ppermute | solution.py:294
  9.5 0.9 %broadcast_select_fusion.4.corner_ref = f32[128,128]{1,0:T(8,128)S(1)} fusion(f32[128,128]{1,0:T(8,128)} %get-tuple-element.26, f32[128,128]{1,0:T(8,128)S(1)} %collective-permute-done.1, pred[]{:T(512)S(6)} %lt.19), kind=kLoop, calls=%fused_computation.6 | loop fusion | flops 16384 | bytes 196609 | tf_op jit(solution)/shard_map/jit(_where)/select_n | solution.py:312
  10.4 2.2 %collective-permute-start.2 = (f32[128,128]{1,0:T(8,128)S(1)}, f32[128,128]{1,0:T(8,128)S(1)}, u32[]{:S(2)}, u32[]{:S(2)}) collective-permute-start(f32[128,128]{1,0:T(8,128)S(1)} %broadcast_select_fusion.4.corner_ref), channel_id=1, source_target_pairs={{0,16},{1,17},{4,20},{5,21},{16,0},{17,1},{20,4},{21,5}} | collective-permute-start | bytes 196616 | tf_op jit(solution)/shard_map/ppermute | solution.py:294
  12.6 1.0 %collective-permute-done.2.beside_ref = f32[128,128]{1,0:T(8,128)S(1)} collective-permute-done((f32[128,128]{1,0:T(8,128)S(1)}, f32[128,128]{1,0:T(8,128)S(1)}, u32[]{:S(2)}, u32[]{:S(2)}) %collective-permute-start.2) | collective-permute-done | bytes 65568 | tf_op jit(solution)/shard_map/ppermute | solution.py:294
  13.5 0.6 copy-done.2
  14.2 0.1 copy-done.1
  14.3 2.1 %pack.1 = (f32[128,512]{1,0:T(8,128)}, f32[128,512]{1,0:T(8,128)}, f32[128,512]{1,0:T(8,128)}, f32[128,512]{1,0:T(8,128)}) custom-call(f32[4,128,128]{2,1,0:T(8,128)} %get-tuple-element.24.keep_ref, f32[4,128,128]{2,1,0:T(8,128)} %copy-done.1, f32[128,128]{1,0:T(8,128)} %copy-done, f32[128,128]{1,0:T(8,128)} %copy-done.2), custom_call_target="tpu_custom_call" | custom-call | tf_op jit(solution)/shard_map/pack/pallas_call | solution.py:159
  16.4 1.9 %collective-permute-start.3 = (f32[128,512]{1,0:T(8,128)}, f32[128,512]{1,0:T(8,128)S(1)}, u32[]{:S(2)}, u32[]{:S(2)}) collective-permute-start(f32[128,512]{1,0:T(8,128)} %get-tuple-element.27), channel_id=1, source_target_pairs={{0,0},{1,16},{2,32},{3,48},{4,68},{5,84},{6,100},{7,116},{8,9},{9,... | collective-permute-start | bytes 786440 | tf_op jit(solution)/shard_map/ppermute | solution.py:294
  18.3 2.2 %collective-permute-start.4 = (f32[128,512]{1,0:T(8,128)}, f32[128,512]{1,0:T(8,128)S(1)}, u32[]{:S(2)}, u32[]{:S(2)}) collective-permute-start(f32[128,512]{1,0:T(8,128)} %get-tuple-element.28), channel_id=1, source_target_pairs={{0,4},{1,20},{2,36},{3,52},{4,72},{5,88},{6,104},{7,120},{8,13},{9... | collective-permute-start | bytes 786440 | tf_op jit(solution)/shard_map/ppermute | solution.py:294
  20.5 2.8 %collective-permute-start.5 = (f32[128,512]{1,0:T(8,128)}, f32[128,512]{1,0:T(8,128)S(1)}, u32[]{:S(2)}, u32[]{:S(2)}) collective-permute-start(f32[128,512]{1,0:T(8,128)} %get-tuple-element.29), channel_id=1, source_target_pairs={{0,12},{1,28},{2,44},{3,60},{4,64},{5,80},{6,96},{7,112},{8,5},{9,... | collective-permute-start | bytes 786440 | tf_op jit(solution)/shard_map/ppermute | solution.py:294
  23.3 1.3 %collective-permute-start.6 = (f32[128,512]{1,0:T(8,128)}, f32[128,512]{1,0:T(8,128)S(1)}, u32[]{:S(2)}, u32[]{:S(2)}) collective-permute-start(f32[128,512]{1,0:T(8,128)} %get-tuple-element.30), channel_id=1, source_target_pairs={{0,8},{1,24},{2,40},{3,56},{4,76},{5,92},{6,108},{7,124},{8,1},{9,... | collective-permute-start | bytes 786440 | tf_op jit(solution)/shard_map/ppermute | solution.py:294
  24.6 1.3 %collective-permute-start.8 = (f32[128,1024]{1,0:T(8,128)}, f32[128,1024]{1,0:T(8,128)S(1)}, u32[]{:S(2)}, u32[]{:S(2)}) collective-permute-start(f32[128,1024]{1,0:T(8,128)} %get-tuple-element.32), channel_id=1, source_target_pairs={{0,96},{1,97},{2,98},{3,99},{4,100},{5,101},{6,102},{7,103},{8,104... | collective-permute-start | bytes 1572872 | tf_op jit(solution)/shard_map/ppermute | solution.py:294
  26.0 5.3 %collective-permute-done.3 = f32[128,512]{1,0:T(8,128)S(1)} collective-permute-done((f32[128,512]{1,0:T(8,128)}, f32[128,512]{1,0:T(8,128)S(1)}, u32[]{:S(2)}, u32[]{:S(2)}) %collective-permute-start.3) | collective-permute-done | bytes 262176 | tf_op jit(solution)/shard_map/ppermute | solution.py:294
  31.3 3.6 %collective-permute-done.5 = f32[128,512]{1,0:T(8,128)S(1)} collective-permute-done((f32[128,512]{1,0:T(8,128)}, f32[128,512]{1,0:T(8,128)S(1)}, u32[]{:S(2)}, u32[]{:S(2)}) %collective-permute-start.5) | collective-permute-done | bytes 262176 | tf_op jit(solution)/shard_map/ppermute | solution.py:294
  35.0 1.3 %collective-permute-start.7 = (f32[128,256]{1,0:T(8,128)S(1)}, f32[128,256]{1,0:T(8,128)S(1)}, u32[]{:S(2)}, u32[]{:S(2)}) collective-permute-start(f32[128,256]{1,0:T(8,128)S(1)} %get-tuple-element.31), channel_id=1, source_target_pairs={{0,32},{2,34},{4,36},{6,38},{8,40},{10,42},{12,44},{14,46},{16,48}... | collective-permute-start | bytes 393224 | tf_op jit(solution)/shard_map/ppermute | solution.py:294
  36.3 1.7 %collective-permute-start.12 = (f32[128,256]{1,0:T(8,128)S(1)}, f32[128,256]{1,0:T(8,128)S(1)}, u32[]{:S(2)}, u32[]{:S(2)}) collective-permute-start(f32[128,256]{1,0:T(8,128)S(1)} %get-tuple-element.34), channel_id=1, source_target_pairs={{0,2},{1,3},{2,0},{3,1},{4,6},{5,7},{6,4},{7,5},{8,10},{9,11},{10,... | collective-permute-start | bytes 393224 | tf_op jit(solution)/shard_map/ppermute | solution.py:294
  38.0 1.9 %collective-permute-start.11 = (f32[128,256]{1,0:T(8,128)S(1)}, f32[128,256]{1,0:T(8,128)S(1)}, u32[]{:S(2)}, u32[]{:S(2)}) collective-permute-start(f32[128,256]{1,0:T(8,128)S(1)} %get-tuple-element.34), channel_id=1, source_target_pairs={{0,3},{1,0},{2,1},{3,2},{4,7},{5,4},{6,5},{7,6},{8,11},{9,8},{10,9... | collective-permute-start | bytes 393224 | tf_op jit(solution)/shard_map/ppermute | solution.py:294
  40.0 0.5 collective-permute-start.10
  40.5 1.1 %broadcast_select_fusion.1 = f32[128,1024]{1,0:T(8,128)S(1)} fusion(f32[128,1024]{1,0:T(8,128)} %get-tuple-element.32, f32[128,1024]{1,0:T(8,128)S(1)} %collective-permute-done.8, pred[]{:T(512)S(6)} %eq.18), kind=kLoop, calls=%fused_computation.3 | loop fusion | flops 131072 | bytes 1572865 | tf_op jit(solution)/shard_map/jit(_where)/select_n | solution.py:337
  41.6 2.1 %collective-permute-start.14 = (f32[128,1024]{1,0:T(8,128)S(1)}, f32[128,1024]{1,0:T(8,128)S(1)}, u32[]{:S(2)}, u32[]{:S(2)}) collective-permute-start(f32[128,1024]{1,0:T(8,128)S(1)} %broadcast_select_fusion.1), channel_id=1, source_target_pairs={{0,32},{1,33},{2,34},{3,35},{4,36},{5,37},{6,38},{7,39},{8,40},{9,... | collective-permute-start | bytes 1572872 | tf_op jit(solution)/shard_map/ppermute | solution.py:294
  43.7 1.3 %collective-permute-start.9 = (f32[128,256]{1,0:T(8,128)S(1)}, f32[128,256]{1,0:T(8,128)S(1)}, u32[]{:S(2)}, u32[]{:S(2)}) collective-permute-start(f32[128,256]{1,0:T(8,128)S(1)} %broadcast_select_fusion.2), channel_id=1, source_target_pairs={{0,1},{2,3},{4,5},{6,7},{8,9},{10,11},{12,13},{14,15},{16,17},{18,... | collective-permute-start | bytes 393224 | tf_op jit(solution)/shard_map/ppermute | solution.py:294
  45.0 0.2 collective-permute-done.10
  45.3 1.8 %collective-permute-done.9 = f32[128,256]{1,0:T(8,128)S(1)} collective-permute-done((f32[128,256]{1,0:T(8,128)S(1)}, f32[128,256]{1,0:T(8,128)S(1)}, u32[]{:S(2)}, u32[]{:S(2)}) %collective-permute-start.9) | collective-permute-done | bytes 131104 | tf_op jit(solution)/shard_map/ppermute | solution.py:294
  47.2 1.6 %collective-permute-start.13 = (f32[128,256]{1,0:T(8,128)S(1)}, f32[128,256]{1,0:T(8,128)S(1)}, u32[]{:S(2)}, u32[]{:S(2)}) collective-permute-start(f32[128,256]{1,0:T(8,128)S(1)} %broadcast_select_fusion.3.mine_ref), channel_id=1, source_target_pairs={{0,16},{1,17},{2,18},{3,19},{4,20},{5,21},{6,22},{7,23},{8,24},{9,... | collective-permute-start | bytes 393224 | tf_op jit(solution)/shard_map/ppermute | solution.py:294
  48.8 2.6 %collective-permute-start.17 = (f32[4,128,256]{2,1,0:T(8,128)S(1)}, f32[4,128,256]{2,1,0:T(8,128)S(1)}, u32[]{:S(2)}, u32[]{:S(2)}) collective-permute-start(f32[4,128,256]{2,1,0:T(8,128)S(1)} %pad_maximum_fusion.row0_ref), channel_id=1, source_target_pairs={{0,8},{1,9},{2,10},{3,11},{4,12},{5,13},{6,14},{7,15},{8,0},{9,1},... | collective-permute-start | bytes 1572872 | tf_op jit(solution)/shard_map/ppermute | solution.py:294
  51.4 2.0 %collective-permute-start.16 = (f32[4,128,256]{2,1,0:T(8,128)S(1)}, f32[4,128,256]{2,1,0:T(8,128)S(1)}, u32[]{:S(2)}, u32[]{:S(2)}) collective-permute-start(f32[4,128,256]{2,1,0:T(8,128)S(1)} %pad_maximum_fusion.row0_ref), channel_id=1, source_target_pairs={{0,12},{1,13},{2,14},{3,15},{4,0},{5,1},{6,2},{7,3},{8,4},{9,5},{1... | collective-permute-start | bytes 1572872 | tf_op jit(solution)/shard_map/ppermute | solution.py:294
  53.4 8.9 %head.1 = (f32[2,128,256]{2,1,0:T(8,128)S(1)}, f32[256,256]{1,0:T(8,128)S(1)}) custom-call(f32[128,256]{1,0:T(8,128)S(1)} %broadcast_select_fusion.3.mine_ref, f32[128,256]{1,0:T(8,128)S(1)} %collective-permute-done.13.other_ref), custom_call_target="tpu_custom_call" | custom-call | flops 100000000 | bytes 1000000 | tf_op jit(solution)/shard_map/head/pallas_call | solution.py:88
  62.4 1.2 %collective-permute-start.18 = (f32[128,1024]{1,0:T(8,128)S(1)}, f32[128,1024]{1,0:T(8,128)S(1)}, u32[]{:S(2)}, u32[]{:S(2)}) collective-permute-start(f32[128,1024]{1,0:T(8,128)S(1)} %broadcast_select_fusion.tall_ref), channel_id=1, source_target_pairs={{0,16},{1,17},{2,18},{3,19},{4,20},{5,21},{6,22},{7,23},{8,24},{9,... | collective-permute-start | bytes 1572872 | tf_op jit(solution)/shard_map/ppermute | solution.py:294
  63.5 3.4 %hold.1.a_ref = f32[16,128,1024]{2,1,0:T(8,128)S(1)} custom-call(f32[16,128,1024]{2,1,0:T(8,128)} %bitcast.7), custom_call_target="tpu_custom_call" | custom-call | bytes 8388608 | tf_op jit(solution)/shard_map/hold/pallas_call | solution.py:107
  67.0 9.0 %update.1 = (f32[16,128,1024]{2,1,0:T(8,128)}, f32[16,128,256]{2,1,0:T(8,128)}) custom-call(f32[2,128,256]{2,1,0:T(8,128)S(1)} %get-tuple-element.36.lower_ref, f32[256,256]{1,0:T(8,128)S(1)} %get-tuple-element.39.inverse_ref, f32[4,128,256]{2,1,0:T(8,128)S(1)} %pad_maximum_fusion.row0_ref, f32[4,128,256]{2,1,0:T(8,128)S(1)} %collective-permute-done.15.row1_ref, ...), custom_call_target="tpu_custom_call" | custom-call | tf_op jit(solution)/shard_map/update/pallas_call | solution.py:259
  (25 shorter events, 0.3 us)
Async XLA Ops:
  2.7 6.8 %collective-permute-start.1 = (f32[128,128]{1,0:T(8,128)}, f32[128,128]{1,0:T(8,128)S(1)}, u32[]{:S(2)}, u32[]{:S(2)}) collective-permute-start(f32[128,128]{1,0:T(8,128)} %get-tuple-element.26), channel_id=1, source_target_pairs={{0,4},{1,5},{16,20},{17,21}} | collective-permute-start | bytes 196616 | tf_op jit(solution)/shard_map/ppermute | solution.py:294
  6.6 6.9 %collective-permute-start = (f32[4,128,128]{2,1,0:T(8,128)}, f32[4,128,128]{2,1,0:T(8,128)S(1)}, u32[]{:S(2)}, u32[]{:S(2)}) collective-permute-start(f32[4,128,128]{2,1,0:T(8,128)} %get-tuple-element.25), channel_id=1, source_target_pairs={{0,16},{1,17},{2,18},{3,19},{4,20},{5,21},{6,22},{7,23},{8,24},{9,... | collective-permute-start | bytes 786440 | tf_op jit(solution)/shard_map/ppermute | solution.py:294
  10.4 3.2 %copy-start = (f32[128,128]{1,0:T(8,128)}, f32[128,128]{1,0:T(8,128)S(1)}, u32[]{:S(2)}) copy-start(f32[128,128]{1,0:T(8,128)S(1)} %broadcast_select_fusion.4.corner_ref) | copy-start | bytes 196612
  10.4 3.1 %collective-permute-start.2 = (f32[128,128]{1,0:T(8,128)S(1)}, f32[128,128]{1,0:T(8,128)S(1)}, u32[]{:S(2)}, u32[]{:S(2)}) collective-permute-start(f32[128,128]{1,0:T(8,128)S(1)} %broadcast_select_fusion.4.corner_ref), channel_id=1, source_target_pairs={{0,16},{1,17},{4,20},{5,21},{16,0},{17,1},{20,4},{21,5}} | collective-permute-start | bytes 196616 | tf_op jit(solution)/shard_map/ppermute | solution.py:294
  13.5 0.6 copy-start.2
  13.5 0.7 copy-start.1
  16.4 14.9 %collective-permute-start.3 = (f32[128,512]{1,0:T(8,128)}, f32[128,512]{1,0:T(8,128)S(1)}, u32[]{:S(2)}, u32[]{:S(2)}) collective-permute-start(f32[128,512]{1,0:T(8,128)} %get-tuple-element.27), channel_id=1, source_target_pairs={{0,0},{1,16},{2,32},{3,48},{4,68},{5,84},{6,100},{7,116},{8,9},{9,... | collective-permute-start | bytes 786440 | tf_op jit(solution)/shard_map/ppermute | solution.py:294
  18.3 13.0 %collective-permute-start.4 = (f32[128,512]{1,0:T(8,128)}, f32[128,512]{1,0:T(8,128)S(1)}, u32[]{:S(2)}, u32[]{:S(2)}) collective-permute-start(f32[128,512]{1,0:T(8,128)} %get-tuple-element.28), channel_id=1, source_target_pairs={{0,4},{1,20},{2,36},{3,52},{4,72},{5,88},{6,104},{7,120},{8,13},{9... | collective-permute-start | bytes 786440 | tf_op jit(solution)/shard_map/ppermute | solution.py:294
  20.5 14.3 %collective-permute-start.5 = (f32[128,512]{1,0:T(8,128)}, f32[128,512]{1,0:T(8,128)S(1)}, u32[]{:S(2)}, u32[]{:S(2)}) collective-permute-start(f32[128,512]{1,0:T(8,128)} %get-tuple-element.29), channel_id=1, source_target_pairs={{0,12},{1,28},{2,44},{3,60},{4,64},{5,80},{6,96},{7,112},{8,5},{9,... | collective-permute-start | bytes 786440 | tf_op jit(solution)/shard_map/ppermute | solution.py:294
  23.3 11.5 %collective-permute-start.6 = (f32[128,512]{1,0:T(8,128)}, f32[128,512]{1,0:T(8,128)S(1)}, u32[]{:S(2)}, u32[]{:S(2)}) collective-permute-start(f32[128,512]{1,0:T(8,128)} %get-tuple-element.30), channel_id=1, source_target_pairs={{0,8},{1,24},{2,40},{3,56},{4,76},{5,92},{6,108},{7,124},{8,1},{9,... | collective-permute-start | bytes 786440 | tf_op jit(solution)/shard_map/ppermute | solution.py:294
  24.6 15.9 %collective-permute-start.8 = (f32[128,1024]{1,0:T(8,128)}, f32[128,1024]{1,0:T(8,128)S(1)}, u32[]{:S(2)}, u32[]{:S(2)}) collective-permute-start(f32[128,1024]{1,0:T(8,128)} %get-tuple-element.32), channel_id=1, source_target_pairs={{0,96},{1,97},{2,98},{3,99},{4,100},{5,101},{6,102},{7,103},{8,104... | collective-permute-start | bytes 1572872 | tf_op jit(solution)/shard_map/ppermute | solution.py:294
  35.0 5.5 %collective-permute-start.7 = (f32[128,256]{1,0:T(8,128)S(1)}, f32[128,256]{1,0:T(8,128)S(1)}, u32[]{:S(2)}, u32[]{:S(2)}) collective-permute-start(f32[128,256]{1,0:T(8,128)S(1)} %get-tuple-element.31), channel_id=1, source_target_pairs={{0,32},{2,34},{4,36},{6,38},{8,40},{10,42},{12,44},{14,46},{16,48}... | collective-permute-start | bytes 393224 | tf_op jit(solution)/shard_map/ppermute | solution.py:294
  36.3 8.7 %collective-permute-start.12 = (f32[128,256]{1,0:T(8,128)S(1)}, f32[128,256]{1,0:T(8,128)S(1)}, u32[]{:S(2)}, u32[]{:S(2)}) collective-permute-start(f32[128,256]{1,0:T(8,128)S(1)} %get-tuple-element.34), channel_id=1, source_target_pairs={{0,2},{1,3},{2,0},{3,1},{4,6},{5,7},{6,4},{7,5},{8,10},{9,11},{10,... | collective-permute-start | bytes 393224 | tf_op jit(solution)/shard_map/ppermute | solution.py:294
  38.0 7.0 %collective-permute-start.11 = (f32[128,256]{1,0:T(8,128)S(1)}, f32[128,256]{1,0:T(8,128)S(1)}, u32[]{:S(2)}, u32[]{:S(2)}) collective-permute-start(f32[128,256]{1,0:T(8,128)S(1)} %get-tuple-element.34), channel_id=1, source_target_pairs={{0,3},{1,0},{2,1},{3,2},{4,7},{5,4},{6,5},{7,6},{8,11},{9,8},{10,9... | collective-permute-start | bytes 393224 | tf_op jit(solution)/shard_map/ppermute | solution.py:294
  40.0 5.3 %collective-permute-start.10 = (f32[128,256]{1,0:T(8,128)S(1)}, f32[128,256]{1,0:T(8,128)S(1)}, u32[]{:S(2)}, u32[]{:S(2)}) collective-permute-start(f32[128,256]{1,0:T(8,128)S(1)} %get-tuple-element.34), channel_id=1, source_target_pairs={{0,1},{1,2},{2,3},{3,0},{4,5},{5,6},{6,7},{7,4},{8,9},{9,10},{10,1... | collective-permute-start | bytes 393224 | tf_op jit(solution)/shard_map/ppermute | solution.py:294
  41.6 20.7 %collective-permute-start.14 = (f32[128,1024]{1,0:T(8,128)S(1)}, f32[128,1024]{1,0:T(8,128)S(1)}, u32[]{:S(2)}, u32[]{:S(2)}) collective-permute-start(f32[128,1024]{1,0:T(8,128)S(1)} %broadcast_select_fusion.1), channel_id=1, source_target_pairs={{0,32},{1,33},{2,34},{3,35},{4,36},{5,37},{6,38},{7,39},{8,40},{9,... | collective-permute-start | bytes 1572872 | tf_op jit(solution)/shard_map/ppermute | solution.py:294
  43.7 3.5 %collective-permute-start.9 = (f32[128,256]{1,0:T(8,128)S(1)}, f32[128,256]{1,0:T(8,128)S(1)}, u32[]{:S(2)}, u32[]{:S(2)}) collective-permute-start(f32[128,256]{1,0:T(8,128)S(1)} %broadcast_select_fusion.2), channel_id=1, source_target_pairs={{0,1},{2,3},{4,5},{6,7},{8,9},{10,11},{12,13},{14,15},{16,17},{18,... | collective-permute-start | bytes 393224 | tf_op jit(solution)/shard_map/ppermute | solution.py:294
  47.2 6.2 %collective-permute-start.13 = (f32[128,256]{1,0:T(8,128)S(1)}, f32[128,256]{1,0:T(8,128)S(1)}, u32[]{:S(2)}, u32[]{:S(2)}) collective-permute-start(f32[128,256]{1,0:T(8,128)S(1)} %broadcast_select_fusion.3.mine_ref), channel_id=1, source_target_pairs={{0,16},{1,17},{2,18},{3,19},{4,20},{5,21},{6,22},{7,23},{8,24},{9,... | collective-permute-start | bytes 393224 | tf_op jit(solution)/shard_map/ppermute | solution.py:294
  48.8 18.1 %collective-permute-start.17 = (f32[4,128,256]{2,1,0:T(8,128)S(1)}, f32[4,128,256]{2,1,0:T(8,128)S(1)}, u32[]{:S(2)}, u32[]{:S(2)}) collective-permute-start(f32[4,128,256]{2,1,0:T(8,128)S(1)} %pad_maximum_fusion.row0_ref), channel_id=1, source_target_pairs={{0,8},{1,9},{2,10},{3,11},{4,12},{5,13},{6,14},{7,15},{8,0},{9,1},... | collective-permute-start | bytes 1572872 | tf_op jit(solution)/shard_map/ppermute | solution.py:294
  51.4 15.6 %collective-permute-start.16 = (f32[4,128,256]{2,1,0:T(8,128)S(1)}, f32[4,128,256]{2,1,0:T(8,128)S(1)}, u32[]{:S(2)}, u32[]{:S(2)}) collective-permute-start(f32[4,128,256]{2,1,0:T(8,128)S(1)} %pad_maximum_fusion.row0_ref), channel_id=1, source_target_pairs={{0,12},{1,13},{2,14},{3,15},{4,0},{5,1},{6,2},{7,3},{8,4},{9,5},{1... | collective-permute-start | bytes 1572872 | tf_op jit(solution)/shard_map/ppermute | solution.py:294
  53.4 13.6 %collective-permute-start.15 = (f32[4,128,256]{2,1,0:T(8,128)S(1)}, f32[4,128,256]{2,1,0:T(8,128)S(1)}, u32[]{:S(2)}, u32[]{:S(2)}) collective-permute-start(f32[4,128,256]{2,1,0:T(8,128)S(1)} %pad_maximum_fusion.row0_ref), channel_id=1, source_target_pairs={{0,4},{1,5},{2,6},{3,7},{4,8},{5,9},{6,10},{7,11},{8,12},{9,13},{1... | collective-permute-start | bytes 1572872 | tf_op jit(solution)/shard_map/ppermute | solution.py:294
  62.4 4.6 %collective-permute-start.18 = (f32[128,1024]{1,0:T(8,128)S(1)}, f32[128,1024]{1,0:T(8,128)S(1)}, u32[]{:S(2)}, u32[]{:S(2)}) collective-permute-start(f32[128,1024]{1,0:T(8,128)S(1)} %broadcast_select_fusion.tall_ref), channel_id=1, source_target_pairs={{0,16},{1,17},{2,18},{3,19},{4,20},{5,21},{6,22},{7,23},{8,24},{9,... | collective-permute-start | bytes 1572872 | tf_op jit(solution)/shard_map/ppermute | solution.py:294

commit v8 on v7

--- a/solution.py
+++ b/solution.py
@@ -238,8 +238,8 @@
             out.append(start(factor_buf.at[a, s], factor_ref.at[place[t]], factor_sem.at[t]))
         high, low = split(factor_buf[a].reshape(4 * BLOCK, WIDE))
         left = jnp.concatenate([high, high, low], axis=1)
-        for n in range(0, cols, 2 * WIDE):
-            span = slice(n, n + 2 * WIDE)
+        for n in range(0, cols, 4 * WIDE):
+            span = slice(n, n + 4 * WIDE)
             part = lax.dot_general(left, right_ref[:, span], NN, preferred_element_type=F32)
             for s in range(4):
                 t = 4 * a + s

time: 77.2 us -> 77.2 us (level)
  no operation moved by 1% of the time
where the time goes in v8:
time: 77.2 us; the launch traced here: 76.1 us
  starting transfers between devices  34.7 us (45%)
  Pallas kernels  25.4 us (33%)
  waiting for transfers between devices  12 us (16%)
  other arithmetic  2.17 us (3%)
  between operations  1.08 us (1%)
    ppermute x19, starting transfers between devices, send(): return lax.ppermute(x, AXES, pairs)  34.7 us
    ppermute x19, waiting for transfers between devices, send(): return lax.ppermute(x, AXES, pairs)  12 us
    pallas_call x1, Pallas kernels, update(): pl.pallas_call(update_kernel, in_specs=[here] * 2 + [there] * 6 + [here],...  8.98 us
    pallas_call x1, Pallas kernels, head(): pl.pallas_call(head_kernel, out_shape=(jax.ShapeDtypeStruct((2, BLOCK, WI...  8.89 us
    pallas_call x1, Pallas kernels, hold(): pl.pallas_call(hold_kernel, in_specs=[pl.BlockSpec(memory_space=pltpu.HBM...  3.39 us
    pallas_call x1, Pallas kernels, pack(): pl.pallas_call(pack_kernel, out_shape=(jax.ShapeDtypeStruct((BLOCK, 2 * W...  2.13 us
    pallas_call x1, Pallas kernels, open_strip(): pl.pallas_call(open_kernel, in_specs=[pl.BlockSpec(memory_space=pl.ANY)],...  2.04 us
  transfers between devices with their start and end apart: 19, of which 5 were waited for; matrix products, arithmetic and copies ran while one was open for 3% of the time, Pallas kernels for 16%

profile of v8, /device:TPU:1, one launch (start us, length us, event | category | flops | bytes accessed | tf_op | source)
XLA Modules:
  0.0 76.1 jit_solution(6172299344649350749)
XLA Ops:
  0.6 2.0 %open.1 = (f32[128,1024]{1,0:T(8,128)}, f32[128,128]{1,0:T(8,128)}, f32[4,128,128]{2,1,0:T(8,128)}, f32[4,128,128]{2,1,0:T(8,128)}) custom-call(f32[2048,1024]{1,0:T(8,128)} %stored_ref.1), custom_call_target="tpu_custom_call" | custom-call | tf_op jit(solution)/shard_map/open/pallas_call | solution.py:136
  2.7 3.9 %collective-permute-start.1 = (f32[128,128]{1,0:T(8,128)}, f32[128,128]{1,0:T(8,128)S(1)}, u32[]{:S(2)}, u32[]{:S(2)}) collective-permute-start(f32[128,128]{1,0:T(8,128)} %get-tuple-element.26), channel_id=1, source_target_pairs={{0,4},{1,5},{16,20},{17,21}} | collective-permute-start | bytes 196616 | tf_op jit(solution)/shard_map/ppermute | solution.py:294
  6.6 2.9 %collective-permute-start = (f32[4,128,128]{2,1,0:T(8,128)}, f32[4,128,128]{2,1,0:T(8,128)S(1)}, u32[]{:S(2)}, u32[]{:S(2)}) collective-permute-start(f32[4,128,128]{2,1,0:T(8,128)} %get-tuple-element.25), channel_id=1, source_target_pairs={{0,16},{1,17},{2,18},{3,19},{4,20},{5,21},{6,22},{7,23},{8,24},{9,... | collective-permute-start | bytes 786440 | tf_op jit(solution)/shard_map/ppermute | solution.py:294
  9.5 0.9 %broadcast_select_fusion.4.corner_ref = f32[128,128]{1,0:T(8,128)S(1)} fusion(f32[128,128]{1,0:T(8,128)} %get-tuple-element.26, f32[128,128]{1,0:T(8,128)S(1)} %collective-permute-done.1, pred[]{:T(512)S(6)} %lt.19), kind=kLoop, calls=%fused_computation.6 | loop fusion | flops 16384 | bytes 196609 | tf_op jit(solution)/shard_map/jit(_where)/select_n | solution.py:312
  10.4 2.2 %collective-permute-start.2 = (f32[128,128]{1,0:T(8,128)S(1)}, f32[128,128]{1,0:T(8,128)S(1)}, u32[]{:S(2)}, u32[]{:S(2)}) collective-permute-start(f32[128,128]{1,0:T(8,128)S(1)} %broadcast_select_fusion.4.corner_ref), channel_id=1, source_target_pairs={{0,16},{1,17},{4,20},{5,21},{16,0},{17,1},{20,4},{21,5}} | collective-permute-start | bytes 196616 | tf_op jit(solution)/shard_map/ppermute | solution.py:294
  12.6 1.0 %collective-permute-done.2.beside_ref = f32[128,128]{1,0:T(8,128)S(1)} collective-permute-done((f32[128,128]{1,0:T(8,128)S(1)}, f32[128,128]{1,0:T(8,128)S(1)}, u32[]{:S(2)}, u32[]{:S(2)}) %collective-permute-start.2) | collective-permute-done | bytes 65568 | tf_op jit(solution)/shard_map/ppermute | solution.py:294
  13.5 0.6 copy-done.2
  14.2 0.1 copy-done.1
  14.3 2.1 %pack.1 = (f32[128,512]{1,0:T(8,128)}, f32[128,512]{1,0:T(8,128)}, f32[128,512]{1,0:T(8,128)}, f32[128,512]{1,0:T(8,128)}) custom-call(f32[4,128,128]{2,1,0:T(8,128)} %get-tuple-element.24.keep_ref, f32[4,128,128]{2,1,0:T(8,128)} %copy-done.1, f32[128,128]{1,0:T(8,128)} %copy-done, f32[128,128]{1,0:T(8,128)} %copy-done.2), custom_call_target="tpu_custom_call" | custom-call | tf_op jit(solution)/shard_map/pack/pallas_call | solution.py:159
  16.4 1.9 %collective-permute-start.3 = (f32[128,512]{1,0:T(8,128)}, f32[128,512]{1,0:T(8,128)S(1)}, u32[]{:S(2)}, u32[]{:S(2)}) collective-permute-start(f32[128,512]{1,0:T(8,128)} %get-tuple-element.27), channel_id=1, source_target_pairs={{0,0},{1,16},{2,32},{3,48},{4,68},{5,84},{6,100},{7,116},{8,9},{9,... | collective-permute-start | bytes 786440 | tf_op jit(solution)/shard_map/ppermute | solution.py:294
  18.3 2.2 %collective-permute-start.4 = (f32[128,512]{1,0:T(8,128)}, f32[128,512]{1,0:T(8,128)S(1)}, u32[]{:S(2)}, u32[]{:S(2)}) collective-permute-start(f32[128,512]{1,0:T(8,128)} %get-tuple-element.28), channel_id=1, source_target_pairs={{0,4},{1,20},{2,36},{3,52},{4,72},{5,88},{6,104},{7,120},{8,13},{9... | collective-permute-start | bytes 786440 | tf_op jit(solution)/shard_map/ppermute | solution.py:294
  20.5 2.8 %collective-permute-start.5 = (f32[128,512]{1,0:T(8,128)}, f32[128,512]{1,0:T(8,128)S(1)}, u32[]{:S(2)}, u32[]{:S(2)}) collective-permute-start(f32[128,512]{1,0:T(8,128)} %get-tuple-element.29), channel_id=1, source_target_pairs={{0,12},{1,28},{2,44},{3,60},{4,64},{5,80},{6,96},{7,112},{8,5},{9,... | collective-permute-start | bytes 786440 | tf_op jit(solution)/shard_map/ppermute | solution.py:294
  23.3 1.3 %collective-permute-start.6 = (f32[128,512]{1,0:T(8,128)}, f32[128,512]{1,0:T(8,128)S(1)}, u32[]{:S(2)}, u32[]{:S(2)}) collective-permute-start(f32[128,512]{1,0:T(8,128)} %get-tuple-element.30), channel_id=1, source_target_pairs={{0,8},{1,24},{2,40},{3,56},{4,76},{5,92},{6,108},{7,124},{8,1},{9,... | collective-permute-start | bytes 786440 | tf_op jit(solution)/shard_map/ppermute | solution.py:294
  24.6 1.3 %collective-permute-start.8 = (f32[128,1024]{1,0:T(8,128)}, f32[128,1024]{1,0:T(8,128)S(1)}, u32[]{:S(2)}, u32[]{:S(2)}) collective-permute-start(f32[128,1024]{1,0:T(8,128)} %get-tuple-element.32), channel_id=1, source_target_pairs={{0,96},{1,97},{2,98},{3,99},{4,100},{5,101},{6,102},{7,103},{8,104... | collective-permute-start | bytes 1572872 | tf_op jit(solution)/shard_map/ppermute | solution.py:294
  26.0 5.3 %collective-permute-done.3 = f32[128,512]{1,0:T(8,128)S(1)} collective-permute-done((f32[128,512]{1,0:T(8,128)}, f32[128,512]{1,0:T(8,128)S(1)}, u32[]{:S(2)}, u32[]{:S(2)}) %collective-permute-start.3) | collective-permute-done | bytes 262176 | tf_op jit(solution)/shard_map/ppermute | solution.py:294
  31.3 3.6 %collective-permute-done.5 = f32[128,512]{1,0:T(8,128)S(1)} collective-permute-done((f32[128,512]{1,0:T(8,128)}, f32[128,512]{1,0:T(8,128)S(1)}, u32[]{:S(2)}, u32[]{:S(2)}) %collective-permute-start.5) | collective-permute-done | bytes 262176 | tf_op jit(solution)/shard_map/ppermute | solution.py:294
  35.0 1.3 %collective-permute-start.7 = (f32[128,256]{1,0:T(8,128)S(1)}, f32[128,256]{1,0:T(8,128)S(1)}, u32[]{:S(2)}, u32[]{:S(2)}) collective-permute-start(f32[128,256]{1,0:T(8,128)S(1)} %get-tuple-element.31), channel_id=1, source_target_pairs={{0,32},{2,34},{4,36},{6,38},{8,40},{10,42},{12,44},{14,46},{16,48}... | collective-permute-start | bytes 393224 | tf_op jit(solution)/shard_map/ppermute | solution.py:294
  36.3 1.7 %collective-permute-start.12 = (f32[128,256]{1,0:T(8,128)S(1)}, f32[128,256]{1,0:T(8,128)S(1)}, u32[]{:S(2)}, u32[]{:S(2)}) collective-permute-start(f32[128,256]{1,0:T(8,128)S(1)} %get-tuple-element.34), channel_id=1, source_target_pairs={{0,2},{1,3},{2,0},{3,1},{4,6},{5,7},{6,4},{7,5},{8,10},{9,11},{10,... | collective-permute-start | bytes 393224 | tf_op jit(solution)/shard_map/ppermute | solution.py:294
  38.0 1.9 %collective-permute-start.11 = (f32[128,256]{1,0:T(8,128)S(1)}, f32[128,256]{1,0:T(8,128)S(1)}, u32[]{:S(2)}, u32[]{:S(2)}) collective-permute-start(f32[128,256]{1,0:T(8,128)S(1)} %get-tuple-element.34), channel_id=1, source_target_pairs={{0,3},{1,0},{2,1},{3,2},{4,7},{5,4},{6,5},{7,6},{8,11},{9,8},{10,9... | collective-permute-start | bytes 393224 | tf_op jit(solution)/shard_map/ppermute | solution.py:294
  40.0 0.5 collective-permute-start.10
  40.5 1.1 %broadcast_select_fusion.1 = f32[128,1024]{1,0:T(8,128)S(1)} fusion(f32[128,1024]{1,0:T(8,128)} %get-tuple-element.32, f32[128,1024]{1,0:T(8,128)S(1)} %collective-permute-done.8, pred[]{:T(512)S(6)} %eq.18), kind=kLoop, calls=%fused_computation.3 | loop fusion | flops 131072 | bytes 1572865 | tf_op jit(solution)/shard_map/jit(_where)/select_n | solution.py:337
  41.6 2.1 %collective-permute-start.14 = (f32[128,1024]{1,0:T(8,128)S(1)}, f32[128,1024]{1,0:T(8,128)S(1)}, u32[]{:S(2)}, u32[]{:S(2)}) collective-permute-start(f32[128,1024]{1,0:T(8,128)S(1)} %broadcast_select_fusion.1), channel_id=1, source_target_pairs={{0,32},{1,33},{2,34},{3,35},{4,36},{5,37},{6,38},{7,39},{8,40},{9,... | collective-permute-start | bytes 1572872 | tf_op jit(solution)/shard_map/ppermute | solution.py:294
  43.7 1.3 %collective-permute-start.9 = (f32[128,256]{1,0:T(8,128)S(1)}, f32[128,256]{1,0:T(8,128)S(1)}, u32[]{:S(2)}, u32[]{:S(2)}) collective-permute-start(f32[128,256]{1,0:T(8,128)S(1)} %broadcast_select_fusion.2), channel_id=1, source_target_pairs={{0,1},{2,3},{4,5},{6,7},{8,9},{10,11},{12,13},{14,15},{16,17},{18,... | collective-permute-start | bytes 393224 | tf_op jit(solution)/shard_map/ppermute | solution.py:294
  45.0 0.2 collective-permute-done.10
  45.3 1.8 %collective-permute-done.9 = f32[128,256]{1,0:T(8,128)S(1)} collective-permute-done((f32[128,256]{1,0:T(8,128)S(1)}, f32[128,256]{1,0:T(8,128)S(1)}, u32[]{:S(2)}, u32[]{:S(2)}) %collective-permute-start.9) | collective-permute-done | bytes 131104 | tf_op jit(solution)/shard_map/ppermute | solution.py:294
  47.2 1.6 %collective-permute-start.13 = (f32[128,256]{1,0:T(8,128)S(1)}, f32[128,256]{1,0:T(8,128)S(1)}, u32[]{:S(2)}, u32[]{:S(2)}) collective-permute-start(f32[128,256]{1,0:T(8,128)S(1)} %broadcast_select_fusion.3.mine_ref), channel_id=1, source_target_pairs={{0,16},{1,17},{2,18},{3,19},{4,20},{5,21},{6,22},{7,23},{8,24},{9,... | collective-permute-start | bytes 393224 | tf_op jit(solution)/shard_map/ppermute | solution.py:294
  48.8 2.6 %collective-permute-start.17 = (f32[4,128,256]{2,1,0:T(8,128)S(1)}, f32[4,128,256]{2,1,0:T(8,128)S(1)}, u32[]{:S(2)}, u32[]{:S(2)}) collective-permute-start(f32[4,128,256]{2,1,0:T(8,128)S(1)} %pad_maximum_fusion.row0_ref), channel_id=1, source_target_pairs={{0,8},{1,9},{2,10},{3,11},{4,12},{5,13},{6,14},{7,15},{8,0},{9,1},... | collective-permute-start | bytes 1572872 | tf_op jit(solution)/shard_map/ppermute | solution.py:294
  51.4 2.0 %collective-permute-start.16 = (f32[4,128,256]{2,1,0:T(8,128)S(1)}, f32[4,128,256]{2,1,0:T(8,128)S(1)}, u32[]{:S(2)}, u32[]{:S(2)}) collective-permute-start(f32[4,128,256]{2,1,0:T(8,128)S(1)} %pad_maximum_fusion.row0_ref), channel_id=1, source_target_pairs={{0,12},{1,13},{2,14},{3,15},{4,0},{5,1},{6,2},{7,3},{8,4},{9,5},{1... | collective-permute-start | bytes 1572872 | tf_op jit(solution)/shard_map/ppermute | solution.py:294
  53.4 8.9 %head.1 = (f32[2,128,256]{2,1,0:T(8,128)S(1)}, f32[256,256]{1,0:T(8,128)S(1)}) custom-call(f32[128,256]{1,0:T(8,128)S(1)} %broadcast_select_fusion.3.mine_ref, f32[128,256]{1,0:T(8,128)S(1)} %collective-permute-done.13.other_ref), custom_call_target="tpu_custom_call" | custom-call | flops 100000000 | bytes 1000000 | tf_op jit(solution)/shard_map/head/pallas_call | solution.py:88
  62.4 1.2 %collective-permute-start.18 = (f32[128,1024]{1,0:T(8,128)S(1)}, f32[128,1024]{1,0:T(8,128)S(1)}, u32[]{:S(2)}, u32[]{:S(2)}) collective-permute-start(f32[128,1024]{1,0:T(8,128)S(1)} %broadcast_select_fusion.tall_ref), channel_id=1, source_target_pairs={{0,16},{1,17},{2,18},{3,19},{4,20},{5,21},{6,22},{7,23},{8,24},{9,... | collective-permute-start | bytes 1572872 | tf_op jit(solution)/shard_map/ppermute | solution.py:294
  63.5 3.4 %hold.1.a_ref = f32[16,128,1024]{2,1,0:T(8,128)S(1)} custom-call(f32[16,128,1024]{2,1,0:T(8,128)} %bitcast.7), custom_call_target="tpu_custom_call" | custom-call | bytes 8388608 | tf_op jit(solution)/shard_map/hold/pallas_call | solution.py:107
  67.0 9.0 %update.1 = (f32[16,128,1024]{2,1,0:T(8,128)}, f32[16,128,256]{2,1,0:T(8,128)}) custom-call(f32[2,128,256]{2,1,0:T(8,128)S(1)} %get-tuple-element.36.lower_ref, f32[256,256]{1,0:T(8,128)S(1)} %get-tuple-element.39.inverse_ref, f32[4,128,256]{2,1,0:T(8,128)S(1)} %pad_maximum_fusion.row0_ref, f32[4,128,256]{2,1,0:T(8,128)S(1)} %collective-permute-done.15.row1_ref, ...), custom_call_target="tpu_custom_call" | custom-call | tf_op jit(solution)/shard_map/update/pallas_call | solution.py:259
  (25 shorter events, 0.3 us)
Async XLA Ops:
  2.7 6.8 %collective-permute-start.1 = (f32[128,128]{1,0:T(8,128)}, f32[128,128]{1,0:T(8,128)S(1)}, u32[]{:S(2)}, u32[]{:S(2)}) collective-permute-start(f32[128,128]{1,0:T(8,128)} %get-tuple-element.26), channel_id=1, source_target_pairs={{0,4},{1,5},{16,20},{17,21}} | collective-permute-start | bytes 196616 | tf_op jit(solution)/shard_map/ppermute | solution.py:294
  6.6 6.9 %collective-permute-start = (f32[4,128,128]{2,1,0:T(8,128)}, f32[4,128,128]{2,1,0:T(8,128)S(1)}, u32[]{:S(2)}, u32[]{:S(2)}) collective-permute-start(f32[4,128,128]{2,1,0:T(8,128)} %get-tuple-element.25), channel_id=1, source_target_pairs={{0,16},{1,17},{2,18},{3,19},{4,20},{5,21},{6,22},{7,23},{8,24},{9,... | collective-permute-start | bytes 786440 | tf_op jit(solution)/shard_map/ppermute | solution.py:294
  10.4 3.2 %copy-start = (f32[128,128]{1,0:T(8,128)}, f32[128,128]{1,0:T(8,128)S(1)}, u32[]{:S(2)}) copy-start(f32[128,128]{1,0:T(8,128)S(1)} %broadcast_select_fusion.4.corner_ref) | copy-start | bytes 196612
  10.4 3.1 %collective-permute-start.2 = (f32[128,128]{1,0:T(8,128)S(1)}, f32[128,128]{1,0:T(8,128)S(1)}, u32[]{:S(2)}, u32[]{:S(2)}) collective-permute-start(f32[128,128]{1,0:T(8,128)S(1)} %broadcast_select_fusion.4.corner_ref), channel_id=1, source_target_pairs={{0,16},{1,17},{4,20},{5,21},{16,0},{17,1},{20,4},{21,5}} | collective-permute-start | bytes 196616 | tf_op jit(solution)/shard_map/ppermute | solution.py:294
  13.5 0.6 copy-start.2
  13.5 0.7 copy-start.1
  16.4 14.9 %collective-permute-start.3 = (f32[128,512]{1,0:T(8,128)}, f32[128,512]{1,0:T(8,128)S(1)}, u32[]{:S(2)}, u32[]{:S(2)}) collective-permute-start(f32[128,512]{1,0:T(8,128)} %get-tuple-element.27), channel_id=1, source_target_pairs={{0,0},{1,16},{2,32},{3,48},{4,68},{5,84},{6,100},{7,116},{8,9},{9,... | collective-permute-start | bytes 786440 | tf_op jit(solution)/shard_map/ppermute | solution.py:294
  18.3 13.0 %collective-permute-start.4 = (f32[128,512]{1,0:T(8,128)}, f32[128,512]{1,0:T(8,128)S(1)}, u32[]{:S(2)}, u32[]{:S(2)}) collective-permute-start(f32[128,512]{1,0:T(8,128)} %get-tuple-element.28), channel_id=1, source_target_pairs={{0,4},{1,20},{2,36},{3,52},{4,72},{5,88},{6,104},{7,120},{8,13},{9... | collective-permute-start | bytes 786440 | tf_op jit(solution)/shard_map/ppermute | solution.py:294
  20.5 14.3 %collective-permute-start.5 = (f32[128,512]{1,0:T(8,128)}, f32[128,512]{1,0:T(8,128)S(1)}, u32[]{:S(2)}, u32[]{:S(2)}) collective-permute-start(f32[128,512]{1,0:T(8,128)} %get-tuple-element.29), channel_id=1, source_target_pairs={{0,12},{1,28},{2,44},{3,60},{4,64},{5,80},{6,96},{7,112},{8,5},{9,... | collective-permute-start | bytes 786440 | tf_op jit(solution)/shard_map/ppermute | solution.py:294
  23.3 11.5 %collective-permute-start.6 = (f32[128,512]{1,0:T(8,128)}, f32[128,512]{1,0:T(8,128)S(1)}, u32[]{:S(2)}, u32[]{:S(2)}) collective-permute-start(f32[128,512]{1,0:T(8,128)} %get-tuple-element.30), channel_id=1, source_target_pairs={{0,8},{1,24},{2,40},{3,56},{4,76},{5,92},{6,108},{7,124},{8,1},{9,... | collective-permute-start | bytes 786440 | tf_op jit(solution)/shard_map/ppermute | solution.py:294
  24.6 15.9 %collective-permute-start.8 = (f32[128,1024]{1,0:T(8,128)}, f32[128,1024]{1,0:T(8,128)S(1)}, u32[]{:S(2)}, u32[]{:S(2)}) collective-permute-start(f32[128,1024]{1,0:T(8,128)} %get-tuple-element.32), channel_id=1, source_target_pairs={{0,96},{1,97},{2,98},{3,99},{4,100},{5,101},{6,102},{7,103},{8,104... | collective-permute-start | bytes 1572872 | tf_op jit(solution)/shard_map/ppermute | solution.py:294
  35.0 5.5 %collective-permute-start.7 = (f32[128,256]{1,0:T(8,128)S(1)}, f32[128,256]{1,0:T(8,128)S(1)}, u32[]{:S(2)}, u32[]{:S(2)}) collective-permute-start(f32[128,256]{1,0:T(8,128)S(1)} %get-tuple-element.31), channel_id=1, source_target_pairs={{0,32},{2,34},{4,36},{6,38},{8,40},{10,42},{12,44},{14,46},{16,48}... | collective-permute-start | bytes 393224 | tf_op jit(solution)/shard_map/ppermute | solution.py:294
  36.3 8.7 %collective-permute-start.12 = (f32[128,256]{1,0:T(8,128)S(1)}, f32[128,256]{1,0:T(8,128)S(1)}, u32[]{:S(2)}, u32[]{:S(2)}) collective-permute-start(f32[128,256]{1,0:T(8,128)S(1)} %get-tuple-element.34), channel_id=1, source_target_pairs={{0,2},{1,3},{2,0},{3,1},{4,6},{5,7},{6,4},{7,5},{8,10},{9,11},{10,... | collective-permute-start | bytes 393224 | tf_op jit(solution)/shard_map/ppermute | solution.py:294
  38.0 7.0 %collective-permute-start.11 = (f32[128,256]{1,0:T(8,128)S(1)}, f32[128,256]{1,0:T(8,128)S(1)}, u32[]{:S(2)}, u32[]{:S(2)}) collective-permute-start(f32[128,256]{1,0:T(8,128)S(1)} %get-tuple-element.34), channel_id=1, source_target_pairs={{0,3},{1,0},{2,1},{3,2},{4,7},{5,4},{6,5},{7,6},{8,11},{9,8},{10,9... | collective-permute-start | bytes 393224 | tf_op jit(solution)/shard_map/ppermute | solution.py:294
  40.0 5.3 %collective-permute-start.10 = (f32[128,256]{1,0:T(8,128)S(1)}, f32[128,256]{1,0:T(8,128)S(1)}, u32[]{:S(2)}, u32[]{:S(2)}) collective-permute-start(f32[128,256]{1,0:T(8,128)S(1)} %get-tuple-element.34), channel_id=1, source_target_pairs={{0,1},{1,2},{2,3},{3,0},{4,5},{5,6},{6,7},{7,4},{8,9},{9,10},{10,1... | collective-permute-start | bytes 393224 | tf_op jit(solution)/shard_map/ppermute | solution.py:294
  41.6 20.7 %collective-permute-start.14 = (f32[128,1024]{1,0:T(8,128)S(1)}, f32[128,1024]{1,0:T(8,128)S(1)}, u32[]{:S(2)}, u32[]{:S(2)}) collective-permute-start(f32[128,1024]{1,0:T(8,128)S(1)} %broadcast_select_fusion.1), channel_id=1, source_target_pairs={{0,32},{1,33},{2,34},{3,35},{4,36},{5,37},{6,38},{7,39},{8,40},{9,... | collective-permute-start | bytes 1572872 | tf_op jit(solution)/shard_map/ppermute | solution.py:294
  43.7 3.5 %collective-permute-start.9 = (f32[128,256]{1,0:T(8,128)S(1)}, f32[128,256]{1,0:T(8,128)S(1)}, u32[]{:S(2)}, u32[]{:S(2)}) collective-permute-start(f32[128,256]{1,0:T(8,128)S(1)} %broadcast_select_fusion.2), channel_id=1, source_target_pairs={{0,1},{2,3},{4,5},{6,7},{8,9},{10,11},{12,13},{14,15},{16,17},{18,... | collective-permute-start | bytes 393224 | tf_op jit(solution)/shard_map/ppermute | solution.py:294
  47.2 6.2 %collective-permute-start.13 = (f32[128,256]{1,0:T(8,128)S(1)}, f32[128,256]{1,0:T(8,128)S(1)}, u32[]{:S(2)}, u32[]{:S(2)}) collective-permute-start(f32[128,256]{1,0:T(8,128)S(1)} %broadcast_select_fusion.3.mine_ref), channel_id=1, source_target_pairs={{0,16},{1,17},{2,18},{3,19},{4,20},{5,21},{6,22},{7,23},{8,24},{9,... | collective-permute-start | bytes 393224 | tf_op jit(solution)/shard_map/ppermute | solution.py:294
  48.8 18.1 %collective-permute-start.17 = (f32[4,128,256]{2,1,0:T(8,128)S(1)}, f32[4,128,256]{2,1,0:T(8,128)S(1)}, u32[]{:S(2)}, u32[]{:S(2)}) collective-permute-start(f32[4,128,256]{2,1,0:T(8,128)S(1)} %pad_maximum_fusion.row0_ref), channel_id=1, source_target_pairs={{0,8},{1,9},{2,10},{3,11},{4,12},{5,13},{6,14},{7,15},{8,0},{9,1},... | collective-permute-start | bytes 1572872 | tf_op jit(solution)/shard_map/ppermute | solution.py:294
  51.4 15.6 %collective-permute-start.16 = (f32[4,128,256]{2,1,0:T(8,128)S(1)}, f32[4,128,256]{2,1,0:T(8,128)S(1)}, u32[]{:S(2)}, u32[]{:S(2)}) collective-permute-start(f32[4,128,256]{2,1,0:T(8,128)S(1)} %pad_maximum_fusion.row0_ref), channel_id=1, source_target_pairs={{0,12},{1,13},{2,14},{3,15},{4,0},{5,1},{6,2},{7,3},{8,4},{9,5},{1... | collective-permute-start | bytes 1572872 | tf_op jit(solution)/shard_map/ppermute | solution.py:294
  53.4 13.6 %collective-permute-start.15 = (f32[4,128,256]{2,1,0:T(8,128)S(1)}, f32[4,128,256]{2,1,0:T(8,128)S(1)}, u32[]{:S(2)}, u32[]{:S(2)}) collective-permute-start(f32[4,128,256]{2,1,0:T(8,128)S(1)} %pad_maximum_fusion.row0_ref), channel_id=1, source_target_pairs={{0,4},{1,5},{2,6},{3,7},{4,8},{5,9},{6,10},{7,11},{8,12},{9,13},{1... | collective-permute-start | bytes 1572872 | tf_op jit(solution)/shard_map/ppermute | solution.py:294
  62.4 4.6 %collective-permute-start.18 = (f32[128,1024]{1,0:T(8,128)S(1)}, f32[128,1024]{1,0:T(8,128)S(1)}, u32[]{:S(2)}, u32[]{:S(2)}) collective-permute-start(f32[128,1024]{1,0:T(8,128)S(1)} %broadcast_select_fusion.tall_ref), channel_id=1, source_target_pairs={{0,16},{1,17},{2,18},{3,19},{4,20},{5,21},{6,22},{7,23},{8,24},{9,... | collective-permute-start | bytes 1572872 | tf_op jit(solution)/shard_map/ppermute | solution.py:294
